TPU v7x, 32 devices: a whole 2x2x4 slice. The times are simulated.
32 devices in a mesh: dp: 8 (over z, y), expert: 4 (over x, core).
Axes of the slice: x: 2, y: 2, z: 4, core: 2. Of those that a mesh axis runs over, the one named last changes fastest.
Arguments:
- tokens: bfloat16 [32768, 384], P(('dp', 'expert')), may hold values from -6 to 6
- cotangent: bfloat16 [32768, 384], P(('dp', 'expert')), may hold values from -6 to 6
- patch_counts: int32 [32, 5], P(('dp', 'expert')), may hold values from 96 to 192
- time_buckets: int32 [32], P(('dp', 'expert')), may hold values from 0 to 999
- image_labels: int32 [32, 5], P(('dp', 'expert')), may hold values from 0 to 1000
- expert_routes: int32 [32, 1024, 2], P(('dp', 'expert')), may hold values from 0 to 15, all different within a row; in each aligned block of 1024 rows (0 to 1023, 1024 to 2047, ..., all dimensions but the last counted through in order) at most 160 rows name the same one
- time_table: bfloat16 [1000, 384], replicated, may hold values from -4 to 4
- label_table: bfloat16 [1001, 384], replicated, may hold values from -4 to 4
- ada_weight: bfloat16 [384, 2304], replicated, may hold values from -0.3125 to 0.3125
- ada_bias: float32 [2304], replicated, may hold values from -2 to 2
- qkv_weight: bfloat16 [384, 1152], replicated, may hold values from -0.3125 to 0.3125
- out_weight: bfloat16 [384, 384], replicated, may hold values from -3.5 to 3.5
- out_bias: float32 [384], replicated, may hold values from -1.5 to 1.5
- router_weight: bfloat16 [384, 16], replicated, may hold values from -0.21875 to 0.21875
- expert_up: bfloat16 [16, 384, 1536], P('expert'), may hold values from -0.3125 to 0.3125
- expert_up_bias: float32 [16, 1536], P('expert'), may hold values from -1.5 to 1.5
- expert_down: bfloat16 [16, 1536, 384], P('expert'), may hold values from -0.15625 to 0.15625
- expert_down_bias: float32 [16, 384], P('expert'), may hold values from -1.5 to 1.5
- shared_up: bfloat16 [2, 384, 1536], replicated, may hold values from -0.3125 to 0.3125
- shared_up_bias: float32 [2, 1536], replicated, may hold values from -1.5 to 1.5
- shared_down: bfloat16 [2, 1536, 384], replicated, may hold values from -0.15625 to 0.15625
- shared_down_bias: float32 [2, 384], replicated, may hold values from -1.5 to 1.5
Outputs:
- layer_out: bfloat16 [32768, 384], P(('dp', 'expert'))
- grad_tokens: float32 [32768, 384], P(('dp', 'expert'))
- rms_stats: float32 [32, 2], P(('dp', 'expert'))
- grad_time_table: float32 [1000, 384], replicated
- grad_label_table: float32 [1001, 384], replicated
- grad_ada_weight: float32 [384, 2304], replicated
- grad_ada_bias: float32 [2304], replicated
- grad_qkv_weight: float32 [384, 1152], replicated
- grad_out_weight: float32 [384, 384], replicated
- grad_out_bias: float32 [384], replicated
- grad_router_weight: float32 [384, 16], replicated
- grad_expert_up: float32 [16, 384, 1536], P('expert', 'dp')
- grad_expert_up_bias: float32 [16, 1536], P('expert', 'dp')
- grad_expert_down: float32 [16, 1536, 384], P('expert', 'dp')
- grad_expert_down_bias: float32 [16, 384], P('expert', 'dp')
- grad_shared_up: float32 [2, 384, 1536], replicated
- grad_shared_up_bias: float32 [2, 1536], replicated
- grad_shared_down: float32 [2, 1536, 384], replicated
- grad_shared_down_bias: float32 [2, 384], replicated
Inputs may be any that keep to these rules, and one draw needn't show every extreme that they name: `patch_counts`: the 5 images of a sequence fill its first slots in order; the remaining slots are padding. `expert_routes`: a slot's two experts differ; in each sequence at most 160 slots name one expert, and in some sequence one expert is named by exactly 160 slots.
All inputs are finite; a program needn't handle non-finite values.
Results may differ from a plain program's by a relative error of at most 0.015.
Values may be sent and summed in bfloat16 or wider, within the bound.
A program may use at most 256 MiB of HBM per device.

v0:
```python
import jax
import jax.numpy as jnp
from jax import lax
from jax.sharding import PartitionSpec as P

HEADS = 6
HDIM = 64
SHARED = 2
CAP = 160


NORM_EPS = 1e-06
MASK_FILL = -1e30
ROWS_FIRST = (((0,), (0,)), ((), ()))
ROWS_LAST = (((1,), (1,)), ((), ()))


def norm_rows(matrix):
    row_mean = jnp.mean(matrix, axis=-1, keepdims=True)
    centred = matrix - row_mean
    row_var = jnp.mean(centred * centred, axis=-1, keepdims=True)
    row_scale = lax.rsqrt(row_var + NORM_EPS)
    return (centred * row_scale, row_scale)


def norm_back(grad_in, normed, row_scale):
    grad_mean = jnp.mean(grad_in, axis=-1, keepdims=True)
    cross_mean = jnp.mean(grad_in * normed, axis=-1, keepdims=True)
    return (grad_in - grad_mean - normed * cross_mean) * row_scale


def gelu_tanh(matrix):
    return jax.nn.gelu(matrix, approximate=True)


def gelu_back(point, grad_out):
    return jax.vjp(gelu_tanh, point)[1](grad_out)[0]


def layout(patch_counts, expert_routes, slot_count, expert_count):
    image_count = patch_counts.shape[0]
    slot_ids = jnp.arange(slot_count, dtype=jnp.int32)
    image_ends = jnp.cumsum(patch_counts)
    image_starts = image_ends - patch_counts
    member = (slot_ids[:, None] >= image_starts[None, :]) & (
        slot_ids[:, None] < image_ends[None, :]
    )
    valid_rows = jnp.sum(member.astype(jnp.int32), axis=1)
    image_ids = jnp.arange(image_count, dtype=jnp.int32)
    segment = jnp.sum(jnp.where(member, image_ids[None, :], 0), axis=1) + (1 - valid_rows) * (
        image_count + slot_ids
    )
    expert_ids = jnp.arange(expert_count, dtype=jnp.int32)
    route_picks = (
        (expert_routes[:, :, None] == expert_ids[None, None, :]).astype(jnp.int32)
        * valid_rows[:, None, None]
    ).reshape(2 * slot_count, expert_count)
    earlier = jnp.cumsum(route_picks, axis=0) - route_picks
    position = jnp.sum(earlier * route_picks, axis=1).reshape(slot_count, 2)
    target = jnp.where(valid_rows[:, None] > 0, expert_routes * CAP + position, -1)
    return (member, valid_rows, segment, target)


def block_scores(query_rows, key_rows, segment, first_row, row_block, attn_scale):
    scores = (
        jnp.einsum("qhd,khd->hqk", query_rows, key_rows, preferred_element_type=jnp.float32)
        * attn_scale
    )
    allowed = segment[first_row : first_row + row_block, None] == segment[None, :]
    return jnp.where(allowed[None], scores, MASK_FILL)


def attend_forward(queries, key_rows, value_rows, segment, row_block, attn_scale):
    slot_count = queries.shape[0]
    outputs = []
    log_parts = []
    for first_row in range(0, slot_count, row_block):
        scores = block_scores(
            queries[first_row : first_row + row_block],
            key_rows,
            segment,
            first_row,
            row_block,
            attn_scale,
        )
        row_top = jnp.max(scores, axis=-1, keepdims=True)
        expo_scores = jnp.exp(scores - row_top)
        row_total = jnp.sum(expo_scores, axis=-1, keepdims=True)
        soft_probs = (expo_scores / row_total).astype(jnp.bfloat16)
        outputs.append(
            jnp.einsum(
                "hqk,khd->qhd", soft_probs, value_rows, preferred_element_type=jnp.float32
            ).astype(jnp.bfloat16)
        )
        log_parts.append(row_top + jnp.log(row_total))
    return (jnp.concatenate(outputs, axis=0), jnp.concatenate(log_parts, axis=1))


def attend_backward(
    queries, key_rows, value_rows, segment, log_totals, grad_attended, row_block, attn_scale
):
    slot_count = queries.shape[0]
    grad_query_parts = []
    grad_keys = jnp.zeros(key_rows.shape, jnp.float32)
    grad_values = jnp.zeros(value_rows.shape, jnp.float32)
    for first_row in range(0, slot_count, row_block):
        query_rows = queries[first_row : first_row + row_block]
        grad_rows_here = grad_attended[first_row : first_row + row_block]
        scores = block_scores(query_rows, key_rows, segment, first_row, row_block, attn_scale)
        soft_probs = jnp.exp(scores - log_totals[:, first_row : first_row + row_block])
        grad_probs = jnp.einsum(
            "qhd,khd->hqk", grad_rows_here, value_rows, preferred_element_type=jnp.float32
        )
        row_inner = jnp.sum(soft_probs * grad_probs, axis=-1, keepdims=True)
        grad_scores = (soft_probs * (grad_probs - row_inner)).astype(jnp.bfloat16)
        grad_query_parts.append(
            jnp.einsum("hqk,khd->qhd", grad_scores, key_rows, preferred_element_type=jnp.float32)
            * attn_scale
        )
        grad_keys = (
            grad_keys
            + jnp.einsum(
                "hqk,qhd->khd", grad_scores, query_rows, preferred_element_type=jnp.float32
            )
            * attn_scale
        )
        grad_values = grad_values + jnp.einsum(
            "hqk,qhd->khd",
            soft_probs.astype(jnp.bfloat16),
            grad_rows_here,
            preferred_element_type=jnp.float32,
        )
    return (jnp.concatenate(grad_query_parts, axis=0), grad_keys, grad_values)


def expert_hidden(expert_in, expert_up, expert_up_bias):
    expert_pre = (
        jnp.einsum("ecd,edh->ech", expert_in, expert_up, preferred_element_type=jnp.float32)
        + expert_up_bias[:, None, :]
    )
    return (expert_pre, gelu_tanh(expert_pre).astype(jnp.bfloat16))


def accumulate_expert_gradients(grad_up, grad_up_bias, grad_down, grad_down_bias):
    return (
        lax.psum_scatter(grad_up, "dp", scatter_dimension=1, tiled=True),
        lax.psum_scatter(grad_up_bias, "dp", scatter_dimension=1, tiled=True),
        lax.psum_scatter(grad_down, "dp", scatter_dimension=1, tiled=True),
        lax.psum_scatter(grad_down_bias, "dp", scatter_dimension=1, tiled=True),
    )


def body(
    tokens,
    cotangent,
    patch_counts,
    time_buckets,
    image_labels,
    expert_routes,
    time_table,
    label_table,
    ada_weight,
    ada_bias,
    qkv_weight,
    out_weight,
    out_bias,
    router_weight,
    expert_up,
    expert_up_bias,
    expert_down,
    expert_down_bias,
    shared_up,
    shared_up_bias,
    shared_down,
    shared_down_bias,
):
    slot_count, model_width = tokens.shape
    expert_count = router_weight.shape[1]
    local_count = expert_up.shape[0]
    owner_count = lax.axis_size("expert")
    row_block = min(512, slot_count)
    attn_scale = HDIM ** (-0.5)
    member, valid_rows, segment, target = layout(
        patch_counts[0], expert_routes[0], slot_count, expert_count
    )
    member_f = member.astype(jnp.float32)
    valid_f = valid_rows.astype(jnp.float32)[:, None]
    label_rows = jnp.take(label_table, image_labels[0], axis=0).astype(jnp.float32)
    time_row = jnp.take(time_table, time_buckets, axis=0).astype(jnp.float32)
    condition = label_rows + time_row
    cond_act = jax.nn.silu(condition).astype(jnp.bfloat16)
    modulation = jnp.dot(cond_act, ada_weight, preferred_element_type=jnp.float32) + ada_bias
    tok_mod = jnp.dot(member_f, modulation, precision=lax.Precision.HIGHEST)
    shift_one, scale_one, gate_one, shift_two, scale_two, gate_two = [
        tok_mod[:, part_index * model_width : (part_index + 1) * model_width]
        for part_index in range(6)
    ]
    inputs = tokens.astype(jnp.float32)
    normed_one, scale_rows_one = norm_rows(inputs)
    mixed_in = (normed_one * (1.0 + scale_one) + shift_one).astype(jnp.bfloat16)
    qkv_rows = jnp.dot(mixed_in, qkv_weight, preferred_element_type=jnp.float32).astype(
        jnp.bfloat16
    )
    queries = qkv_rows[:, :model_width].reshape(slot_count, HEADS, HDIM)
    key_rows = qkv_rows[:, model_width : 2 * model_width].reshape(slot_count, HEADS, HDIM)
    value_rows = qkv_rows[:, 2 * model_width :].reshape(slot_count, HEADS, HDIM)
    attended, log_totals = attend_forward(
        queries, key_rows, value_rows, segment, row_block, attn_scale
    )
    attended_flat = attended.reshape(slot_count, model_width)
    attn_out = jnp.dot(attended_flat, out_weight, preferred_element_type=jnp.float32) + out_bias
    hidden_one = inputs + valid_f * gate_one * attn_out
    normed_two, scale_rows_two = norm_rows(hidden_one)
    moe_in = (normed_two * (1.0 + scale_two) + shift_two).astype(jnp.bfloat16)
    logits = jnp.dot(moe_in, router_weight, preferred_element_type=jnp.float32)
    route_hot = (
        expert_routes[0][:, :, None] == jnp.arange(expert_count, dtype=jnp.int32)[None, None, :]
    ).astype(jnp.float32)
    chosen = jnp.sum(route_hot * logits[:, None, :], axis=2)
    gate_values = jax.nn.softmax(chosen, axis=1)
    slot_hot = (
        target[:, :, None] == jnp.arange(expert_count * CAP, dtype=jnp.int32)[None, None, :]
    ).astype(jnp.bfloat16)
    hot_first = slot_hot[:, 0]
    hot_second = slot_hot[:, 1]
    dispatch_hot = hot_first + hot_second
    routed_rows = lax.dot_general(
        dispatch_hot, moe_in, ROWS_FIRST, preferred_element_type=jnp.float32
    ).astype(jnp.bfloat16)
    send_rows = routed_rows.reshape(owner_count, local_count, CAP, model_width)
    expert_in = lax.all_to_all(send_rows, "expert", split_axis=0, concat_axis=2, tiled=True)[0]
    expert_pre, expert_act = expert_hidden(expert_in, expert_up, expert_up_bias)
    expert_res = (
        jnp.einsum("ech,ehd->ecd", expert_act, expert_down, preferred_element_type=jnp.float32)
        + expert_down_bias[:, None, :]
    ).astype(jnp.bfloat16)
    returned = lax.all_to_all(
        expert_res[None], "expert", split_axis=2, concat_axis=0, tiled=True
    ).reshape(expert_count * CAP, model_width)
    picked_first = jnp.dot(hot_first, returned, preferred_element_type=jnp.float32)
    picked_second = jnp.dot(hot_second, returned, preferred_element_type=jnp.float32)
    routed = gate_values[:, 0:1] * picked_first + gate_values[:, 1:2] * picked_second
    shared_total = jnp.zeros((slot_count, model_width), jnp.float32)
    shared_pres = []
    shared_acts = []
    for shared_index in range(SHARED):
        shared_pre = (
            jnp.dot(moe_in, shared_up[shared_index], preferred_element_type=jnp.float32)
            + shared_up_bias[shared_index]
        )
        shared_act = gelu_tanh(shared_pre).astype(jnp.bfloat16)
        shared_pres.append(shared_pre)
        shared_acts.append(shared_act)
        shared_total = (
            shared_total
            + jnp.dot(shared_act, shared_down[shared_index], preferred_element_type=jnp.float32)
            + shared_down_bias[shared_index]
        )
    branch = routed + shared_total
    hidden_two = hidden_one + valid_f * gate_two * branch
    slot_total = jnp.sum(valid_f) * model_width
    rms_stats = jnp.stack(
        [
            jnp.sqrt(jnp.sum(valid_f * hidden_two * hidden_two) / slot_total),
            jnp.sqrt(jnp.sum(valid_f * branch * branch) / slot_total),
        ]
    )[None, :]
    grad_out = cotangent.astype(jnp.float32)
    grad_branch = (valid_f * gate_two * grad_out).astype(jnp.bfloat16)
    grad_branch_f = grad_branch.astype(jnp.float32)
    grad_gate_two = valid_f * grad_out * branch
    grad_moe_in = jnp.zeros((slot_count, model_width), jnp.float32)
    grad_sdown_parts = []
    grad_sup_parts = []
    grad_sup_bias_parts = []
    for shared_index in range(SHARED):
        grad_sdown_parts.append(
            lax.dot_general(
                shared_acts[shared_index],
                grad_branch,
                ROWS_FIRST,
                preferred_element_type=jnp.float32,
            )
        )
        grad_shared_act = lax.dot_general(
            grad_branch, shared_down[shared_index], ROWS_LAST, preferred_element_type=jnp.float32
        )
        grad_shared_pre = gelu_back(shared_pres[shared_index], grad_shared_act).astype(jnp.bfloat16)
        grad_sup_parts.append(
            lax.dot_general(moe_in, grad_shared_pre, ROWS_FIRST, preferred_element_type=jnp.float32)
        )
        grad_sup_bias_parts.append(jnp.sum(grad_shared_pre.astype(jnp.float32), axis=0))
        grad_moe_in = grad_moe_in + lax.dot_general(
            grad_shared_pre, shared_up[shared_index], ROWS_LAST, preferred_element_type=jnp.float32
        )
    grad_sdown = jnp.stack(grad_sdown_parts)
    grad_sdown_bias = jnp.stack([jnp.sum(grad_branch_f, axis=0)] * SHARED)
    grad_sup = jnp.stack(grad_sup_parts)
    grad_sup_bias = jnp.stack(grad_sup_bias_parts)
    grad_gates = jnp.stack(
        [
            jnp.sum(picked_first * grad_branch_f, axis=1),
            jnp.sum(picked_second * grad_branch_f, axis=1),
        ],
        axis=1,
    )
    slot_gate = jnp.einsum(
        "tks,tk->s", slot_hot.astype(jnp.float32), gate_values, precision=lax.Precision.HIGHEST
    )
    picked_back = lax.dot_general(
        dispatch_hot, grad_branch, ROWS_FIRST, preferred_element_type=jnp.float32
    )
    grad_returned = (
        (picked_back * slot_gate[:, None])
        .astype(jnp.bfloat16)
        .reshape(owner_count, local_count, CAP, model_width)
    )
    grad_expert_res = lax.all_to_all(
        grad_returned, "expert", split_axis=0, concat_axis=2, tiled=True
    )[0]
    grad_expert_act = jnp.einsum(
        "ecd,ehd->ech", grad_expert_res, expert_down, preferred_element_type=jnp.float32
    )
    expert_preactivation_gradient = gelu_back(expert_pre, grad_expert_act).astype(jnp.bfloat16)
    expert_down_weight_gradient = jnp.einsum(
        "ech,ecd->ehd", expert_act, grad_expert_res, preferred_element_type=jnp.float32
    )
    expert_down_bias_gradient = jnp.sum(grad_expert_res.astype(jnp.float32), axis=1)
    expert_up_weight_gradient = jnp.einsum(
        "ecd,ech->edh", expert_in, expert_preactivation_gradient, preferred_element_type=jnp.float32
    )
    expert_up_bias_gradient = jnp.sum(expert_preactivation_gradient.astype(jnp.float32), axis=1)
    grad_expert_in = jnp.einsum(
        "ech,edh->ecd", expert_preactivation_gradient, expert_up, preferred_element_type=jnp.float32
    ).astype(jnp.bfloat16)
    grad_rows = lax.all_to_all(
        grad_expert_in[None], "expert", split_axis=2, concat_axis=0, tiled=True
    ).reshape(expert_count * CAP, model_width)
    grad_moe_in = grad_moe_in + jnp.dot(dispatch_hot, grad_rows, preferred_element_type=jnp.float32)
    gate_inner = jnp.sum(gate_values * grad_gates, axis=1, keepdims=True)
    grad_chosen = gate_values * (grad_gates - gate_inner)
    grad_logits = jnp.sum(route_hot * grad_chosen[:, :, None], axis=1).astype(jnp.bfloat16)
    grad_router = lax.dot_general(
        moe_in, grad_logits, ROWS_FIRST, preferred_element_type=jnp.float32
    )
    grad_moe_in = grad_moe_in + lax.dot_general(
        grad_logits, router_weight, ROWS_LAST, preferred_element_type=jnp.float32
    )
    grad_scale_two = grad_moe_in * normed_two
    grad_hidden_one = grad_out + norm_back(
        grad_moe_in * (1.0 + scale_two), normed_two, scale_rows_two
    )
    grad_attn = (valid_f * gate_one * grad_hidden_one).astype(jnp.bfloat16)
    grad_gate_one = valid_f * grad_hidden_one * attn_out
    grad_out_bias = jnp.sum(grad_attn.astype(jnp.float32), axis=0)
    grad_out_weight = lax.dot_general(
        attended_flat, grad_attn, ROWS_FIRST, preferred_element_type=jnp.float32
    )
    grad_attended = (
        lax.dot_general(grad_attn, out_weight, ROWS_LAST, preferred_element_type=jnp.float32)
        .astype(jnp.bfloat16)
        .reshape(slot_count, HEADS, HDIM)
    )
    grad_queries, grad_keys, grad_values = attend_backward(
        queries, key_rows, value_rows, segment, log_totals, grad_attended, row_block, attn_scale
    )
    grad_qkv = jnp.concatenate(
        [
            grad_queries.reshape(slot_count, model_width),
            grad_keys.reshape(slot_count, model_width),
            grad_values.reshape(slot_count, model_width),
        ],
        axis=1,
    ).astype(jnp.bfloat16)
    grad_qkv_weight = lax.dot_general(
        mixed_in, grad_qkv, ROWS_FIRST, preferred_element_type=jnp.float32
    )
    grad_mixed_in = lax.dot_general(
        grad_qkv, qkv_weight, ROWS_LAST, preferred_element_type=jnp.float32
    )
    grad_scale_one = grad_mixed_in * normed_one
    grad_tokens = grad_hidden_one + norm_back(
        grad_mixed_in * (1.0 + scale_one), normed_one, scale_rows_one
    )
    grad_tok_mod = jnp.concatenate(
        [grad_mixed_in, grad_scale_one, grad_gate_one, grad_moe_in, grad_scale_two, grad_gate_two],
        axis=1,
    )
    grad_modulation = lax.dot_general(
        member_f, grad_tok_mod, ROWS_FIRST, precision=lax.Precision.HIGHEST
    )
    grad_ada = lax.dot_general(
        cond_act.astype(jnp.float32), grad_modulation, ROWS_FIRST, precision=lax.Precision.HIGHEST
    )
    grad_ada_bias = jnp.sum(grad_modulation, axis=0)
    grad_cond_act = lax.dot_general(
        grad_modulation, ada_weight.astype(jnp.float32), ROWS_LAST, precision=lax.Precision.HIGHEST
    )
    grad_condition = jax.vjp(jax.nn.silu, condition)[1](grad_cond_act)[0]
    label_hot = (
        image_labels[0][:, None] == jnp.arange(label_table.shape[0], dtype=jnp.int32)[None, :]
    ).astype(jnp.float32)
    grad_label = lax.dot_general(
        label_hot, grad_condition, ROWS_FIRST, precision=lax.Precision.HIGHEST
    )
    time_hot = (
        time_buckets[:, None] == jnp.arange(time_table.shape[0], dtype=jnp.int32)[None, :]
    ).astype(jnp.float32)
    grad_time = lax.dot_general(
        time_hot,
        jnp.sum(grad_condition, axis=0, keepdims=True),
        ROWS_FIRST,
        precision=lax.Precision.HIGHEST,
    )
    expert_gradient_totals = accumulate_expert_gradients(
        expert_up_weight_gradient,
        expert_up_bias_gradient,
        expert_down_weight_gradient,
        expert_down_bias_gradient,
    )
    every_sum = lax.psum(
        (
            grad_qkv_weight,
            grad_out_weight,
            grad_out_bias,
            grad_ada,
            grad_ada_bias,
            grad_time,
            grad_label,
            grad_router,
            grad_sup,
            grad_sup_bias,
            grad_sdown,
            grad_sdown_bias,
        ),
        ("dp", "expert"),
    )
    (
        sum_qkv,
        sum_out_weight,
        sum_out_bias,
        sum_ada,
        sum_ada_bias,
        sum_time,
        sum_label,
        sum_router,
        sum_sup,
        sum_sup_bias,
        sum_sdown,
        sum_sdown_bias,
    ) = every_sum
    (
        summed_expert_up_weight,
        summed_expert_up_bias,
        summed_expert_down_weight,
        summed_expert_down_bias,
    ) = expert_gradient_totals
    return (
        hidden_two.astype(jnp.bfloat16),
        grad_tokens,
        rms_stats,
        sum_time,
        sum_label,
        sum_ada,
        sum_ada_bias,
        sum_qkv,
        sum_out_weight,
        sum_out_bias,
        sum_router,
        summed_expert_up_weight,
        summed_expert_up_bias,
        summed_expert_down_weight,
        summed_expert_down_bias,
        sum_sup,
        sum_sup_bias,
        sum_sdown,
        sum_sdown_bias,
    )


def solution(mesh):
    in_specs = (
        P(("dp", "expert"), None),
        P(("dp", "expert"), None),
        P(("dp", "expert"), None),
        P(("dp", "expert")),
        P(("dp", "expert"), None),
        P(("dp", "expert"), None, None),
        P(),
        P(),
        P(),
        P(),
        P(),
        P(),
        P(),
        P(),
        P("expert", None, None),
        P("expert", None),
        P("expert", None, None),
        P("expert", None),
        P(),
        P(),
        P(),
        P(),
    )
    out_specs = (
        P(("dp", "expert"), None),
        P(("dp", "expert"), None),
        P(("dp", "expert"), None),
        P(),
        P(),
        P(),
        P(),
        P(),
        P(),
        P(),
        P(),
        P("expert", "dp", None),
        P("expert", "dp"),
        P("expert", "dp", None),
        P("expert", "dp"),
        P(),
        P(),
        P(),
        P(),
    )
    return jax.shard_map(body, mesh=mesh, in_specs=in_specs, out_specs=out_specs, check_vma=False)
```

profile of v0, /device:TPU:0, one launch (start us, length us, event | category | flops | bytes accessed | tf_op | source)
XLA Modules:
  0.0 957.4 jit_solution(694431594901536008)
XLA Ops:
  19.9 4.0 fusion.112
  32.4 5.1 reduce-window.11
  51.3 3.4 fusion.142
  54.7 2.8 fusion.8
  59.2 3.3 fusion.74
  62.6 2.4 fusion.143
  65.0 2.8 fusion.7
  67.8 2.9 copy-done.1
  70.7 3.5 fusion.73
  78.1 11.8 %iota_compare_fusion = (pred[1024,2,2560]{2,0,1:T(32,128)(4,1)}, bf16[1024,2,2560]{2,0,1:T(8,128)(2,1)}) fusion(s32[1024,2]{0,1:T(2,128)S(1)} %copy.216), kind=kLoop, calls=%fused_computation.3 | loop fusion | flops 10485760 | bytes 15736832 | tf_op jit(solution)/shard_map/eq | solution.py:222
  89.9 8.3 convolution_convert_fusion
  98.2 4.8 all-to-all-start
  106.1 21.9 %all-to-all-done = bf16[4,4,160,384]{3,2,1,0:T(8,128)(2,1)} async-done(((bf16[4,4,160,384]{3,2,1,0:T(8,128)(2,1)}), bf16[4,4,160,384]{3,2,1,0:T(8,128)(2,1)}, u32[]{:S(2)}, u32[]{:S(2)}) %all-to-all-start) | async-done | bytes 1966112 | tf_op jit(solution)/shard_map/all_to_all | solution.py:231
  130.0 12.3 %multiply_convert_fusion = (bf16[4,640,1536]{2,1,0:T(8,128)(2,1)S(1)}, f32[4,640,1536]{2,1,0:T(8,128)}) fusion(f32[4,1536]{1,0:T(4,128)S(1)} %copy-done.90, bf16[4,640,384]{2,1,0:T(8,128)(2,1)S(1)} %bitcast.229, bf16[4,384,1536]{2,1,0:T(8,128)(2,1)} %param.36), kind=kOutput, calls=%fused_computation.12 | convolution fusion | flops 3059220480 | bytes 30302208 | tf_op jit(solution)/shard_map/ecd,edh->ech/dot_general | solution.py:138
  142.3 4.3 fusion.40
  146.6 2.8 copy.218
  149.4 4.4 all-to-all-start.1
  153.9 6.5 multiply_convert_fusion.4
  160.4 2.9 fusion.82
  163.3 4.5 fusion.79
  167.8 10.4 %all-to-all-done.1 = bf16[1,4,640,384]{3,1,0,2:T(4,128)(2,1)} async-done(((bf16[1,4,640,384]{3,1,0,2:T(4,128)(2,1)}), bf16[1,4,640,384]{3,1,0,2:T(4,128)(2,1)}, u32[]{:S(2)}, u32[]{:S(2)}) %all-to-all-start.1) | async-done | bytes 1966112 | tf_op jit(solution)/shard_map/all_to_all | solution.py:237
  180.3 4.7 fusion.13
  185.1 7.7 convert_reduce_fusion.4
  192.8 3.3 convolution_bitcast_fusion.1
  196.1 4.2 convolution_bitcast_fusion
  200.3 7.6 convert_reduce_fusion.1
  207.9 7.6 convert_reduce_fusion.2
  215.5 6.6 fusion.88
  222.2 4.6 fusion.39
  226.8 4.4 all-to-all-start.2
  231.2 5.0 pad_maximum_fusion.1
  239.6 2.5 pad_maximum_fusion
  242.1 13.5 %all-to-all-done.2 = bf16[4,4,160,384]{3,2,1,0:T(8,128)(2,1)} async-done(((bf16[4,4,160,384]{3,2,1,0:T(8,128)(2,1)}), bf16[4,4,160,384]{3,2,1,0:T(8,128)(2,1)}, u32[]{:S(2)}, u32[]{:S(2)}) %all-to-all-start.2) | async-done | bytes 1966112 | tf_op jit(solution)/shard_map/all_to_all | solution.py:318
  255.6 3.1 copy.227
  258.7 18.0 %convert_reduce_fusion = (f32[4,1536]{1,0:T(4,128)S(1)}, bf16[4,640,1536]{2,1,0:T(8,128)(2,1)S(1)}) fusion(f32[4,640,1536]{2,1,0:T(8,128)} %get-tuple-element.95, f32[4,1536]{1,0:T(4,128)S(1)} %copy-done.90, bf16[4,640,384]{2,1,0:T(8,128)(2,1)} %bitcast.231, bf16[4,1536,384]{2,1,0:T(8,128)(2,1)} %param.38), kind=kOutput, calls=%fused_computation.11 | convolution fusion | flops 3110332416 | bytes 30326784 | tf_op jit(solution)/shard_map/ecd,ehd->ech/dot_general | solution.py:321
  276.7 9.4 convert_bitcast_fusion
  286.2 2.8 copy.228
  289.0 4.4 all-to-all-start.3
  293.5 5.3 fusion.84
  298.8 3.0 fusion.77
  305.8 11.9 %all-to-all-done.3 = bf16[1,4,640,384]{3,1,0,2:T(4,128)(2,1)} async-done(((bf16[1,4,640,384]{3,1,0,2:T(4,128)(2,1)}), bf16[1,4,640,384]{3,1,0,2:T(4,128)(2,1)}, u32[]{:S(2)}, u32[]{:S(2)}) %all-to-all-start.3) | async-done | bytes 1966112 | tf_op jit(solution)/shard_map/all_to_all | solution.py:336
  320.0 6.0 fusion.127
  327.6 9.7 %fusion.60 = (f32[]{:T(128)}, f32[1024]{0:T(1024)S(1)}, f32[1024]{0:T(1024)S(1)}, f32[]{:T(128)}, bf16[1024,384]{1,0:T(8,128)(2,1)}, /*index=5*/f32[1024,384]{1,0:T(8,128)}) fusion(f32[1024]{0:T(1024)S(1)} %get-tuple-element.81, f32[1024,384]{1,0:T(8,128)S(1)} %copy-done.5, f32[1024,2304]{1,0:T(8,128)S(1)} %bitcast.219, f32[1024]{0:T(1024)S(1)} %copy-done.59, ...), kind=kOutput, calls=%fused_computation.112 | convolution fusion | flops 1233123328 | bytes 20878344 | tf_op jit(solution)/shard_map/dot_general | solution.py:256
  337.3 2.7 convert_reduce_fusion.6
  342.9 6.3 multiply_reduce_fusion.1
  349.2 10.0 %multiply_convert_fusion.2 = bf16[6,512,1024]{2,1,0:T(8,128)(2,1)} fusion(f32[6,512,1024]{2,1,0:T(8,128)} %get-tuple-element.99, f32[6,512,1024]{2,1,0:T(8,128)S(1)} %bitcast.213, f32[6,512]{1,0:T(8,128)S(1)} %get-tuple-element.98, f32[6,512]{1,0:T(8,128)S(1)} %copy-done.47), kind=kLoop, calls=%fused_computation.16 | loop fusion | flops 12582912 | bytes 31481856 | tf_op jit(solution)/shard_map/convert_element_type | solution.py:115
  359.2 5.8 fusion.72
  365.0 5.2 fusion.146
  370.3 3.2 fusion.30
  373.5 8.2 multiply_reduce_fusion
  381.7 4.5 add_convert_fusion.1
  386.2 6.4 multiply_convert_fusion.1
  396.1 2.5 fusion.97
  398.6 3.7 fusion.125
  402.3 3.3 fusion.53
  407.9 3.2 fusion.144
  412.7 3.5 fusion.123
  419.8 9.8 %fusion.149 = f32[4,1536,384]{2,1,0:T(8,128)} fusion(bf16[4,640,1536]{2,1,0:T(8,128)(2,1)} %copy-done.19, bf16[4,640,384]{2,1,0:T(8,128)(2,1)} %bitcast.232), kind=kOutput, calls=%fused_computation.270 | convolution fusion | flops 3019898880 | bytes 19267584 | tf_op jit(solution)/shard_map/ech,ecd->ehd/dot_general | solution.py:325
  430.0 11.5 %fusion.148 = f32[4,384,1536]{2,1,0:T(8,128)} fusion(bf16[4,640,384]{2,1,0:T(8,128)(2,1)} %bitcast.230, bf16[4,640,1536]{2,1,0:T(8,128)(2,1)} %copy-done.20), kind=kOutput, calls=%fused_computation.269 | convolution fusion | flops 3019898880 | bytes 19267584 | tf_op jit(solution)/shard_map/ecd,ech->edh/dot_general | solution.py:329
  448.2 45.0 %all-reduce = (f32[2304]{0:T(1024)}, f32[384]{0:T(512)}, f32[384,16]{0,1:T(8,128)}, f32[2,1536]{1,0:T(2,128)}, f32[2,384]{1,0:T(2,128)}) all-reduce(f32[2304]{0:T(1024)S(1)} %get-tuple-element.103, f32[384]{0:T(512)S(1)} %copy-done.75, f32[384,16]{0,1:T(8,128)S(1)} %fusion.150, ...), channel_id=1, replica_groups=mesh['dp'=8,'expert'=4] {'dp','expert'}, use_global_device_ids=true, to_apply=%region_35.36 | all-reduce | flops 12672 | bytes 101376 | tf_op jit(solution)/shard_map/psum | solution.py:421
  493.7 440.9 %all-reduce.4.cloned.1.call-done = (f32[1000,384]{1,0:T(8,128)}, f32[1001,384]{1,0:T(8,128)}, f32[384,2304]{1,0:T(8,128)}, f32[384,1152]{1,0:T(8,128)}, f32[384,...) async-done(((f32[1000,384]{1,0:T(8,128)}, f32[1001,384]{1,0:T(8,128)}, f32[384,2304]{1,0:T(8,128)}, f32[384,1152]{1,0:T(8,128)}, f32[384,384]{1,0:T(8,128)}, ...) | async-done | bytes 18408976 | tf_op jit(solution)/shard_map/psum | solution.py:421
  934.6 2.8 copy.275
  937.4 2.8 copy.276
  944.0 2.4 copy.280
  (377 shorter events, 83.3 us)
Async XLA Ops:
  8.0 10.8 %copy-start = (bf16[384,2304]{1,0:T(8,128)(2,1)S(1)}, bf16[384,2304]{1,0:T(8,128)(2,1)}, u32[]{:S(2)}) copy-start(bf16[384,2304]{1,0:T(8,128)(2,1)} %param.30) | copy-start | bytes 5308420
  8.8 15.0 %copy-start.78 = (pred[5]{0:T(512)(128)(4,1)}, pred[5]{0:T(512)(128)(4,1)S(1)}, u32[]{:S(2)}) copy-start(pred[5]{0:T(512)(128)(4,1)S(1)} %compare_and_fusion) | copy-start | bytes 19
  10.3 13.6 %copy-start.71 = (s32[5,1]{0,1:T(1,128)}, s32[5,1]{0,1:T(1,128)S(1)}, u32[]{:S(2)}) copy-start(s32[5,1]{0,1:T(1,128)S(1)} %reduce-window.10) | copy-start | bytes 64
  11.0 12.9 %copy-start.73 = (s32[5]{0:T(128)}, s32[5]{0:T(128)S(1)}, u32[]{:S(2)}) copy-start(s32[5]{0:T(128)S(1)} %fusion.120) | copy-start | bytes 64
  11.1 19.0 %copy-start.50 = (s32[1024]{0:T(1024)}, s32[1024]{0:T(1024)S(1)}, u32[]{:S(2)}) copy-start(s32[1024]{0:T(1024)S(1)} %get-tuple-element.43) | copy-start | bytes 12292
  12.1 27.4 %copy-start.16 = (s32[1,1024,2]{2,1,0:T(8,128)}, s32[1,1024,2]{2,1,0:T(8,128)S(1)}, u32[]{:S(2)}) copy-start(s32[1,1024,2]{2,1,0:T(8,128)S(1)} %copy.210) | copy-start | bytes 24580
  14.7 9.2 copy-start.61
  16.2 7.7 copy-start.65
  18.0 5.9 copy-start.54
  44.2 18.4 %copy-start.10 = (bf16[1024,384]{0,1:T(8,128)(2,1)}, bf16[1024,384]{0,1:T(8,128)(2,1)S(1)}, u32[]{:S(2)}) copy-start(bf16[1024,384]{0,1:T(8,128)(2,1)S(1)} %copy.207) | copy-start | bytes 2359300
  65.0 5.7 copy-start.1
  65.0 9.3 slice-start.6
  76.4 13.5 %copy-start.52 = (f32[1024]{0:T(1024)}, f32[1024]{0:T(1024)S(1)}, u32[]{:S(2)}) copy-start(f32[1024]{0:T(1024)S(1)} %broadcast_multiply_fusion.5) | copy-start | bytes 12292
  77.6 12.3 %copy-start.58 = (f32[1024]{0:T(1024)}, f32[1024]{0:T(1024)S(1)}, u32[]{:S(2)}) copy-start(f32[1024]{0:T(1024)S(1)} %add_rsqrt_fusion) | copy-start | bytes 12292
  78.1 159.6 %copy-start.13 = (bf16[1024,384]{1,0:T(8,128)(2,1)}, bf16[1024,384]{1,0:T(8,128)(2,1)S(1)}, u32[]{:S(2)}) copy-start(bf16[1024,384]{1,0:T(8,128)(2,1)S(1)} %fusion.62) | copy-start | bytes 2359300
  89.9 13.1 %copy-start.17 = (s32[1,1024,2]{2,1,0:T(8,128)S(1)}, s32[1,1024,2]{2,1,0:T(8,128)}, u32[]{:S(2)}) copy-start(s32[1,1024,2]{2,1,0:T(8,128)} %copy-done.16) | copy-start | bytes 24580
  89.9 13.3 %copy-start.63 = (bf16[384,16]{0,1:T(8,128)(2,1)S(1)}, bf16[384,16]{0,1:T(8,128)(2,1)}, u32[]{:S(2)}) copy-start(bf16[384,16]{0,1:T(8,128)(2,1)} %param.35) | copy-start | bytes 36868
  98.2 6.0 copy-start.80
  98.2 6.6 copy-start.70
  98.2 31.7 %copy-start.90 = (f32[4,1536]{1,0:T(4,128)S(1)}, f32[4,1536]{1,0:T(4,128)}, u32[]{:S(2)}) copy-start(f32[4,1536]{1,0:T(4,128)} %param.37) | copy-start | bytes 73732
  98.2 29.7 %all-to-all-start = ((bf16[4,4,160,384]{3,2,1,0:T(8,128)(2,1)}), bf16[4,4,160,384]{3,2,1,0:T(8,128)(2,1)}, u32[]{:S(2)}, u32[]{:S(2)}) async-start(bf16[4,4,160,384]{3,2,1,0:T(8,128)(2,1)} %bitcast.256), calls=%async_computation | async-start | bytes 3932160 | tf_op jit(solution)/shard_map/all_to_all | solution.py:231
  103.2 39.1 %copy-start.56 = (s32[1024,2]{0,1:T(2,128)}, s32[1024,2]{0,1:T(2,128)S(1)}, u32[]{:S(2)}) copy-start(s32[1024,2]{0,1:T(2,128)S(1)} %copy.211) | copy-start | bytes 24580
  128.0 14.3 %slice-start.23 = ((s8[4718592]{0:T(1024)(128)(4,1)}), s8[4194304]{0:T(1024)(128)(4,1)S(1)}, s32[]{:S(2)}) async-start(s8[4718592]{0:T(1024)(128)(4,1)} %bitcast.284), calls=%async_computation.36 | async-start | bytes 8388608
  129.9 12.4 %copy-start.21 = (bf16[1,4,4,160,384]{4,3,2,1,0:T(8,128)(2,1)}, bf16[1,4,4,160,384]{4,3,2,1,0:T(8,128)(2,1)S(1)}, u32[]{:S(2)}) copy-start(bf16[1,4,4,160,384]{4,3,2,1,0:T(8,128)(2,1)S(1)} %copy.217) | copy-start | bytes 5898244
  129.9 12.4 %slice-start.24 = ((s8[4718592]{0:T(1024)(128)(4,1)}), s8[524288]{0:T(1024)(128)(4,1)S(1)}, s32[]{:S(2)}) async-start(s8[4718592]{0:T(1024)(128)(4,1)} %bitcast.284), calls=%async_computation.37 | async-start | bytes 1048576
  129.9 12.4 %copy-start.91 = (f32[4,384]{1,0:T(4,128)S(1)}, f32[4,384]{1,0:T(4,128)}, u32[]{:S(2)}) copy-start(f32[4,384]{1,0:T(4,128)} %param.39) | copy-start | bytes 18436
  149.4 28.8 %all-to-all-start.1 = ((bf16[1,4,640,384]{3,1,0,2:T(4,128)(2,1)}), bf16[1,4,640,384]{3,1,0,2:T(4,128)(2,1)}, u32[]{:S(2)}, u32[]{:S(2)}) async-start(bf16[1,4,640,384]{3,1,0,2:T(4,128)(2,1)} %copy.218), calls=%async_computation.1 | async-start | bytes 3932160 | tf_op jit(solution)/shard_map/all_to_all | solution.py:237
  153.8 6.5 copy-start.86
  180.3 15.8 %slice-start.15 = ((s8[6291456]{0:T(1024)(128)(4,1)}), s8[4194304]{0:T(1024)(128)(4,1)S(1)}, s32[]{:S(2)}) async-start(s8[6291456]{0:T(1024)(128)(4,1)} %bitcast.227), calls=%async_computation.28 | async-start | bytes 8388608
  185.0 7.7 copy-start.97
  185.0 7.7 copy-start.96
  185.1 11.0 %slice-start.16 = ((s8[6291456]{0:T(1024)(128)(4,1)}), s8[2097152]{0:T(1024)(128)(4,1)S(1)}, s32[]{:S(2)}) async-start(s8[6291456]{0:T(1024)(128)(4,1)} %bitcast.227), calls=%async_computation.29 | async-start | bytes 4194304
  196.1 11.8 %slice-start.25 = ((s8[6291456]{0:T(1024)(128)(4,1)}), s8[4194304]{0:T(1024)(128)(4,1)S(1)}, s32[]{:S(2)}) async-start(s8[6291456]{0:T(1024)(128)(4,1)} %bitcast.287), calls=%async_computation.38 | async-start | bytes 8388608
  200.3 7.6 slice-start.26
  207.9 14.3 %slice-start.12 = ((s8[10485760]{0:T(1024)(128)(4,1)}), s8[4194304]{0:T(1024)(128)(4,1)S(1)}, s32[]{:S(2)}) async-start(s8[10485760]{0:T(1024)(128)(4,1)} %bitcast.225), calls=%async_computation.25 | async-start | bytes 8388608
  207.9 14.3 %slice-start.13 = ((s8[10485760]{0:T(1024)(128)(4,1)}), s8[4194304]{0:T(1024)(128)(4,1)S(1)}, s32[]{:S(2)}) async-start(s8[10485760]{0:T(1024)(128)(4,1)} %bitcast.225), calls=%async_computation.26 | async-start | bytes 8388608
  207.9 14.3 %slice-start.14 = ((s8[10485760]{0:T(1024)(128)(4,1)}), s8[2097152]{0:T(1024)(128)(4,1)S(1)}, s32[]{:S(2)}) async-start(s8[10485760]{0:T(1024)(128)(4,1)} %bitcast.225), calls=%async_computation.27 | async-start | bytes 4194304
  226.8 28.8 %all-to-all-start.2 = ((bf16[4,4,160,384]{3,2,1,0:T(8,128)(2,1)}), bf16[4,4,160,384]{3,2,1,0:T(8,128)(2,1)}, u32[]{:S(2)}, u32[]{:S(2)}) async-start(bf16[4,4,160,384]{3,2,1,0:T(8,128)(2,1)} %bitcast.257), calls=%async_computation.2 | async-start | bytes 3932160 | tf_op jit(solution)/shard_map/all_to_all | solution.py:318
  276.7 9.4 copy-start.20
  289.0 28.8 %all-to-all-start.3 = ((bf16[1,4,640,384]{3,1,0,2:T(4,128)(2,1)}), bf16[1,4,640,384]{3,1,0,2:T(4,128)(2,1)}, u32[]{:S(2)}, u32[]{:S(2)}) async-start(bf16[1,4,640,384]{3,1,0,2:T(4,128)(2,1)} %copy.228), calls=%async_computation.3 | async-start | bytes 3932160 | tf_op jit(solution)/shard_map/all_to_all | solution.py:336
  293.4 150.4 %reduce-scatter.15.cloned.1.call-start = ((), (), s32[]{:S(2)}) async-start(), calls=%async_computation.11 | async-start | bytes 221184
  304.5 140.7 %reduce-scatter.13.cloned.1.call-start = ((), (), s32[]{:S(2)}) async-start(), calls=%async_computation.10 | async-start | bytes 884736
  305.8 628.8 %all-reduce.4.cloned.1.call-start = ((), (), s32[]{:S(2)}) async-start(), calls=%async_computation.12 | async-start | bytes 36839424 | tf_op jit(solution)/shard_map/psum | solution.py:421
  317.7 8.7 slice-start.9
  319.9 6.0 copy-start.37
  319.9 6.0 copy-start.38
  320.0 6.0 copy-start.64
  320.0 6.5 slice-start.10
  320.0 6.6 slice-start.11
  326.0 16.8 %slice-start = ((s8[12582912]{0:T(1024)(128)(4,1)}), s8[4194304]{0:T(1024)(128)(4,1)S(1)}, s32[]{:S(2)}) async-start(s8[12582912]{0:T(1024)(128)(4,1)} %bitcast.212), calls=%async_computation.13 | async-start | bytes 8388608
  326.5 10.8 %copy-start.6 = (f32[1024,384]{1,0:T(8,128)}, f32[1024,384]{1,0:T(8,128)S(1)}, u32[]{:S(2)}) copy-start(f32[1024,384]{1,0:T(8,128)S(1)} %add_add_fusion) | copy-start | bytes 4718596
  327.6 15.3 %slice-start.1 = ((s8[12582912]{0:T(1024)(128)(4,1)}), s8[4194304]{0:T(1024)(128)(4,1)S(1)}, s32[]{:S(2)}) async-start(s8[12582912]{0:T(1024)(128)(4,1)} %bitcast.212), calls=%async_computation.14 | async-start | bytes 8388608
  327.6 15.3 %slice-start.2 = ((s8[12582912]{0:T(1024)(128)(4,1)}), s8[4194304]{0:T(1024)(128)(4,1)S(1)}, s32[]{:S(2)}) async-start(s8[12582912]{0:T(1024)(128)(4,1)} %bitcast.212), calls=%async_computation.15 | async-start | bytes 8388608
  349.2 10.0 %copy-start.11 = (bf16[1024,384]{0,1:T(8,128)(2,1)S(1)}, bf16[1024,384]{0,1:T(8,128)(2,1)}, u32[]{:S(2)}) copy-start(bf16[1024,384]{0,1:T(8,128)(2,1)} %copy-done.10) | copy-start | bytes 2359300
  349.2 21.0 %slice-start.3 = ((s8[12582912]{0:T(1024)(128)(4,1)}), s8[4194304]{0:T(1024)(128)(4,1)S(1)}, s32[]{:S(2)}) async-start(s8[12582912]{0:T(1024)(128)(4,1)} %bitcast.214), calls=%async_computation.16 | async-start | bytes 8388608
  349.2 21.0 %slice-start.4 = ((s8[12582912]{0:T(1024)(128)(4,1)}), s8[4194304]{0:T(1024)(128)(4,1)S(1)}, s32[]{:S(2)}) async-start(s8[12582912]{0:T(1024)(128)(4,1)} %bitcast.214), calls=%async_computation.17 | async-start | bytes 8388608
  359.2 5.8 copy-start.29
  359.2 11.0 %slice-start.5 = ((s8[12582912]{0:T(1024)(128)(4,1)}), s8[4194304]{0:T(1024)(128)(4,1)S(1)}, s32[]{:S(2)}) async-start(s8[12582912]{0:T(1024)(128)(4,1)} %bitcast.214), calls=%async_computation.18 | async-start | bytes 8388608
  386.1 6.4 copy-start.12
  411.1 7.3 copy-start.69
  419.8 514.9 %reduce-scatter.11.cloned.1.call-start = ((), (), s32[]{:S(2)}) async-start(), calls=%async_computation.9 | async-start | bytes 10616832 | tf_op jit(solution)/shard_map/reduce_scatter | solution.py:148
  429.7 505.0 %reduce-scatter.9.cloned.1.call-start = ((), (), s32[]{:S(2)}) async-start(), calls=%async_computation.8 | async-start | bytes 10616832 | tf_op jit(solution)/shard_map/reduce_scatter | solution.py:146
  441.5 6.6 copy-start.75
  937.4 6.6 slice-start.21
  (70 other events, 225.1 us)
Sparse Core Ops, SparseCore 0:
  304.6 63.5 reduce-scatter.14
  371.5 66.9 reduce-scatter.12
  443.1 210.6 reduce-scatter.10
  658.3 203.0 reduce-scatter.8
Sparse Core Ops, SparseCore 1:
  419.9 514.7 all-reduce.3
where the time goes:
time: 965 us; the launch traced here: 957 us
  waiting for transfers between devices  499 us (52%)
  matrix products  238 us (25%)
  other arithmetic  70.8 us (7%)
  local copies, waits for them, and re-layouts  66.4 us (7%)
  blocking collectives  45 us (5%)
  between operations  20.2 us (2%)
  starting transfers between devices  18.5 us (2%)
    psum x1, waiting for transfers between devices, body(): lax.psum((grad_qkv_weight, grad_out_weight, grad_out_bias, grad_ada, grad...  441 us
    psum x1, blocking collectives, body(): lax.psum((grad_qkv_weight, grad_out_weight, grad_out_bias, grad_ada, grad...  45 us
    unnamed x263, local copies, waits for them, and re-layouts  32 us
    all_to_all x1, waiting for transfers between devices, body(): lax.all_to_all(send_rows, 'expert', split_axis=0, concat_axis=2, tiled=True)  21.9 us
  transfers between devices with their start and end apart: 9, of which 5 were waited for; matrix products, arithmetic and copies ran while one was open for 17% of the time, Pallas kernels for 0%

commit v1 on v0

v1 whole, which is shorter than its diff:
```python
import functools

import jax
import jax.numpy as jnp
from jax import lax
from jax.experimental import pallas as pl
from jax.experimental.pallas import tpu as pltpu
from jax.sharding import Mesh, PartitionSpec as P

HEADS = 6
HDIM = 64
CAP = 160
PAD = 16
NORM_EPS = 1e-06
MASK_FILL = -1e30
ROWS_FIRST = (((0,), (0,)), ((), ()))
ROWS_LAST = (((1,), (1,)), ((), ()))
GELU_C = 0.7978845608028654
GELU_K = 0.044715
ALL = ("p0", "p1", "p2", "expert")
GROUP = ("p1", "p2", "expert")
F32 = jnp.float32
BF16 = jnp.bfloat16


def norm_rows(matrix):
    row_mean = jnp.mean(matrix, axis=-1, keepdims=True)
    centred = matrix - row_mean
    row_var = jnp.mean(centred * centred, axis=-1, keepdims=True)
    row_scale = lax.rsqrt(row_var + NORM_EPS)
    return (centred * row_scale, row_scale)


def norm_back(grad_in, normed, row_scale):
    grad_mean = jnp.mean(grad_in, axis=-1, keepdims=True)
    cross_mean = jnp.mean(grad_in * normed, axis=-1, keepdims=True)
    return (grad_in - grad_mean - normed * cross_mean) * row_scale


def high_low(values):
    high = values.astype(BF16)
    return (high, (values - high.astype(F32)).astype(BF16))


def ffn_kernel(
    routed,
    sources,
    row_block,
    pick_ref,
    x_ref,
    g_ref,
    up_ref,
    bu_ref,
    dn_ref,
    bd_ref,
    y_ref,
    dx_ref,
    dup_ref,
    dbu_ref,
    ddn_ref,
    dbd_ref,
    xs,
    gs,
    xt,
    gt,
    acts,
    dpres,
    yacc,
    dxacc,
    gate_rows,
    gate_cols,
):
    net = pl.program_id(0)
    chunk = pl.program_id(1)
    nets = pl.num_programs(0)
    chunks = pl.num_programs(1)
    rows, width = xs.shape

    @pl.when((net == 0) & (chunk == 0))
    def _():
        if routed:
            gate_rows[...] = jnp.zeros_like(gate_rows)
            for s in range(sources):
                xs[s * CAP : (s + 1) * CAP, :] = x_ref[s, :CAP, :]
                tail = x_ref[s, CAP : CAP + PAD, :256].astype(F32)
                gate_rows[s : s + 1, :] = tail[0:1] + tail[1:2]
            gate_cols[...] = gate_rows[...].T
            for s in range(sources):
                gate = gate_cols[:CAP, s : s + 1]
                gs[s * CAP : (s + 1) * CAP, :] = (g_ref[s].astype(F32) * gate).astype(BF16)
        else:
            xs[...] = x_ref[...]
            gs[...] = g_ref[...]
        for r in range(0, rows, 256):
            xt[:width, r : r + 256] = xs[r : r + 256, :].T
            gt[:, r : r + 256] = gs[r : r + 256, :].T
        xt[width:, :] = jnp.ones((xt.shape[0] - width, rows), BF16)
        yacc[...] = jnp.zeros_like(yacc)
        dxacc[...] = jnp.zeros_like(dxacc)
        dbd_ref[...] = jnp.sum(gs[...].astype(F32), axis=0, keepdims=True)

    up = up_ref[0]
    dn = dn_ref[0]
    bu = bu_ref[0]

    def block(i, carry):
        r = pl.ds(pl.multiple_of(i * row_block, row_block), row_block)
        pre = jnp.dot(xs[r, :], up, preferred_element_type=F32) + bu
        dact = lax.dot_general(gs[r, :], dn, ROWS_LAST, preferred_element_type=F32)
        square = pre * pre
        th = jnp.tanh(pre * (GELU_C + (GELU_C * GELU_K) * square))
        half = 0.5 + 0.5 * th
        act = (pre * half).astype(BF16)
        slope = half + (0.5 * pre) * (1.0 - th * th) * (GELU_C + (3 * GELU_C * GELU_K) * square)
        dpre = (dact * slope).astype(BF16)
        acts[r, :] = act
        dpres[r, :] = dpre
        yacc[r, :] += jnp.dot(act, dn, preferred_element_type=F32)
        dxacc[r, :] += lax.dot_general(dpre, up, ROWS_LAST, preferred_element_type=F32)
        return carry

    lax.fori_loop(0, rows // row_block, block, 0)
    dup = jnp.dot(xt[...], dpres[...], preferred_element_type=F32)
    dup_ref[0] = dup[:width].astype(BF16)
    dbu_ref[0] = dup[width : width + 1]
    ddn_ref[0] = jnp.dot(gt[...], acts[...], preferred_element_type=F32).T.astype(BF16)

    @pl.when((net == nets - 1) & (chunk == chunks - 1))
    def _():
        if routed:
            gate_rows[...] = jnp.zeros_like(gate_rows)
            place = lax.broadcasted_iota(jnp.int32, (CAP, 128), 1)
            total = jnp.zeros((CAP, 128), F32)
            for s in range(sources):
                r = slice(s * CAP, (s + 1) * CAP)
                res = (yacc[r, :] + bd_ref[0]).astype(BF16).astype(F32)
                gate = gate_cols[:CAP, s : s + 1]
                y_ref[s] = (res * gate).astype(BF16)
                inner = jnp.sum(res * g_ref[s].astype(F32), axis=1, keepdims=True)
                total = jnp.where(place == s, inner, total)
                dx_ref[s, :CAP, :] = dxacc[r, :].astype(BF16)
            gate_cols[:CAP, :] = total
            gate_rows[...] = gate_cols[...].T
            for s in range(sources):
                row = gate_rows[s : s + 1, :]
                high = row.astype(BF16).astype(F32)
                low = row - high
                rest = jnp.zeros((PAD - 2, 256), F32)
                tail = jnp.concatenate([high, low, rest], axis=0)
                tail = jnp.concatenate([tail, jnp.zeros((PAD, width - 256), F32)], axis=1)
                dx_ref[s, CAP : CAP + PAD, :] = tail.astype(BF16)
        else:
            bias = jnp.sum(bd_ref[...], axis=0)
            y_ref[...] = yacc[...] + bias
            dx_ref[...] = dxacc[...]


def ffn(routed, pick, x, g, up, bias_up, down, bias_down, chunk=256, row_block=320):
    nets = 1 if routed else up.shape[0]
    width, hidden = up.shape[1:]
    if routed:
        sources = x.shape[0]
        rows = sources * CAP
        y_shape = jax.ShapeDtypeStruct((sources, CAP, width), BF16)
        dx_shape = jax.ShapeDtypeStruct((sources, CAP + PAD, width), BF16)
    else:
        sources = 1
        rows = x.shape[0]
        y_shape = jax.ShapeDtypeStruct((rows, width), F32)
        dx_shape = y_shape

    def whole(shape):
        return pl.BlockSpec(shape, lambda n, h, p: (0,) * len(shape))

    flops = 12 * nets * rows * width * hidden
    return pl.pallas_call(
        functools.partial(ffn_kernel, routed, sources, row_block),
        grid_spec=pltpu.PrefetchScalarGridSpec(
            num_scalar_prefetch=1,
            grid=(nets, hidden // chunk),
            in_specs=[
                whole(x.shape),
                whole(g.shape),
                pl.BlockSpec((1, width, chunk), lambda n, h, p: (p[0] + n, 0, h)),
                pl.BlockSpec((1, 1, chunk), lambda n, h, p: (p[0] + n, 0, h)),
                pl.BlockSpec((1, chunk, width), lambda n, h, p: (p[0] + n, h, 0)),
                pl.BlockSpec((nets, 1, width), lambda n, h, p: (p[0], 0, 0)),
            ],
            out_specs=[
                whole(y_shape.shape),
                whole(dx_shape.shape),
                pl.BlockSpec((1, width, chunk), lambda n, h, p: (n, 0, h)),
                pl.BlockSpec((1, 1, chunk), lambda n, h, p: (n, 0, h)),
                pl.BlockSpec((1, chunk, width), lambda n, h, p: (n, h, 0)),
                whole((1, width)),
            ],
            scratch_shapes=[
                pltpu.VMEM((rows, width), BF16),
                pltpu.VMEM((rows, width), BF16),
                pltpu.VMEM((width + 16, rows), BF16),
                pltpu.VMEM((width, rows), BF16),
                pltpu.VMEM((rows, chunk), BF16),
                pltpu.VMEM((rows, chunk), BF16),
                pltpu.VMEM((rows, width), F32),
                pltpu.VMEM((rows, width), F32),
                pltpu.VMEM((128, 256), F32),
                pltpu.VMEM((256, 128), F32),
            ],
        ),
        out_shape=[
            y_shape,
            dx_shape,
            jax.ShapeDtypeStruct((nets, width, hidden), BF16),
            jax.ShapeDtypeStruct((nets, 1, hidden), F32),
            jax.ShapeDtypeStruct((nets, hidden, width), BF16),
            jax.ShapeDtypeStruct((1, width), F32),
        ],
        compiler_params=pltpu.CompilerParams(vmem_limit_bytes=56 * 2**20),
        cost_estimate=pl.CostEstimate(
            flops=flops, bytes_accessed=16 * 2**20, transcendentals=nets * rows * hidden
        ),
        name="routed_net" if routed else "shared_net",
    )(pick, x, g, up, bias_up[:, None, :], down, bias_down[:, None, :])


def exchange(blocks, axes):
    return lax.all_to_all(blocks, axes, split_axis=0, concat_axis=0, tiled=True)


def spread(block, axes):
    count = lax.axis_size(axes)
    return exchange(jnp.broadcast_to(block[None], (count,) + block.shape), axes)


def sum_blocks(blocks):
    return jnp.sum(blocks.astype(F32), axis=0)


def sum_everywhere(payload):
    rows, width = payload.shape
    near = ("p2", "expert")
    far = ("p0", "p1")
    near_count = lax.axis_size(near)
    far_count = lax.axis_size(far)
    piece = rows // near_count
    part = exchange(payload.astype(BF16).reshape(near_count, piece, width), near)
    part = sum_blocks(part).astype(BF16)
    part = part.reshape(piece, far_count, width // far_count).transpose(1, 0, 2)
    part = sum_blocks(exchange(part, far)).astype(BF16)
    part = spread(part, far).transpose(1, 0, 2).reshape(piece, width)
    return spread(part, near).reshape(rows, width)


def layout(patch_counts, expert_routes, slot_count, expert_count):
    image_count = patch_counts.shape[0]
    slot_ids = jnp.arange(slot_count, dtype=jnp.int32)
    image_ends = jnp.cumsum(patch_counts)
    image_starts = image_ends - patch_counts
    member = (slot_ids[:, None] >= image_starts[None, :]) & (
        slot_ids[:, None] < image_ends[None, :]
    )
    valid_rows = jnp.sum(member.astype(jnp.int32), axis=1)
    image_ids = jnp.arange(image_count, dtype=jnp.int32)
    segment = jnp.sum(jnp.where(member, image_ids[None, :], 0), axis=1) + (1 - valid_rows) * (
        image_count + slot_ids
    )
    expert_ids = jnp.arange(expert_count, dtype=jnp.int32)
    route_picks = (
        (expert_routes[:, :, None] == expert_ids[None, None, :]).astype(jnp.int32)
        * valid_rows[:, None, None]
    ).reshape(2 * slot_count, expert_count)
    earlier = jnp.cumsum(route_picks, axis=0) - route_picks
    position = jnp.sum(earlier * route_picks, axis=1).reshape(slot_count, 2)
    return (member, valid_rows, segment, position)


def block_scores(query_rows, key_rows, segment, first_row, row_block, attn_scale):
    scores = (
        jnp.einsum("qhd,khd->hqk", query_rows, key_rows, preferred_element_type=F32) * attn_scale
    )
    allowed = segment[first_row : first_row + row_block, None] == segment[None, :]
    return jnp.where(allowed[None], scores, MASK_FILL)


def attend_forward(queries, key_rows, value_rows, segment, row_block, attn_scale):
    slot_count = queries.shape[0]
    outputs = []
    log_parts = []
    for first_row in range(0, slot_count, row_block):
        scores = block_scores(
            queries[first_row : first_row + row_block],
            key_rows,
            segment,
            first_row,
            row_block,
            attn_scale,
        )
        row_top = jnp.max(scores, axis=-1, keepdims=True)
        expo_scores = jnp.exp(scores - row_top)
        row_total = jnp.sum(expo_scores, axis=-1, keepdims=True)
        soft_probs = (expo_scores / row_total).astype(BF16)
        outputs.append(
            jnp.einsum(
                "hqk,khd->qhd", soft_probs, value_rows, preferred_element_type=F32
            ).astype(BF16)
        )
        log_parts.append(row_top + jnp.log(row_total))
    return (jnp.concatenate(outputs, axis=0), jnp.concatenate(log_parts, axis=1))


def attend_backward(
    queries, key_rows, value_rows, segment, log_totals, grad_attended, row_block, attn_scale
):
    slot_count = queries.shape[0]
    grad_query_parts = []
    grad_keys = jnp.zeros(key_rows.shape, F32)
    grad_values = jnp.zeros(value_rows.shape, F32)
    for first_row in range(0, slot_count, row_block):
        query_rows = queries[first_row : first_row + row_block]
        grad_rows_here = grad_attended[first_row : first_row + row_block]
        scores = block_scores(query_rows, key_rows, segment, first_row, row_block, attn_scale)
        soft_probs = jnp.exp(scores - log_totals[:, first_row : first_row + row_block])
        grad_probs = jnp.einsum(
            "qhd,khd->hqk", grad_rows_here, value_rows, preferred_element_type=F32
        )
        row_inner = jnp.sum(soft_probs * grad_probs, axis=-1, keepdims=True)
        grad_scores = (soft_probs * (grad_probs - row_inner)).astype(BF16)
        grad_query_parts.append(
            jnp.einsum("hqk,khd->qhd", grad_scores, key_rows, preferred_element_type=F32)
            * attn_scale
        )
        grad_keys = (
            grad_keys
            + jnp.einsum("hqk,qhd->khd", grad_scores, query_rows, preferred_element_type=F32)
            * attn_scale
        )
        grad_values = grad_values + jnp.einsum(
            "hqk,qhd->khd", soft_probs.astype(BF16), grad_rows_here, preferred_element_type=F32
        )
    return (jnp.concatenate(grad_query_parts, axis=0), grad_keys, grad_values)


def body(
    tokens,
    cotangent,
    patch_counts,
    time_buckets,
    image_labels,
    expert_routes,
    time_table,
    label_table,
    ada_weight,
    ada_bias,
    qkv_weight,
    out_weight,
    out_bias,
    router_weight,
    expert_up,
    expert_up_bias,
    expert_down,
    expert_down_bias,
    shared_up,
    shared_up_bias,
    shared_down,
    shared_down_bias,
):
    slot_count, width = tokens.shape
    expert_count = router_weight.shape[1]
    local_count, _, hidden = expert_up.shape
    owners = lax.axis_size("expert")
    dp_count = lax.axis_size(("p0", "p1", "p2"))
    outer = lax.axis_size("p0")
    my_pick = lax.axis_index("p1") * lax.axis_size("p2") + lax.axis_index("p2")
    row_block = min(512, slot_count)
    attn_scale = HDIM ** (-0.5)
    routes = expert_routes[0]

    label_rows = jnp.take(label_table, image_labels[0], axis=0).astype(F32)
    time_row = jnp.take(time_table, time_buckets, axis=0).astype(F32)
    condition = label_rows + time_row
    cond_act = jax.nn.silu(condition).astype(BF16)
    modulation = jnp.dot(cond_act, ada_weight, preferred_element_type=F32) + ada_bias
    all_ids = spread(jnp.concatenate([image_labels, time_buckets[:, None]], axis=1), ALL)
    all_labels = all_ids[:, 0, :-1].reshape(-1)
    all_times = all_ids[:, 0, -1]

    member, valid_rows, segment, position = layout(
        patch_counts[0], routes, slot_count, expert_count
    )
    member_f = member.astype(F32)
    valid_f = valid_rows.astype(F32)[:, None]
    tok_mod = jnp.dot(member_f, modulation, precision=lax.Precision.HIGHEST)
    shift_one, scale_one, gate_one, shift_two, scale_two, gate_two = [
        tok_mod[:, part_index * width : (part_index + 1) * width] for part_index in range(6)
    ]

    block_of = (routes % local_count) * owners + routes // local_count
    target = jnp.where(valid_rows[:, None] > 0, block_of * CAP + position, -1)
    slots = jnp.arange(expert_count * CAP, dtype=jnp.int32)[:, None]
    hot = ((slots == target[None, :, 0]) | (slots == target[None, :, 1])).astype(BF16)

    grad_out = cotangent.astype(F32)
    grad_branch = (valid_f * gate_two * grad_out).astype(BF16)
    grad_branch_f = grad_branch.astype(F32)
    branch_rows = jnp.dot(hot, grad_branch, preferred_element_type=F32).astype(BF16)
    owner_branch = exchange(branch_rows.reshape(expert_count, CAP, width), GROUP)

    inputs = tokens.astype(F32)
    normed_one, scale_rows_one = norm_rows(inputs)
    mixed_in = (normed_one * (1.0 + scale_one) + shift_one).astype(BF16)
    qkv_rows = jnp.dot(mixed_in, qkv_weight, preferred_element_type=F32).astype(BF16)
    queries = qkv_rows[:, :width].reshape(slot_count, HEADS, HDIM)
    key_rows = qkv_rows[:, width : 2 * width].reshape(slot_count, HEADS, HDIM)
    value_rows = qkv_rows[:, 2 * width :].reshape(slot_count, HEADS, HDIM)
    attended, log_totals = attend_forward(
        queries, key_rows, value_rows, segment, row_block, attn_scale
    )
    attended_flat = attended.reshape(slot_count, width)
    attn_out = jnp.dot(attended_flat, out_weight, preferred_element_type=F32) + out_bias
    hidden_one = inputs + valid_f * gate_one * attn_out
    normed_two, scale_rows_two = norm_rows(hidden_one)
    moe_in = (normed_two * (1.0 + scale_two) + shift_two).astype(BF16)
    logits = jnp.dot(moe_in, router_weight, preferred_element_type=F32)
    expert_ids = jnp.arange(expert_count, dtype=jnp.int32)
    chosen = (routes[:, 0:1] == expert_ids) | (routes[:, 1:2] == expert_ids)
    gates = jax.nn.softmax(jnp.where(chosen, logits, -jnp.inf), axis=1)

    block_experts = (expert_ids % owners) * local_count + expert_ids // owners
    moe_rows = jnp.dot(hot, moe_in, preferred_element_type=F32).astype(BF16)
    gate_high, gate_low = high_low(gates[:, block_experts])

    def gate_slots(part):
        values = jnp.dot(hot, part, preferred_element_type=F32)
        values = values.reshape(expert_count, CAP, expert_count)
        return jnp.einsum("jpj->jp", values).astype(BF16)

    gate_tail = jnp.stack([gate_slots(gate_high), gate_slots(gate_low)], axis=1)
    gate_tail = jnp.pad(gate_tail, ((0, 0), (0, PAD - 2), (0, width - CAP)))
    send_rows = jnp.concatenate([moe_rows.reshape(expert_count, CAP, width), gate_tail], axis=1)
    owner_rows = exchange(send_rows, GROUP)

    no_pick = jnp.zeros((1,), jnp.int32)
    shared_total, grad_moe_in, grad_sup, grad_sup_bias, grad_sdown, grad_sdown_bias = ffn(
        False,
        no_pick,
        moe_in,
        grad_branch,
        shared_up,
        shared_up_bias,
        shared_down,
        shared_down_bias,
        chunk=768,
        row_block=1024,
    )
    shared_payload = jnp.concatenate(
        [grad_sup.reshape(-1, hidden), grad_sdown.reshape(-1, hidden)], axis=0
    )
    shared_sums = sum_everywhere(shared_payload).astype(F32)

    pick = jnp.full((1,), my_pick, jnp.int32)
    owner_res, owner_grads, grad_eup, grad_eup_bias, grad_edown, grad_edown_bias = ffn(
        True,
        pick,
        owner_rows,
        owner_branch,
        expert_up,
        expert_up_bias,
        expert_down,
        expert_down_bias,
        chunk=768,
        row_block=640,
    )
    returned = exchange(owner_res, GROUP).reshape(expert_count * CAP, width)
    returned_grads = exchange(owner_grads, GROUP)

    up_blocks = exchange(grad_eup.reshape(outer, width // outer, hidden), "p0")
    up_part = sum_blocks(up_blocks).astype(BF16).reshape(-1, width // dp_count, hidden)
    sum_eup = exchange(up_part, ("p1", "p2")).astype(F32)
    side = jnp.concatenate(
        [grad_eup_bias.reshape(dp_count, -1), grad_edown_bias.reshape(dp_count, -1)], axis=1
    )
    side_width = side.shape[1]
    side = jnp.pad(side.astype(BF16)[:, None, :], ((0, 0), (0, PAD - 1), (0, width - side_width)))
    down_payload = jnp.concatenate(
        [grad_edown.reshape(dp_count, hidden // dp_count, width), side], axis=1
    )
    down_rows = down_payload.shape[1]
    down_blocks = exchange(down_payload.reshape(outer, -1, down_rows, width), "p0")
    down_part = exchange(sum_blocks(down_blocks).astype(BF16), ("p1", "p2")).astype(F32)
    sum_edown = down_part[:, : hidden // dp_count]
    side_sums = down_part[:, hidden // dp_count]
    sum_eup_bias = side_sums[:, : hidden // dp_count]
    sum_edown_bias = side_sums[:, hidden // dp_count : side_width]

    routed = lax.dot_general(hot, returned, ROWS_FIRST, preferred_element_type=F32)
    branch = routed + shared_total
    hidden_two = hidden_one + valid_f * gate_two * branch
    slot_total = jnp.sum(valid_f) * width
    rms_stats = jnp.stack(
        [
            jnp.sqrt(jnp.sum(valid_f * hidden_two * hidden_two) / slot_total),
            jnp.sqrt(jnp.sum(valid_f * branch * branch) / slot_total),
        ]
    )[None, :]
    grad_gate_two = valid_f * grad_out * branch

    grad_rows = returned_grads[:, :CAP].reshape(expert_count * CAP, width)
    grad_moe_in = grad_moe_in + lax.dot_general(
        hot, grad_rows, ROWS_FIRST, preferred_element_type=F32
    )
    gate_grads = returned_grads[:, CAP : CAP + 2, :CAP].astype(F32)
    gate_grads = gate_grads[:, 0] + gate_grads[:, 1]
    hot_blocks = hot.reshape(expert_count, CAP, slot_count).astype(F32)
    grad_gates = jnp.einsum(
        "jpt,jp->tj", hot_blocks, gate_grads, precision=lax.Precision.HIGHEST
    )
    grad_gates = grad_gates.reshape(slot_count, local_count, owners)
    grad_gates = grad_gates.transpose(0, 2, 1).reshape(slot_count, expert_count)
    gate_inner = jnp.sum(gates * grad_gates, axis=1, keepdims=True)
    grad_logits = (gates * (grad_gates - gate_inner)).astype(BF16)
    grad_router = lax.dot_general(moe_in, grad_logits, ROWS_FIRST, preferred_element_type=F32)
    grad_moe_in = grad_moe_in + lax.dot_general(
        grad_logits, router_weight, ROWS_LAST, preferred_element_type=F32
    )
    grad_scale_two = grad_moe_in * normed_two
    grad_hidden_one = grad_out + norm_back(
        grad_moe_in * (1.0 + scale_two), normed_two, scale_rows_two
    )
    grad_attn = (valid_f * gate_one * grad_hidden_one).astype(BF16)
    grad_gate_one = valid_f * grad_hidden_one * attn_out
    grad_out_bias = jnp.sum(grad_attn.astype(F32), axis=0)
    grad_out_weight = lax.dot_general(
        attended_flat, grad_attn, ROWS_FIRST, preferred_element_type=F32
    )
    grad_attended = (
        lax.dot_general(grad_attn, out_weight, ROWS_LAST, preferred_element_type=F32)
        .astype(BF16)
        .reshape(slot_count, HEADS, HDIM)
    )
    grad_queries, grad_keys, grad_values = attend_backward(
        queries, key_rows, value_rows, segment, log_totals, grad_attended, row_block, attn_scale
    )
    grad_qkv = jnp.concatenate(
        [
            grad_queries.reshape(slot_count, width),
            grad_keys.reshape(slot_count, width),
            grad_values.reshape(slot_count, width),
        ],
        axis=1,
    ).astype(BF16)
    grad_qkv_weight = lax.dot_general(mixed_in, grad_qkv, ROWS_FIRST, preferred_element_type=F32)
    grad_mixed_in = lax.dot_general(grad_qkv, qkv_weight, ROWS_LAST, preferred_element_type=F32)
    grad_scale_one = grad_mixed_in * normed_one
    grad_tokens = grad_hidden_one + norm_back(
        grad_mixed_in * (1.0 + scale_one), normed_one, scale_rows_one
    )
    grad_tok_mod = jnp.concatenate(
        [grad_mixed_in, grad_scale_one, grad_gate_one, grad_moe_in, grad_scale_two, grad_gate_two],
        axis=1,
    )
    grad_modulation = lax.dot_general(
        member_f, grad_tok_mod, ROWS_FIRST, precision=lax.Precision.HIGHEST
    )
    grad_cond_act = lax.dot_general(
        grad_modulation, ada_weight.astype(F32), ROWS_LAST, precision=lax.Precision.HIGHEST
    )
    grad_condition = jax.vjp(jax.nn.silu, condition)[1](grad_cond_act)[0]

    image_count = grad_condition.shape[0]
    rows_out = jnp.concatenate([grad_modulation, grad_condition], axis=1).astype(BF16)
    rows_out = jnp.concatenate([rows_out, cond_act], axis=1)
    all_rows = spread(rows_out, ALL).reshape(-1, 8 * width)
    all_modulation = all_rows[:, : 6 * width]
    all_condition = all_rows[:, 6 * width : 7 * width]
    all_cond_act = all_rows[:, 7 * width :]
    sum_ada = lax.dot_general(
        all_cond_act, all_modulation, ROWS_FIRST, preferred_element_type=F32
    )
    sum_ada_bias = jnp.sum(all_modulation.astype(F32), axis=0)
    label_hot = (
        all_labels[:, None] == jnp.arange(label_table.shape[0], dtype=jnp.int32)[None, :]
    ).astype(BF16)
    sum_label = lax.dot_general(label_hot, all_condition, ROWS_FIRST, preferred_element_type=F32)
    time_hot = (
        jnp.repeat(all_times, image_count)[:, None]
        == jnp.arange(time_table.shape[0], dtype=jnp.int32)[None, :]
    ).astype(BF16)
    sum_time = lax.dot_general(time_hot, all_condition, ROWS_FIRST, preferred_element_type=F32)

    tail = jnp.concatenate(
        [
            jnp.concatenate([grad_qkv_weight, grad_out_weight], axis=1),
            grad_router.reshape(-1, hidden),
            grad_sup_bias.reshape(-1, hidden),
            jnp.pad(
                jnp.concatenate([grad_out_bias, grad_sdown_bias[0]])[None],
                ((0, 0), (0, hidden - 2 * width)),
            ),
        ],
        axis=0,
    )
    used = tail.shape[0]
    near_count = lax.axis_size(("p2", "expert"))
    tail = jnp.pad(tail, ((0, -used % (16 * near_count)), (0, 0)))
    tail = sum_everywhere(tail).astype(F32)
    router_rows = width * expert_count // hidden
    shared_count = shared_up.shape[0]
    sum_qkv = tail[:width, : 3 * width]
    sum_out_weight = tail[:width, 3 * width :]
    place = width + router_rows
    sum_router = tail[width:place].reshape(width, expert_count)
    sum_sup_bias = tail[place : place + shared_count]
    sum_out_bias = tail[place + shared_count, :width]
    sum_sdown_bias = jnp.broadcast_to(
        tail[place + shared_count, width : 2 * width][None], (shared_count, width)
    )
    half = grad_sup.size // hidden
    sum_sup = shared_sums[:half].reshape(grad_sup.shape)
    sum_sdown = shared_sums[half:].reshape(grad_sdown.shape)
    return (
        hidden_two.astype(BF16),
        grad_tokens,
        rms_stats,
        sum_time,
        sum_label,
        sum_ada,
        sum_ada_bias,
        sum_qkv,
        sum_out_weight,
        sum_out_bias,
        sum_router,
        sum_eup,
        sum_eup_bias,
        sum_edown,
        sum_edown_bias,
        sum_sup,
        sum_sup_bias,
        sum_sdown,
        sum_sdown_bias,
    )


def solution(mesh):
    dp_count = mesh.shape["dp"]
    owners = mesh.shape["expert"]
    split = Mesh(mesh.devices.reshape(dp_count // 4, 2, 2, owners), ALL)
    dp = ("p0", "p1", "p2")
    in_specs = (
        P(ALL, None),
        P(ALL, None),
        P(ALL, None),
        P(ALL),
        P(ALL, None),
        P(ALL, None, None),
        P(),
        P(),
        P(),
        P(),
        P(),
        P(),
        P(),
        P(),
        P("expert", None, None),
        P("expert", None),
        P("expert", None, None),
        P("expert", None),
        P(),
        P(),
        P(),
        P(),
    )
    out_specs = (
        P(ALL, None),
        P(ALL, None),
        P(ALL, None),
        P(),
        P(),
        P(),
        P(),
        P(),
        P(),
        P(),
        P(),
        P("expert", dp, None),
        P("expert", dp),
        P("expert", dp, None),
        P("expert", dp),
        P(),
        P(),
        P(),
        P(),
    )
    return jax.shard_map(body, mesh=split, in_specs=in_specs, out_specs=out_specs, check_vma=False)
```

time: 965 us -> 709 us (0.73)
  waiting for transfers between devices: 499 us -> 196 us
  matrix products: 238 us -> 120 us
  Pallas kernels: 0 us -> 63.3 us
  starting transfers between devices: 18.5 us -> 70.8 us
  blocking collectives: 45 us -> 68.2 us
  local copies, waits for them, and re-layouts: 66.4 us -> 87.8 us
  other arithmetic: 70.8 us -> 85.8 us
  between operations: 20.2 us -> 5.47 us
    psum x1 -> x0, waiting for transfers between devices: 441 us -> none  [body(): lax.psum((grad_qkv_weight, grad_out_weight, grad_out_bias, grad_ada, grad...]
    all_to_all x4 -> x16, waiting for transfers between devices: 57.7 us -> 196 us  [exchange(): return lax.all_to_all(blocks, axes, split_axis=0, concat_axis=0, tiled=True)]
    dot_general x38 -> x22, matrix products: 193 us -> 65.5 us  [the longest x1 9.22 us: body(): lax.dot_general(hot, returned, ROWS_FIRST, preferred_element_type=F32)]
    all_to_all x0 -> x2, blocking collectives: none -> 68.2 us  [exchange(): return lax.all_to_all(blocks, axes, split_axis=0, concat_axis=0, tiled=True)]
    pallas_call x0 -> x2, Pallas kernels: none -> 63.3 us  [ffn(): pl.pallas_call(functools.partial(ffn_kernel, routed, sources, row_block),...]
    all_to_all x4 -> x16, starting transfers between devices: 18 us -> 70.8 us  [exchange(): return lax.all_to_all(blocks, axes, split_axis=0, concat_axis=0, tiled=True)]
    psum x1 -> x0, blocking collectives: 45 us -> none  [body(): lax.psum((grad_qkv_weight, grad_out_weight, grad_out_bias, grad_ada, grad...]
    reshape x0 -> x11, local copies, waits for them, and re-layouts: none -> 20.2 us  [the longest x1 6.09 us: body(): sum_sdown = shared_sums[half:].reshape(grad_sdown.shape)]
  transfers between devices with their start and end apart: 9 -> 16, of which waited for: 5 -> 12; matrix products, arithmetic and copies ran while one was open for 17% -> 30% of each run, Pallas kernels for 0% -> 9%
where the time goes in v1:
time: 709 us; the launch traced here: 697 us
  waiting for transfers between devices  196 us (28%)
  matrix products  120 us (17%)
  local copies, waits for them, and re-layouts  87.8 us (12%)
  other arithmetic  85.8 us (12%)
  starting transfers between devices  70.8 us (10%)
  blocking collectives  68.2 us (10%)
  Pallas kernels  63.3 us (9%)
    all_to_all x16, waiting for transfers between devices, exchange(): return lax.all_to_all(blocks, axes, split_axis=0, concat_axis=0, tiled=True)  196 us
    all_to_all x16, starting transfers between devices, exchange(): return lax.all_to_all(blocks, axes, split_axis=0, concat_axis=0, tiled=True)  70.8 us
    all_to_all x2, blocking collectives, exchange(): return lax.all_to_all(blocks, axes, split_axis=0, concat_axis=0, tiled=True)  68.2 us
    pallas_call x2, Pallas kernels, ffn(): pl.pallas_call(functools.partial(ffn_kernel, routed, sources, row_block),...  63.3 us
    convert_element_type x2, other arithmetic, attend_backward(): grad_scores = (soft_probs * (grad_probs - row_inner)).astype(BF16)  15.5 us
    dot_general x2, matrix products, attend_backward(): jnp.einsum('qhd,khd->hqk', grad_rows_here, value_rows, preferred_element_...  15.4 us
  transfers between devices with their start and end apart: 16, of which 12 were waited for; matrix products, arithmetic and copies ran while one was open for 30% of the time, Pallas kernels for 9%

profile of v1, /device:TPU:0, one launch (start us, length us, event | category | flops | bytes accessed | tf_op | source)
XLA Modules:
  0.0 697.3 jit_solution(12835738148214861713)
XLA Ops:
  8.1 4.0 fusion.94
  30.1 3.0 fusion.1
  34.6 3.3 fusion.50
  45.5 4.0 fusion.49
  49.7 4.5 reduce-window.11
  57.5 4.1 fusion.117
  61.6 4.1 convolution_convert_fusion
  65.7 6.9 all-to-all-start.1
  74.2 3.2 fusion.37.x_ref
  77.4 26.5 %shared_net.1 = (f32[1024,384]{1,0:T(8,128)}, f32[1024,384]{1,0:T(8,128)}, bf16[2,384,1536]{2,1,0:T(8,128)(2,1)}, f32[2,1,1536]{2,1,0:T(1,128)}, bf16[2,1536,384]{2,1,0:T(8,128)(2,1)}, /*index=5*/f32[1,384]{1,0:T(1,128)}) custom-call(s32[1]{0:T(128)} %constant.131.clone.1.pick_ref, bf16[1024,384]{1,0:T(8,128)(2,1)} %fusion.37.x_ref, ...), custom_call_target="tpu_custom_call" | custom-call | flops 14495514624 | bytes 16777216 | tf_op jit(solution)/shard_map/shared_net/pallas_call | solution.py:176
  103.9 4.9 reshape.536
  108.8 4.9 pad_maximum_fusion
  113.7 4.9 all-to-all-start.14
  124.4 3.6 fusion.85
  129.8 2.9 fusion.82
  135.8 4.2 convolution_convert_fusion.1
  141.5 31.8 %all-to-all-done.14 = bf16[8,192,1536]{2,1,0:T(8,128)(2,1)} async-done(((bf16[8,192,1536]{2,1,0:T(8,128)(2,1)}), bf16[8,192,1536]{2,1,0:T(8,128)(2,1)}, u32[]{:S(2)}, u32[]{:S(2)}) %all-to-all-start.14) | async-done | bytes 4718624 | tf_op jit(solution)/shard_map/all_to_all | solution.py:227
  173.4 4.4 all-to-all-start
  179.1 4.0 reduce_sum.316
  187.3 20.6 %all-to-all-done.x_ref = bf16[16,176,384]{2,1,0:T(8,128)(2,1)} async-done(((bf16[16,176,384]{2,1,0:T(8,128)(2,1)}), bf16[16,176,384]{2,1,0:T(8,128)(2,1)}, u32[]{:S(2)}, u32[]{:S(2)}) %all-to-all-start) | async-done | bytes 2162720 | tf_op jit(solution)/shard_map/all_to_all | solution.py:227
  207.9 4.6 all-to-all-start.15
  212.5 36.8 %routed_net.1 = (bf16[16,160,384]{2,1,0:T(8,128)(2,1)}, bf16[16,176,384]{2,1,0:T(8,128)(2,1)}, bf16[1,384,1536]{2,1,0:T(8,128)(2,1)}, f32[1,1,1536]{2,1,0:T(1,12...) custom-call(s32[1]{0:T(128)} %bitcast.19.pick_ref, bf16[16,176,384]{2,1,0:T(8,128)(2,1)} %all-to-all-done.x_ref, ...), custom_call_target="tpu_custom_call" | custom-call | flops 18119393280 | bytes 16777216 | tf_op jit(solution)/shard_map/routed_net/pallas_call | solution.py:176
  249.3 4.5 all-to-all-start.10
  256.6 25.8 %all-to-all-done.10 = bf16[2,192,1536]{2,1,0:T(8,128)(2,1)} async-done(((bf16[2,192,1536]{2,1,0:T(8,128)(2,1)}), bf16[2,192,1536]{2,1,0:T(8,128)(2,1)}, u32[]{:S(2)}, u32[]{:S(2)}) %all-to-all-start.10) | async-done | bytes 1179680 | tf_op jit(solution)/shard_map/all_to_all | solution.py:227
  282.5 34.3 %all_to_all.90 = bf16[2,4,208,384]{3,2,1,0:T(8,128)(2,1)} all-to-all(bf16[2,4,208,384]{3,2,1,0:T(8,128)(2,1)} %pad_maximum_fusion.3), channel_id=1, replica_groups=mesh['p0'=2,'p1'=2,'p2'=2,'expert'=4] {'p0'}, dimensions={0} | all-to-all | bytes 2555904 | tf_op jit(solution)/shard_map/all_to_all | solution.py:227
  316.8 33.9 %all_to_all.91 = bf16[16,176,384]{2,1,0:T(8,128)(2,1)} all-to-all(bf16[16,176,384]{2,1,0:T(8,128)(2,1)S(1)} %copy-done.29), channel_id=1, replica_groups=mesh['p0'=2,'p1'=2,'p2'=2,'expert'=4] {'p1','p2','expert'}, dimensions={0} | all-to-all | bytes 4325376 | tf_op jit(solution)/shard_map/all_to_all | solution.py:227
  350.7 4.6 all-to-all-start.2
  364.9 3.6 fusion.3
  373.1 2.9 fusion.107
  377.7 5.4 all-to-all-done.2
  383.6 3.3 all-to-all-start.4
  387.1 9.2 %fusion.35 = (f32[]{:T(128)}, f32[1024]{0:T(1024)S(1)}, f32[1024]{0:T(1024)S(1)}, f32[]{:T(128)}, bf16[1024,384]{1,0:T(8,128)(2,1)}, /*index=5*/f32[1024,384]{1,0:T(8,128)}) fusion(f32[1024]{0:T(1024)S(1)} %copy-done.55, f32[1024,384]{1,0:T(8,128)S(1)} %get-tuple-element.188, f32[1024,2304]{1,0:T(8,128)} %copy-done.3, f32[1024]{0:T(1024)S(1)} %copy-done.66, ...), kind=kOutput, calls=%fused_computation.67 | convolution fusion | flops 2028206080 | bytes 12218376 | tf_op jit(solution)/shard_map/dot_general | solution.py:495
  396.3 4.2 fusion.116
  402.7 3.2 fusion.6
  405.9 7.7 %multiply_reduce_fusion = (f32[6,512]{1,0:T(8,128)S(1)}, f32[6,512,1024]{2,1,0:T(8,128)}) fusion(f32[6,512,1024]{2,1,0:T(8,128)S(1)} %bitcast.186, f32[6,512]{1,0:T(8,128)S(1)} %log_add_fusion, bf16[512,6,64]{0,2,1:T(8,128)(2,1)} %bitcast.207, bf16[1024,6,64]{0,2,1:T(8,128)(2,1)} %bitcast.194), kind=kOutput, calls=%fused_computation.3 | convolution fusion | flops 412087296 | bytes 26370048 | tf_op jit(solution)/shard_map/qhd,khd->hqk/dot_general | solution.py:323
  413.7 7.6 %multiply_reduce_fusion.1 = (f32[6,512]{1,0:T(8,128)S(1)}, f32[6,512,1024]{2,1,0:T(8,128)}) fusion(f32[6,512,1024]{2,1,0:T(8,128)S(1)} %bitcast.184, f32[6,512]{1,0:T(8,128)S(1)} %log_add_fusion.1, bf16[512,6,64]{0,2,1:T(8,128)(2,1)} %bitcast.204, bf16[1024,6,64]{0,2,1:T(8,128)(2,1)} %bitcast.195), kind=kOutput, calls=%fused_computation.6 | convolution fusion | flops 412087296 | bytes 26370048 | tf_op jit(solution)/shard_map/qhd,khd->hqk/dot_general | solution.py:323
  421.4 9.0 %multiply_convert_fusion.1 = bf16[6,512,1024]{2,1,0:T(8,128)(2,1)} fusion(f32[6,512,1024]{2,1,0:T(8,128)} %get-tuple-element.217, f32[6,512,1024]{2,1,0:T(8,128)S(1)} %bitcast.184, f32[6,512]{1,0:T(8,128)S(1)} %get-tuple-element.216, f32[6,512]{1,0:T(8,128)S(1)} %log_add_fusion.1), kind=kLoop, calls=%fused_computation.5 | loop fusion | flops 12582912 | bytes 31481856 | tf_op jit(solution)/shard_map/convert_element_type | solution.py:327
  430.4 5.4 fusion.130
  435.8 4.0 fusion.48
  443.9 3.1 add_convert_fusion
  447.1 6.5 multiply_convert_fusion
  458.0 5.0 all-to-all-start.16
  463.4 4.7 multiply_convert_fusion.2
  471.1 8.2 %all-to-all-done.16 = bf16[4,192,384]{2,1,0:T(8,128)(2,1)} async-done(((bf16[4,192,384]{2,1,0:T(8,128)(2,1)}), bf16[4,192,384]{2,1,0:T(8,128)(2,1)}, u32[]{:S(2)}, u32[]{:S(2)}) %all-to-all-start.16) | async-done | bytes 589856 | tf_op jit(solution)/shard_map/all_to_all | solution.py:227
  479.3 4.2 all-to-all-start.11
  486.4 4.6 fusion.106
  491.8 4.3 all-to-all-start.6
  496.2 4.3 fusion.30
  505.5 11.7 %all-to-all-done.6 = bf16[8,64,1536]{2,1,0:T(8,128)(2,1)} async-done(((bf16[8,64,1536]{2,1,0:T(8,128)(2,1)}), bf16[8,64,1536]{2,1,0:T(8,128)(2,1)}, u32[]{:S(2)}, u32[]{:S(2)}) %all-to-all-start.6) | async-done | bytes 1572896 | tf_op jit(solution)/shard_map/all_to_all | solution.py:227
  517.2 3.7 all-to-all-start.13
  520.9 3.0 fusion.34
  524.0 6.8 fusion.127
  534.8 3.4 all-to-all-start.7
  538.2 6.2 all-to-all-done.7
  545.7 4.6 all-to-all-start.5
  551.0 37.1 %all-to-all-done.5 = bf16[32,5,3072]{2,1,0:T(8,128)(2,1)S(1)} async-done(((bf16[32,5,3072]{2,1,0:T(8,128)(2,1)}), bf16[32,5,3072]{2,1,0:T(8,128)(2,1)S(1)}, u32[]{:S(2)}, u32[]{:S(2)}) %all-to-all-start.5) | async-done | bytes 983072 | tf_op jit(solution)/shard_map/all_to_all | solution.py:227
  589.6 3.4 all-to-all-start.8
  594.9 5.6 all-to-all-done.8
  600.5 3.7 broadcast_in_dim.232
  604.2 4.7 all-to-all-start.17
  623.3 40.3 %all-to-all-done.17 = bf16[8,192,1536]{2,1,0:T(8,128)(2,1)} async-done(((bf16[8,192,1536]{2,1,0:T(8,128)(2,1)}), bf16[8,192,1536]{2,1,0:T(8,128)(2,1)}, u32[]{:S(2)}, u32[]{:S(2)}) %all-to-all-start.17) | async-done | bytes 4718624 | tf_op jit(solution)/shard_map/all_to_all | solution.py:227
  664.9 4.3 all-to-all-start.9
  674.2 7.4 %fusion.118 = (f32[4,192,1536]{2,1,0:T(8,128)}, f32[4,192,1536]{2,1,0:T(8,128)}) fusion(bf16[8,192,1536]{2,1,0:T(8,128)(2,1)} %all-to-all-done.17), kind=kLoop, calls=%fused_computation.254 | loop fusion | bytes 18874368 | tf_op jit(solution)/shard_map/slice | solution.py:619
  681.6 6.1 reshape.540
  (396 shorter events, 134.9 us)
Async XLA Ops:
  0.7 6.4 copy-start
  2.1 10.0 %copy-start.100 = (pred[5]{0:T(512)(128)(4,1)}, pred[5]{0:T(512)(128)(4,1)S(1)}, u32[]{:S(2)}) copy-start(pred[5]{0:T(512)(128)(4,1)S(1)} %compare_and_fusion) | copy-start | bytes 19
  3.0 9.1 %copy-start.84 = (s32[5,1]{0,1:T(1,128)}, s32[5,1]{0,1:T(1,128)S(1)}, u32[]{:S(2)}) copy-start(s32[5,1]{0,1:T(1,128)S(1)} %reduce-window.10) | copy-start | bytes 64
  3.6 8.5 %copy-start.86 = (s32[5]{0:T(128)}, s32[5]{0:T(128)S(1)}, u32[]{:S(2)}) copy-start(s32[5]{0:T(128)S(1)} %fusion.102) | copy-start | bytes 64
  4.4 50.5 %copy-start.45 = (s32[1024]{0:T(1024)}, s32[1024]{0:T(1024)S(1)}, u32[]{:S(2)}) copy-start(s32[1024]{0:T(1024)S(1)} %get-tuple-element.182) | copy-start | bytes 12292
  6.2 5.9 copy-start.67
  18.4 37.5 %copy-start.13 = (s32[1,1024,2]{2,1,0:T(8,128)}, s32[1,1024,2]{2,1,0:T(8,128)S(1)}, u32[]{:S(2)}) copy-start(s32[1,1024,2]{2,1,0:T(8,128)S(1)} %copy.166) | copy-start | bytes 24580
  20.8 36.4 %copy-start.54 = (f32[1024]{0:T(1024)}, f32[1024]{0:T(1024)S(1)}, u32[]{:S(2)}) copy-start(f32[1024]{0:T(1024)S(1)} %get-tuple-element.202) | copy-start | bytes 12292
  23.2 6.9 copy-start.23
  24.7 13.2 %copy-start.11 = (bf16[1024,384]{0,1:T(8,128)(2,1)}, bf16[1024,384]{0,1:T(8,128)(2,1)S(1)}, u32[]{:S(2)}) copy-start(bf16[1024,384]{0,1:T(8,128)(2,1)S(1)} %copy.163) | copy-start | bytes 2359300
  49.5 6.5 copy-start.98
  65.7 6.9 copy-start.81
  65.7 7.5 %copy-start.99 = (f32[2,384]{1,0:T(2,128)S(1)}, f32[2,384]{1,0:T(2,128)}, u32[]{:S(2)}) copy-start(f32[2,384]{1,0:T(2,128)} %param.43) | copy-start | bytes 9220
  65.7 47.9 %all-to-all-start.1 = ((bf16[16,160,384]{2,1,0:T(8,128)(2,1)}), bf16[16,160,384]{2,1,0:T(8,128)(2,1)}, u32[]{:S(2)}, u32[]{:S(2)}) async-start(bf16[16,160,384]{2,1,0:T(8,128)(2,1)} %bitcast.214), calls=%async_computation.1 | async-start | bytes 3932160 | tf_op jit(solution)/shard_map/all_to_all | solution.py:227
  113.7 7.3 %copy-start.71 = (bf16[384,16]{0,1:T(8,128)(2,1)S(1)}, bf16[384,16]{0,1:T(8,128)(2,1)}, u32[]{:S(2)}) copy-start(bf16[384,16]{0,1:T(8,128)(2,1)} %param.35) | copy-start | bytes 36868
  113.7 59.7 %all-to-all-start.14 = ((bf16[8,192,1536]{2,1,0:T(8,128)(2,1)}), bf16[8,192,1536]{2,1,0:T(8,128)(2,1)}, u32[]{:S(2)}, u32[]{:S(2)}) async-start(bf16[8,192,1536]{2,1,0:T(8,128)(2,1)} %bitcast.191), calls=%async_computation.14 | async-start | bytes 9437184 | tf_op jit(solution)/shard_map/all_to_all | solution.py:227
  141.5 36.3 %copy-start.77 = (f32[4,1536]{1,0:T(4,128)S(1)}, f32[4,1536]{1,0:T(4,128)}, u32[]{:S(2)}) copy-start(f32[4,1536]{1,0:T(4,128)} %param.37) | copy-start | bytes 73732
  141.5 36.9 %copy-start.88 = (f32[4,384]{1,0:T(4,128)S(1)}, f32[4,384]{1,0:T(4,128)}, u32[]{:S(2)}) copy-start(f32[4,384]{1,0:T(4,128)} %param.39) | copy-start | bytes 18436
  173.4 34.6 %all-to-all-start = ((bf16[16,176,384]{2,1,0:T(8,128)(2,1)}), bf16[16,176,384]{2,1,0:T(8,128)(2,1)}, u32[]{:S(2)}, u32[]{:S(2)}) async-start(bf16[16,176,384]{2,1,0:T(8,128)(2,1)} %pad_maximum_fusion.2), calls=%async_computation | async-start | bytes 4325376 | tf_op jit(solution)/shard_map/all_to_all | solution.py:227
  207.9 41.4 %all-to-all-start.15 = ((bf16[4,192,384]{2,1,0:T(8,128)(2,1)}), bf16[4,192,384]{2,1,0:T(8,128)(2,1)}, u32[]{:S(2)}, u32[]{:S(2)}) async-start(bf16[4,192,384]{2,1,0:T(8,128)(2,1)} %copy.185), calls=%async_computation.15 | async-start | bytes 1179648 | tf_op jit(solution)/shard_map/all_to_all | solution.py:227
  249.3 33.1 %all-to-all-start.10 = ((bf16[2,192,1536]{2,1,0:T(8,128)(2,1)}), bf16[2,192,1536]{2,1,0:T(8,128)(2,1)}, u32[]{:S(2)}, u32[]{:S(2)}) async-start(bf16[2,192,1536]{2,1,0:T(8,128)(2,1)} %bitcast.219), calls=%async_computation.10 | async-start | bytes 2359296 | tf_op jit(solution)/shard_map/all_to_all | solution.py:227
  282.5 34.3 %copy-start.29 = (bf16[16,176,384]{2,1,0:T(8,128)(2,1)S(1)}, bf16[16,176,384]{2,1,0:T(8,128)(2,1)}, u32[]{:S(2)}) copy-start(bf16[16,176,384]{2,1,0:T(8,128)(2,1)} %get-tuple-element.34) | copy-start | bytes 6488068
  350.7 5.8 copy-start.103
  350.7 6.4 copy-start.60
  350.7 6.4 copy-start.49
  350.7 6.4 copy-start.62
  350.7 32.3 %all-to-all-start.2 = ((bf16[16,160,384]{2,1,0:T(8,128)(2,1)}), bf16[16,160,384]{2,1,0:T(8,128)(2,1)}, u32[]{:S(2)}, u32[]{:S(2)}) async-start(bf16[16,160,384]{2,1,0:T(8,128)(2,1)} %get-tuple-element.31), calls=%async_computation.2 | async-start | bytes 3932160 | tf_op jit(solution)/shard_map/all_to_all | solution.py:227
  376.1 7.0 copy-start.105
  376.1 10.9 %copy-start.53 = (f32[1024]{0:T(1024)S(1)}, f32[1024]{0:T(1024)}, u32[]{:S(2)}) copy-start(f32[1024]{0:T(1024)} %copy-done.52) | copy-start | bytes 12292
  376.1 10.9 %copy-start.55 = (f32[1024]{0:T(1024)S(1)}, f32[1024]{0:T(1024)}, u32[]{:S(2)}) copy-start(f32[1024]{0:T(1024)} %copy-done.54) | copy-start | bytes 12292
  376.1 10.9 %copy-start.66 = (f32[1024]{0:T(1024)S(1)}, f32[1024]{0:T(1024)}, u32[]{:S(2)}) copy-start(f32[1024]{0:T(1024)} %copy-done.65) | copy-start | bytes 12292
  383.6 73.5 %all-to-all-start.4 = ((s32[32,1,6]{2,1,0:T(1,128)}), s32[32,1,6]{2,1,0:T(1,128)S(1)}, u32[]{:S(2)}, u32[]{:S(2)}) async-start(s32[32,1,6]{2,1,0:T(1,128)} %broadcast_in_dim.223), calls=%async_computation.4 | async-start | bytes 32768 | tf_op jit(solution)/shard_map/all_to_all | solution.py:227
  387.0 9.3 %copy-start.6 = (f32[1024,384]{1,0:T(8,128)S(1)}, f32[1024,384]{1,0:T(8,128)}, u32[]{:S(2)}) copy-start(f32[1024,384]{1,0:T(8,128)} %add_add_fusion) | copy-start | bytes 4718596
  387.0 9.3 %copy-start.17 = (bf16[1024,384]{1,0:T(8,128)(2,1)S(1)}, bf16[1024,384]{1,0:T(8,128)(2,1)}, u32[]{:S(2)}) copy-start(bf16[1024,384]{1,0:T(8,128)(2,1)} %param.23) | copy-start | bytes 2359300
  387.0 15.6 %slice-start.3 = ((s8[12582912]{0:T(1024)(128)(4,1)}), s8[4194304]{0:T(1024)(128)(4,1)S(1)}, s32[]{:S(2)}) async-start(s8[12582912]{0:T(1024)(128)(4,1)} %bitcast.185), calls=%async_computation.21 | async-start | bytes 8388608
  387.0 15.6 %slice-start.4 = ((s8[12582912]{0:T(1024)(128)(4,1)}), s8[4194304]{0:T(1024)(128)(4,1)S(1)}, s32[]{:S(2)}) async-start(s8[12582912]{0:T(1024)(128)(4,1)} %bitcast.185), calls=%async_computation.22 | async-start | bytes 8388608
  396.3 6.4 slice-start.5
  402.7 11.0 %slice-start = ((s8[12582912]{0:T(1024)(128)(4,1)}), s8[4194304]{0:T(1024)(128)(4,1)S(1)}, s32[]{:S(2)}) async-start(s8[12582912]{0:T(1024)(128)(4,1)} %bitcast.183), calls=%async_computation.18 | async-start | bytes 8388608
  402.7 11.0 %slice-start.1 = ((s8[12582912]{0:T(1024)(128)(4,1)}), s8[4194304]{0:T(1024)(128)(4,1)S(1)}, s32[]{:S(2)}) async-start(s8[12582912]{0:T(1024)(128)(4,1)} %bitcast.183), calls=%async_computation.19 | async-start | bytes 8388608
  405.9 7.8 %slice-start.2 = ((s8[12582912]{0:T(1024)(128)(4,1)}), s8[4194304]{0:T(1024)(128)(4,1)S(1)}, s32[]{:S(2)}) async-start(s8[12582912]{0:T(1024)(128)(4,1)} %bitcast.183), calls=%async_computation.20 | async-start | bytes 8388608
  447.1 6.5 copy-start.12
  456.2 6.9 copy-start.96
  456.2 6.9 copy-start.97
  457.2 10.9 %copy-start.47 = (s32[32,1,6]{2,1,0:T(1,128)}, s32[32,1,6]{2,1,0:T(1,128)S(1)}, u32[]{:S(2)}) copy-start(s32[32,1,6]{2,1,0:T(1,128)S(1)} %all-to-all-done.4) | copy-start | bytes 2308
  458.0 21.3 %all-to-all-start.16 = ((bf16[4,192,384]{2,1,0:T(8,128)(2,1)}), bf16[4,192,384]{2,1,0:T(8,128)(2,1)}, u32[]{:S(2)}, u32[]{:S(2)}) async-start(bf16[4,192,384]{2,1,0:T(8,128)(2,1)} %broadcast_in_dim.230), calls=%async_computation.16 | async-start | bytes 1179648 | tf_op jit(solution)/shard_map/all_to_all | solution.py:227
  469.0 14.5 %copy-start.78 = (bf16[2,1,1536]{2,0,1:T(2,128)(2,1)S(1)}, bf16[2,1,1536]{2,0,1:T(2,128)(2,1)}, u32[]{:S(2)}) copy-start(bf16[2,1,1536]{2,0,1:T(2,128)(2,1)} %copy.208) | copy-start | bytes 18436
  479.3 12.5 %all-to-all-start.11 = ((bf16[4,48,1536]{2,1,0:T(8,128)(2,1)}), bf16[4,48,1536]{2,1,0:T(8,128)(2,1)}, u32[]{:S(2)}, u32[]{:S(2)}) async-start(bf16[4,48,1536]{2,1,0:T(8,128)(2,1)} %bitcast.211), calls=%async_computation.11 | async-start | bytes 1179648 | tf_op jit(solution)/shard_map/all_to_all | solution.py:227
  491.8 25.3 %all-to-all-start.6 = ((bf16[8,64,1536]{2,1,0:T(8,128)(2,1)}), bf16[8,64,1536]{2,1,0:T(8,128)(2,1)}, u32[]{:S(2)}, u32[]{:S(2)}) async-start(bf16[8,64,1536]{2,1,0:T(8,128)(2,1)} %bitcast.198), calls=%async_computation.6 | async-start | bytes 3145728 | tf_op jit(solution)/shard_map/all_to_all | solution.py:227
  503.9 17.1 %copy-start.56 = (f32[1024]{0:T(1024)S(1)}, f32[1024]{0:T(1024)}, u32[]{:S(2)}) copy-start(f32[1024]{0:T(1024)} %copy-done.54) | copy-start | bytes 12292
  505.5 18.5 %copy-start.85 = (s32[5,1]{0,1:T(1,128)S(1)}, s32[5,1]{0,1:T(1,128)}, u32[]{:S(2)}) copy-start(s32[5,1]{0,1:T(1,128)} %copy-done.84) | copy-start | bytes 64
  505.5 18.5 %copy-start.87 = (s32[5]{0:T(128)S(1)}, s32[5]{0:T(128)}, u32[]{:S(2)}) copy-start(s32[5]{0:T(128)} %copy-done.86) | copy-start | bytes 64
  517.2 17.6 %all-to-all-start.13 = ((bf16[4,208,384]{2,1,0:T(8,128)(2,1)}), bf16[4,208,384]{2,1,0:T(8,128)(2,1)S(1)}, u32[]{:S(2)}, u32[]{:S(2)}) async-start(bf16[4,208,384]{2,1,0:T(8,128)(2,1)} %reduce_sum.315), calls=%async_computation.13 | async-start | bytes 1277952 | tf_op jit(solution)/shard_map/all_to_all | solution.py:227
  524.0 6.9 copy-start.68
  524.0 6.9 copy-start.80
  524.0 6.9 copy-start.101
  530.8 7.3 %copy-start.70 = (bf16[5,384]{1,0:T(8,128)(2,1)S(1)}, bf16[5,384]{1,0:T(8,128)(2,1)}, u32[]{:S(2)}) copy-start(bf16[5,384]{1,0:T(8,128)(2,1)} %copy-done.69) | copy-start | bytes 11524
  534.8 10.9 %copy-start.21 = (bf16[4,208,384]{2,1,0:T(8,128)(2,1)}, bf16[4,208,384]{2,1,0:T(8,128)(2,1)S(1)}, u32[]{:S(2)}) copy-start(bf16[4,208,384]{2,1,0:T(8,128)(2,1)S(1)} %all-to-all-done.13) | copy-start | bytes 1916932
  534.8 9.6 %all-to-all-start.7 = ((bf16[4,64,384]{2,1,0:T(8,128)(2,1)}), bf16[4,64,384]{2,1,0:T(8,128)(2,1)S(1)}, u32[]{:S(2)}, u32[]{:S(2)}) async-start(bf16[4,64,384]{2,1,0:T(8,128)(2,1)} %copy.182), calls=%async_computation.7 | async-start | bytes 393216 | tf_op jit(solution)/shard_map/all_to_all | solution.py:227
  545.7 42.4 %all-to-all-start.5 = ((bf16[32,5,3072]{2,1,0:T(8,128)(2,1)}), bf16[32,5,3072]{2,1,0:T(8,128)(2,1)S(1)}, u32[]{:S(2)}, u32[]{:S(2)}) async-start(bf16[32,5,3072]{2,1,0:T(8,128)(2,1)} %broadcast_in_dim.225), calls=%async_computation.5 | async-start | bytes 3145728 | tf_op jit(solution)/shard_map/all_to_all | solution.py:227
  588.1 16.1 %copy-start.18 = (bf16[32,5,3072]{2,1,0:T(8,128)(2,1)}, bf16[32,5,3072]{2,1,0:T(8,128)(2,1)S(1)}, u32[]{:S(2)}) copy-start(bf16[32,5,3072]{2,1,0:T(8,128)(2,1)S(1)} %all-to-all-done.5) | copy-start | bytes 2949124
  589.6 10.9 %all-to-all-start.8 = ((bf16[4,64,384]{2,1,0:T(8,128)(2,1)}), bf16[4,64,384]{2,1,0:T(8,128)(2,1)S(1)}, u32[]{:S(2)}, u32[]{:S(2)}) async-start(bf16[4,64,384]{2,1,0:T(8,128)(2,1)} %broadcast_in_dim.227), calls=%async_computation.8 | async-start | bytes 393216 | tf_op jit(solution)/shard_map/all_to_all | solution.py:227
  604.2 59.5 %all-to-all-start.17 = ((bf16[8,192,1536]{2,1,0:T(8,128)(2,1)}), bf16[8,192,1536]{2,1,0:T(8,128)(2,1)}, u32[]{:S(2)}, u32[]{:S(2)}) async-start(bf16[8,192,1536]{2,1,0:T(8,128)(2,1)} %broadcast_in_dim.232), calls=%async_computation.17 | async-start | bytes 9437184 | tf_op jit(solution)/shard_map/all_to_all | solution.py:227
  608.9 8.0 %copy-start.22 = (bf16[4,208,384]{2,1,0:T(8,128)(2,1)S(1)}, bf16[4,208,384]{2,1,0:T(8,128)(2,1)}, u32[]{:S(2)}) copy-start(bf16[4,208,384]{2,1,0:T(8,128)(2,1)} %copy-done.21) | copy-start | bytes 1916932
  664.9 25.3 %all-to-all-start.9 = ((bf16[8,64,1536]{2,1,0:T(8,128)(2,1)}), bf16[8,64,1536]{2,1,0:T(8,128)(2,1)}, u32[]{:S(2)}, u32[]{:S(2)}) async-start(bf16[8,64,1536]{2,1,0:T(8,128)(2,1)} %broadcast_in_dim.229), calls=%async_computation.9 | async-start | bytes 3145728 | tf_op jit(solution)/shard_map/all_to_all | solution.py:227
  (68 other events, 233.4 us)

commit v2 on v1

v2 whole, which is shorter than its diff:
```python
import functools

import jax
import jax.numpy as jnp
from jax import lax
from jax.experimental import pallas as pl
from jax.experimental.pallas import tpu as pltpu
from jax.sharding import Mesh, PartitionSpec as P

HEADS = 6
HDIM = 64
CAP = 160
PAD = 16
WINDOW = 192
BLOCK = 128
SPAN = BLOCK + 2 * WINDOW
TILE = 256
NORM_EPS = 1e-06
MASK_FILL = -1e30
ROWS_FIRST = (((0,), (0,)), ((), ()))
ROWS_LAST = (((1,), (1,)), ((), ()))
GELU_C = 0.7978845608028654
GELU_K = 0.044715
ALL = ("p0", "p1", "p2", "expert")
GROUP = ("p1", "p2", "expert")
MESH = pl.DeviceIdType.MESH
F32 = jnp.float32
BF16 = jnp.bfloat16
VMEM_BYTES = 56 * 2**20


def norm_rows(matrix):
    row_mean = jnp.mean(matrix, axis=-1, keepdims=True)
    centred = matrix - row_mean
    row_var = jnp.mean(centred * centred, axis=-1, keepdims=True)
    row_scale = lax.rsqrt(row_var + NORM_EPS)
    return (centred * row_scale, row_scale)


def norm_back(grad_in, normed, row_scale):
    grad_mean = jnp.mean(grad_in, axis=-1, keepdims=True)
    cross_mean = jnp.mean(grad_in * normed, axis=-1, keepdims=True)
    return (grad_in - grad_mean - normed * cross_mean) * row_scale


def high_low(values):
    high = values.astype(BF16)
    return (high, (values - high.astype(F32)).astype(BF16))


def iota(shape, dim):
    return lax.broadcasted_iota(jnp.int32, shape, dim)


def dot(left, right):
    return jnp.dot(left, right, preferred_element_type=F32)


def dot_t(left, right):
    return lax.dot_general(left, right, ROWS_LAST, preferred_element_type=F32)


def in_vmem():
    return pl.BlockSpec(memory_space=pltpu.VMEM)


def in_smem():
    return pl.BlockSpec(memory_space=pltpu.SMEM)


def anywhere():
    return pl.BlockSpec(memory_space=pl.ANY)


def like(shape, dtype):
    return jax.ShapeDtypeStruct(shape, dtype)


def image_bounds(counts_ref):
    bounds = []
    start = 0
    for image in range(counts_ref.shape[1]):
        end = start + counts_ref[0, image]
        bounds.append((start, end))
        start = end
    return bounds


def member_block(bounds, first, rows):
    lane = iota((1, 128), 1)
    low = jnp.zeros((1, 128), jnp.int32)
    high = jnp.zeros((1, 128), jnp.int32)
    for image, (start, end) in enumerate(bounds):
        hit = (lane == image) | (lane == 8 + image)
        low = jnp.where(hit, start, low)
        high = jnp.where(hit, end, high)
    slot = first + iota((rows, 128), 0)
    return ((slot >= low) & (slot < high)).astype(F32).astype(BF16)


def stack_modulation(mod, stack):
    high, low = high_low(mod)
    stack[...] = jnp.zeros_like(stack)
    stack[0:16, :] = jnp.concatenate([high.astype(F32), low.astype(F32)], axis=0).astype(BF16)


def segments(bounds, slot):
    total = bounds[-1][1]
    image = jnp.zeros(slot.shape, jnp.int32)
    for _, end in bounds[:-1]:
        image = image + (slot >= end).astype(jnp.int32)
    image = jnp.where(slot >= total, len(bounds) + slot, image)
    return jnp.where(slot < 0, -1, image)


def front_kernel(
    owners,
    local_count,
    counts_ref,
    labels_ref,
    time_ref,
    routes_ref,
    time_table_ref,
    label_table_ref,
    ada_ref,
    ada_bias_ref,
    cot_ref,
    mod_ref,
    cond_ref,
    act_ref,
    pos_ref,
    tgt_ref,
    gb_ref,
    rows_ref,
    stack,
    hot,
    lines,
):
    slots, width = cot_ref.shape
    experts = owners * local_count
    bounds = image_bounds(counts_ref)
    total = bounds[-1][1]

    label_count = label_table_ref.shape[0]
    time_count = time_table_ref.shape[0]
    row = iota((8, label_count), 0)
    wanted = jnp.full((8, label_count), -1, jnp.int32)
    for image in range(len(bounds)):
        wanted = jnp.where(row == image, labels_ref[0, image], wanted)
    label_hot = (iota((8, label_count), 1) == wanted).astype(F32).astype(BF16)
    time_hot = (iota((8, time_count), 1) == time_ref[0]).astype(F32).astype(BF16)
    condition = dot(label_hot, label_table_ref[...]) + dot(time_hot, time_table_ref[...])
    act = (condition / (1.0 + jnp.exp(-condition))).astype(BF16)
    mod = dot(act, ada_ref[...]) + ada_bias_ref[...]
    cond_ref[...] = condition
    act_ref[...] = act
    mod_ref[...] = mod
    stack_modulation(mod[:, 5 * width :], stack)

    first = routes_ref[0:1, :]
    second = routes_ref[1:2, :]
    expert = iota((experts, slots), 0)
    valid = iota((experts, slots), 1) < total
    hit_first = (first == expert) & valid
    hit_second = (second == expert) & valid
    picks = (hit_first | hit_second).astype(F32)
    earlier = (iota((128, 128), 0) < iota((128, 128), 1)).astype(F32).astype(BF16)
    carry = jnp.zeros((experts, 1), F32)
    parts = []
    for lane in range(0, slots, 128):
        part = picks[:, lane : lane + 128]
        parts.append(dot(part.astype(BF16), earlier) + carry)
        carry = carry + jnp.sum(part, axis=1, keepdims=True)
    place = jnp.concatenate(parts, axis=1)
    pos_ref[...] = jnp.where(picks > 0.0, place, -1.0)
    base = (expert % local_count) * owners + expert // local_count
    slot_of = (base * CAP).astype(F32) + place
    lines[...] = jnp.full(lines.shape, -1.0, F32)
    lines[0:1, :] = jnp.sum(jnp.where(hit_first, slot_of + 1.0, 0.0), axis=0, keepdims=True) - 1.0
    lines[1:2, :] = jnp.sum(jnp.where(hit_second, slot_of + 1.0, 0.0), axis=0, keepdims=True) - 1.0
    tgt_ref[...] = lines[...].T

    def gradient(i, carry):
        r = pl.ds(pl.multiple_of(i * TILE, TILE), TILE)
        gate = dot(member_block(bounds, i * TILE, TILE), stack[...])
        gb_ref[r, :] = (gate * cot_ref[r, :].astype(F32)).astype(BF16)
        return carry

    lax.fori_loop(0, slots // TILE, gradient, 0)
    row = iota((CAP, slots), 0).astype(F32)
    for j in range(experts):
        expert = (j % owners) * local_count + j // owners
        line = pos_ref[expert : expert + 1, :]
        hot[...] = (row == line).astype(F32).astype(BF16)
        rows_ref[j] = dot(hot[...], gb_ref[...]).astype(BF16)


def front(owners, counts, labels, times, routes, time_table, label_table, ada, ada_bias, cot, experts):
    slots, width = cot.shape
    return pl.pallas_call(
        functools.partial(front_kernel, owners, experts // owners),
        in_specs=[in_smem()] * 3 + [in_vmem()] * 6,
        out_specs=[in_vmem()] * 7,
        out_shape=[
            like((8, 6 * width), F32),
            like((8, width), F32),
            like((8, width), BF16),
            like((experts, slots), F32),
            like((slots, 128), F32),
            like((slots, width), BF16),
            like((experts, CAP, width), BF16),
        ],
        scratch_shapes=[
            pltpu.VMEM((128, width), BF16),
            pltpu.VMEM((CAP, slots), BF16),
            pltpu.VMEM((128, slots), F32),
        ],
        compiler_params=pltpu.CompilerParams(vmem_limit_bytes=VMEM_BYTES),
        name="front",
    )(counts, labels, times, routes, time_table, label_table, ada, ada_bias[None], cot)


def attention_kernel(
    owners,
    local_count,
    counts_ref,
    tokens_ref,
    mod_ref,
    qkv_w_ref,
    out_w_ref,
    out_b_ref,
    router_ref,
    routes_ref,
    pos_ref,
    qkv_ref,
    att_ref,
    lse_ref,
    hidden_ref,
    moe_ref,
    gates_ref,
    send_ref,
    stack,
    values_t,
    hot,
    lines,
    columns,
):
    slots, width = tokens_ref.shape
    experts = owners * local_count
    padded = qkv_ref.shape[0]
    bounds = image_bounds(counts_ref)
    stack_modulation(mod_ref[...], stack)
    scale = HDIM ** (-0.5)

    def part(member, index):
        return dot(member, stack[:, index * width : (index + 1) * width])

    qkv_ref[0:WINDOW, :] = jnp.zeros((WINDOW, 3 * width), BF16)
    qkv_ref[padded - WINDOW :, :] = jnp.zeros((WINDOW, 3 * width), BF16)

    def project(i, carry):
        r = pl.ds(pl.multiple_of(i * TILE, TILE), TILE)
        member = member_block(bounds, i * TILE, TILE)
        normed, _ = norm_rows(tokens_ref[r, :].astype(F32))
        mixed = (normed * (1.0 + part(member, 1)) + part(member, 0)).astype(BF16)
        to = pl.ds(pl.multiple_of(i * TILE + WINDOW, 64), TILE)
        qkv_ref[to, :] = dot(mixed, qkv_w_ref[...]).astype(BF16)
        return carry

    lax.fori_loop(0, slots // TILE, project, 0)
    for r in range(0, padded, BLOCK):
        values_t[:, r : r + BLOCK] = qkv_ref[r : r + BLOCK, 2 * width :].T

    first_half = iota((BLOCK, 128), 1) < HDIM

    def attend(i, carry):
        q_rows = pl.ds(pl.multiple_of(i * BLOCK + WINDOW, 64), BLOCK)
        k_rows = pl.ds(pl.multiple_of(i * BLOCK, BLOCK), SPAN)
        o_rows = pl.ds(pl.multiple_of(i * BLOCK, BLOCK), BLOCK)
        key_segment = segments(bounds, i * BLOCK - WINDOW + iota((SPAN, BLOCK), 0))
        query_segment = segments(bounds, i * BLOCK + iota((1, BLOCK), 1))
        allowed = key_segment == query_segment
        allowed = jnp.concatenate([allowed, allowed], axis=1)
        for pair in range(HEADS // 2):
            lanes = slice(pair * 128, (pair + 1) * 128)
            q = qkv_ref[q_rows, lanes]
            k = qkv_ref[k_rows, width + pair * 128 : width + (pair + 1) * 128]
            zero = jnp.zeros_like(q)
            q = jnp.concatenate(
                [jnp.where(first_half, q, zero), jnp.where(first_half, zero, q)], axis=0
            )
            scores = jnp.where(allowed, dot_t(k, q) * scale, MASK_FILL)
            top = jnp.max(scores, axis=0, keepdims=True)
            expo = jnp.exp(scores - top)
            total = jnp.sum(expo, axis=0, keepdims=True)
            out = dot(values_t[lanes, k_rows], expo.astype(BF16)) / total
            out = jnp.concatenate([out[:HDIM, :BLOCK], out[HDIM:, BLOCK:]], axis=0)
            att_ref[o_rows, lanes] = out.T.astype(BF16)
            log_total = top + jnp.log(total)
            lse_ref[2 * pair : 2 * pair + 1, o_rows] = log_total[:, :BLOCK]
            lse_ref[2 * pair + 1 : 2 * pair + 2, o_rows] = log_total[:, BLOCK:]
        return carry

    lax.fori_loop(0, slots // BLOCK, attend, 0)

    def mix(i, carry):
        r = pl.ds(pl.multiple_of(i * TILE, TILE), TILE)
        member = member_block(bounds, i * TILE, TILE)
        attn_out = dot(att_ref[r, :], out_w_ref[...]) + out_b_ref[...]
        hidden = tokens_ref[r, :].astype(F32) + part(member, 2) * attn_out
        hidden_ref[r, :] = hidden
        normed, _ = norm_rows(hidden)
        moe_ref[r, :] = (normed * (1.0 + part(member, 4)) + part(member, 3)).astype(BF16)
        return carry

    lax.fori_loop(0, slots // TILE, mix, 0)

    logits = dot_t(router_ref[...], moe_ref[...])
    expert = iota((experts, slots), 0)
    chosen = (routes_ref[0:1, :] == expert) | (routes_ref[1:2, :] == expert)
    top = jnp.max(jnp.where(chosen, logits, MASK_FILL), axis=0, keepdims=True)
    expo = jnp.where(chosen, jnp.exp(logits - top), 0.0)
    gates_ref[...] = expo / jnp.sum(expo, axis=0, keepdims=True)

    row = iota((CAP, slots), 0).astype(F32)
    lane = iota((CAP, 128), 1)
    table = jnp.zeros((CAP, 128), F32)
    for j in range(experts):
        expert = (j % owners) * local_count + j // owners
        match = row == pos_ref[expert : expert + 1, :]
        hot[...] = match.astype(F32).astype(BF16)
        gate = jnp.sum(
            jnp.where(match, gates_ref[expert : expert + 1, :], 0.0), axis=1, keepdims=True
        )
        table = jnp.where(lane == j, gate, table)
        send_ref[j, :CAP, :] = dot(hot[...], moe_ref[...]).astype(BF16)
    columns[...] = jnp.zeros_like(columns)
    columns[:CAP, :] = table
    lines[...] = columns[...].T
    for j in range(experts):
        send_ref[j, CAP:, :] = tail_rows(lines[j : j + 1, :], width)


def tail_rows(line, width):
    high = line.astype(BF16).astype(F32)
    row = iota((PAD, line.shape[1]), 0)
    tail = jnp.where(row == 0, high, jnp.where(row == 1, line - high, 0.0))
    rest = jnp.zeros((PAD, width - line.shape[1]), F32)
    return jnp.concatenate([tail, rest], axis=1).astype(BF16)


def attention(owners, counts, tokens, mod, qkv_weight, out_weight, out_bias, router, routes, pos):
    slots, width = tokens.shape
    experts = pos.shape[0]
    padded = slots + 2 * WINDOW
    return pl.pallas_call(
        functools.partial(attention_kernel, owners, experts // owners),
        in_specs=[in_smem()] + [in_vmem()] * 8,
        out_specs=[in_vmem()] * 7,
        out_shape=[
            like((padded, 3 * width), BF16),
            like((slots, width), BF16),
            like((8, slots), F32),
            like((slots, width), F32),
            like((slots, width), BF16),
            like((experts, slots), F32),
            like((experts, CAP + PAD, width), BF16),
        ],
        scratch_shapes=[
            pltpu.VMEM((128, 6 * width), BF16),
            pltpu.VMEM((width, padded), BF16),
            pltpu.VMEM((CAP, slots), BF16),
            pltpu.VMEM((128, 256), F32),
            pltpu.VMEM((256, 128), F32),
        ],
        compiler_params=pltpu.CompilerParams(vmem_limit_bytes=VMEM_BYTES),
        name="attention",
    )(counts, tokens, mod, qkv_weight, out_weight, out_bias[None], router, routes, pos)


def group_partner(owners, a, b, c):
    first = lax.rem(lax.axis_index("p1") + a, 2)
    second = lax.rem(lax.axis_index("p2") + b, 2)
    third = lax.rem(lax.axis_index("expert") + c, owners)
    device = (lax.axis_index("p0"), first, second, third)
    return device, (first * 2 + second) * owners + third


def group_offsets(owners):
    return [(a, b, c) for a in range(2) for b in range(2) for c in range(owners)]


def greet(devices):
    barrier = pltpu.get_barrier_semaphore()
    for device in devices:
        pl.semaphore_signal(barrier, inc=1, device_id=device, device_id_type=MESH)
    pl.semaphore_wait(barrier, len(devices))


def group_copy(owners, index, offsets, source, target, send_sems, recv_sems):
    device, place = group_partner(owners, *offsets)
    _, me = group_partner(owners, 0, 0, 0)
    return pltpu.make_async_remote_copy(
        src_ref=source.at[place],
        dst_ref=target.at[me],
        send_sem=send_sems.at[index],
        recv_sem=recv_sems.at[index],
        device_id=device,
        device_id_type=MESH,
    )


def gelu_parts(pre, grad):
    square = pre * pre
    th = jnp.tanh(pre * (GELU_C + (GELU_C * GELU_K) * square))
    half = 0.5 + 0.5 * th
    slope = half + (0.5 * pre) * (1.0 - th * th) * (GELU_C + (3 * GELU_C * GELU_K) * square)
    return (pre * half).astype(BF16), (grad * slope).astype(BF16)


def shared_kernel(
    owners,
    x_ref,
    g_ref,
    up_ref,
    bu_ref,
    dn_ref,
    bd_ref,
    rows_ref,
    y_ref,
    dx_ref,
    dup_ref,
    dbu_ref,
    ddn_ref,
    dbd_ref,
    owner_ref,
    xt,
    gt,
    send_sems,
    recv_sems,
    own_sem,
):
    net = pl.program_id(0)
    chunk = pl.program_id(1)
    rows, width = x_ref.shape
    offsets = group_offsets(owners)
    copies = [
        group_copy(owners, index, offset, rows_ref, owner_ref, send_sems, recv_sems)
        for index, offset in enumerate(offsets)
        if index
    ]
    _, me = group_partner(owners, 0, 0, 0)
    own = pltpu.make_async_copy(rows_ref.at[me], owner_ref.at[me], own_sem)

    @pl.when((net == 0) & (chunk == 0))
    def _():
        greet([group_partner(owners, *offset)[0] for offset in offsets[1:]])
        own.start()
        for copy in copies:
            copy.start()
        for r in range(0, rows, 256):
            xt[:width, r : r + 256] = x_ref[r : r + 256, :].T
            gt[:, r : r + 256] = g_ref[r : r + 256, :].T
        xt[width:, :] = jnp.ones((xt.shape[0] - width, rows), BF16)
        y_ref[...] = jnp.zeros_like(y_ref)
        dx_ref[...] = jnp.zeros_like(dx_ref)
        dbd_ref[...] = jnp.sum(g_ref[...].astype(F32), axis=0, keepdims=True)

    up = up_ref[0]
    dn = dn_ref[0]
    pre = dot(x_ref[...], up) + bu_ref[0]
    act, dpre = gelu_parts(pre, dot_t(g_ref[...], dn))
    y_ref[...] += dot(act, dn)
    dx_ref[...] += dot_t(dpre, up)
    dup = dot(xt[...], dpre)
    dup_ref[0] = dup[:width].astype(BF16)
    dbu_ref[0] = dup[width : width + 1]
    ddn_ref[0] = dot(gt[...], act).T.astype(BF16)

    @pl.when((net == pl.num_programs(0) - 1) & (chunk == pl.num_programs(1) - 1))
    def _():
        y_ref[...] += jnp.sum(bd_ref[...], axis=0)
        own.wait()
        for copy in copies:
            copy.wait()


def shared_nets(owners, x, g, up, bias_up, down, bias_down, rows_out, chunk=768):
    nets, width, hidden = up.shape
    rows = x.shape[0]
    count = rows_out.shape[0]

    def whole(shape):
        return pl.BlockSpec(shape, lambda n, h: (0,) * len(shape))

    return pl.pallas_call(
        functools.partial(shared_kernel, owners),
        grid=(nets, hidden // chunk),
        in_specs=[
            whole(x.shape),
            whole(g.shape),
            pl.BlockSpec((1, width, chunk), lambda n, h: (n, 0, h)),
            pl.BlockSpec((1, 1, chunk), lambda n, h: (n, 0, h)),
            pl.BlockSpec((1, chunk, width), lambda n, h: (n, h, 0)),
            whole((nets, 1, width)),
            anywhere(),
        ],
        out_specs=[
            whole((rows, width)),
            whole((rows, width)),
            pl.BlockSpec((1, width, chunk), lambda n, h: (n, 0, h)),
            pl.BlockSpec((1, 1, chunk), lambda n, h: (n, 0, h)),
            pl.BlockSpec((1, chunk, width), lambda n, h: (n, h, 0)),
            whole((1, width)),
            anywhere(),
        ],
        out_shape=[
            like((rows, width), F32),
            like((rows, width), F32),
            like((nets, width, hidden), BF16),
            like((nets, 1, hidden), F32),
            like((nets, hidden, width), BF16),
            like((1, width), F32),
            like(rows_out.shape, BF16),
        ],
        scratch_shapes=[
            pltpu.VMEM((width + 16, rows), BF16),
            pltpu.VMEM((width, rows), BF16),
            pltpu.SemaphoreType.DMA((count,)),
            pltpu.SemaphoreType.DMA((count,)),
            pltpu.SemaphoreType.DMA,
        ],
        compiler_params=pltpu.CompilerParams(
            vmem_limit_bytes=VMEM_BYTES, collective_id=1, has_side_effects=True
        ),
        name="shared_nets",
    )(x, g, up, bias_up[:, None, :], down, bias_down[:, None, :], rows_out)


def routed_kernel(
    owners,
    x_ref,
    g_ref,
    up_any,
    bu_ref,
    dn_any,
    bd_ref,
    y_ref,
    dup_ref,
    dbu_ref,
    ddn_ref,
    dbd_ref,
    back_ref,
    up,
    dn,
    xt,
    gt,
    acts,
    dpres,
    outgoing,
    lines,
    columns,
    load_sems,
    send_sems,
    recv_sems,
    own_sem,
):
    width, hidden = up.shape
    chunk = 768
    pick = lax.axis_index("p1") * 2 + lax.axis_index("p2")
    loads = [
        pltpu.make_async_copy(up_any.at[pick], up, load_sems.at[0]),
        pltpu.make_async_copy(dn_any.at[pick], dn, load_sems.at[1]),
    ]
    for load in loads:
        load.start()
    offsets = group_offsets(owners)
    places = [group_partner(owners, *offset)[1] for offset in offsets]
    greet([group_partner(owners, *offset)[0] for offset in offsets[1:]])
    copies = [
        group_copy(owners, index, offset, outgoing, back_ref, send_sems, recv_sems)
        if index
        else pltpu.make_async_copy(outgoing.at[places[0]], back_ref.at[places[0]], own_sem)
        for index, offset in enumerate(offsets)
    ]

    lines[...] = jnp.zeros_like(lines)
    for index, place in enumerate(places):
        tail = x_ref[place, CAP:, :256].astype(F32)
        lines[index : index + 1, :] = tail[0:1] + tail[1:2]
    columns[...] = lines[...].T
    gates = columns[:CAP, :]
    for load in loads:
        load.wait()
    bu = bu_ref[pick]
    bd = bd_ref[pick]
    lane = iota((CAP, 128), 1)
    group = owners
    size = group * CAP
    xt[width:, :] = jnp.ones((xt.shape[0] - width, xt.shape[1]), BF16)
    dbd = jnp.zeros((1, width), F32)
    for first in range(0, len(offsets), group):
        members = range(first, first + group)
        span = slice(first * CAP, first * CAP + size)
        x = jnp.concatenate([x_ref[places[k], :CAP, :] for k in members], axis=0)
        raw = [g_ref[places[k]].astype(F32) for k in members]
        g = jnp.concatenate([raw[k - first] * gates[:, k : k + 1] for k in members], axis=0)
        g = g.astype(BF16)
        dbd = dbd + jnp.sum(g.astype(F32), axis=0, keepdims=True)
        xt[:width, span] = x.T
        gt[:, span] = g.T
        y = jnp.zeros((size, width), F32)
        dx = jnp.zeros((size, width), F32)
        for h in range(0, hidden, chunk):
            pre = dot(x, up[:, h : h + chunk]) + bu[:, h : h + chunk]
            act, dpre = gelu_parts(pre, dot_t(g, dn[h : h + chunk, :]))
            acts[span, h : h + chunk] = act
            dpres[span, h : h + chunk] = dpre
            y = y + dot(act, dn[h : h + chunk, :])
            dx = dx + dot_t(dpre, up[:, h : h + chunk])
        table = jnp.zeros((CAP, 128), F32)
        for k in members:
            r = slice((k - first) * CAP, (k - first + 1) * CAP)
            res = (y[r] + bd).astype(BF16).astype(F32)
            y_ref[places[k]] = (res * gates[:, k : k + 1]).astype(BF16)
            inner = jnp.sum(res * raw[k - first], axis=1, keepdims=True)
            table = jnp.where(lane == k - first, inner, table)
            outgoing[places[k], :CAP, :] = dx[r].astype(BF16)
        columns[:CAP, :] = table
        lines[...] = columns[...].T
        for k in members:
            outgoing[places[k], CAP:, :] = tail_rows(lines[k - first : k - first + 1, :], width)
            copies[k].start()
    dbd_ref[...] = dbd
    for h in range(0, hidden, 512):
        dup = dot(xt[...], dpres[:, h : h + 512])
        dup_ref[:, h : h + 512] = dup[:width].astype(BF16)
        dbu_ref[:, h : h + 512] = dup[width : width + 1]
        ddn_ref[h : h + 512, :] = dot(gt[...], acts[:, h : h + 512]).T.astype(BF16)
    for copy in copies:
        copy.wait()


def routed_net(owners, x, g, up, bias_up, down, bias_down):
    count = x.shape[0]
    rows = count * CAP
    width, hidden = up.shape[1:]
    return pl.pallas_call(
        functools.partial(routed_kernel, owners),
        in_specs=[in_vmem(), in_vmem(), anywhere(), in_vmem(), anywhere(), in_vmem()],
        out_specs=[in_vmem()] * 5 + [anywhere()],
        out_shape=[
            like((count, CAP, width), BF16),
            like((width, hidden), BF16),
            like((1, hidden), F32),
            like((hidden, width), BF16),
            like((1, width), F32),
            like((count, CAP + PAD, width), BF16),
        ],
        scratch_shapes=[
            pltpu.VMEM((width, hidden), BF16),
            pltpu.VMEM((hidden, width), BF16),
            pltpu.VMEM((width + 16, rows), BF16),
            pltpu.VMEM((width, rows), BF16),
            pltpu.VMEM((rows, hidden), BF16),
            pltpu.VMEM((rows, hidden), BF16),
            pltpu.VMEM((count, CAP + PAD, width), BF16),
            pltpu.VMEM((128, 256), F32),
            pltpu.VMEM((256, 128), F32),
            pltpu.SemaphoreType.DMA((2,)),
            pltpu.SemaphoreType.DMA((count,)),
            pltpu.SemaphoreType.DMA((count,)),
            pltpu.SemaphoreType.DMA,
        ],
        compiler_params=pltpu.CompilerParams(
            vmem_limit_bytes=VMEM_BYTES, collective_id=2, has_side_effects=True
        ),
        name="routed_net",
    )(x, g, up, bias_up[:, None, :], down, bias_down[:, None, :])


def member_rows(bounds, first, rows):
    image = iota((16, rows), 0)
    slot = first + iota((16, rows), 1)
    low = jnp.zeros((16, rows), jnp.int32)
    high = jnp.zeros((16, rows), jnp.int32)
    for index, (start, end) in enumerate(bounds):
        low = jnp.where(image == index, start, low)
        high = jnp.where(image == index, end, high)
    return ((slot >= low) & (slot < high)).astype(F32).astype(BF16)


def backward_kernel(
    owners,
    local_count,
    counts_ref,
    labels_ref,
    time_ref,
    tokens_ref,
    cot_ref,
    mod_ref,
    cond_ref,
    act_ref,
    qkv_ref,
    att_ref,
    lse_ref,
    hidden_ref,
    moe_ref,
    gates_ref,
    tgt_ref,
    shared_ref,
    dmoe_ref,
    grads_ref,
    res_ref,
    qkv_w_ref,
    out_w_ref,
    out_b_ref,
    router_ref,
    ada_ref,
    layer_ref,
    dtok_ref,
    rms_ref,
    dqkv_w_ref,
    dout_w_ref,
    dout_b_ref,
    drouter_ref,
    note_ref,
    stack,
    hot,
    rows_ext,
    gate_cols,
    ghid,
    gatt,
    kt,
    dkeys,
    dvals,
    dqkv,
    turned,
    dlog,
    sums,
    lines,
    columns,
    router,
):
    slots, width = tokens_ref.shape
    experts = owners * local_count
    padded = qkv_ref.shape[0]
    blocks = slots // TILE
    bounds = image_bounds(counts_ref)
    total = bounds[-1][1]
    scale = HDIM ** (-0.5)
    stack_modulation(mod_ref[...], stack)
    sums[...] = jnp.zeros_like(sums)

    def part(member, index):
        return dot(member, stack[:, index * width : (index + 1) * width])

    def collect(turned_member, index, values):
        sums[:, index * width : (index + 1) * width] += dot(turned_member, values.astype(BF16))

    lines[...] = jnp.zeros_like(lines)
    for j in range(experts):
        tail = grads_ref[j, CAP:, :256].astype(F32)
        lines[j : j + 1, :] = tail[0:1] + tail[1:2]
    columns[...] = lines[...].T
    lane = iota((CAP, 128), 1)
    for j in range(experts):
        expert = (j % owners) * local_count + j // owners
        r = slice(j * CAP, (j + 1) * CAP)
        rows_ext[r, :width] = grads_ref[j, :CAP, :]
        inner = columns[:CAP, j : j + 1]
        high = inner.astype(BF16).astype(F32)
        spread_out = jnp.where(
            lane == expert, high, jnp.where(lane == experts + expert, inner - high, 0.0)
        )
        rows_ext[r, width:] = spread_out.astype(BF16)
    gate_cols[...] = jnp.zeros_like(gate_cols)
    gate_cols[:experts, :] = gates_ref[...]
    router[...] = jnp.zeros_like(router)
    router[:experts, :] = router_ref[...]

    def routing(i, carry):
        r = pl.ds(pl.multiple_of(i * TILE, TILE), TILE)
        first = tgt_ref[r, 0:1]
        second = tgt_ref[r, 1:2]
        slot = iota((TILE, hot.shape[1]), 1).astype(F32)
        hot[r, :] = ((slot == first) | (slot == second)).astype(F32).astype(BF16)
        back = dot(hot[r, :], rows_ext[...])
        inner = back[:, width : width + experts] + back[:, width + experts : width + 2 * experts]
        gates = gate_cols[:, r].T[:, :experts]
        grad = gates * (inner - jnp.sum(gates * inner, axis=1, keepdims=True))
        grad = jnp.concatenate([grad, jnp.zeros((TILE, 128 - experts), F32)], axis=1)
        grad = grad.astype(BF16)
        dlog[:, r] = grad.T
        gmoe = dmoe_ref[r, :] + back[:, :width] + dot(grad, router[...])
        member = member_block(bounds, i * TILE, TILE)
        turned_member = member_rows(bounds, i * TILE, TILE)
        normed, row_scale = norm_rows(hidden_ref[r, :])
        collect(turned_member, 3, gmoe)
        collect(turned_member, 4, gmoe * normed)
        grad_hidden = cot_ref[r, :].astype(F32) + norm_back(
            gmoe * (1.0 + part(member, 4)), normed, row_scale
        )
        ghid[r, :] = grad_hidden
        grad_attn = (part(member, 2) * grad_hidden).astype(BF16)
        attn_out = dot(att_ref[r, :], out_w_ref[...]) + out_b_ref[...]
        collect(turned_member, 2, grad_hidden * attn_out)
        to = pl.ds(pl.multiple_of(i * TILE, TILE), TILE)
        gatt[to, :] = dot_t(grad_attn, out_w_ref[...]).astype(BF16)
        dqkv[r, :width] = grad_attn
        turned[:, r] = att_ref[r, :].T
        return carry

    lax.fori_loop(0, blocks, routing, 0)
    drouter_ref[...] = dot(dlog[...], moe_ref[...])[:experts]
    dout_w_ref[...] = dot(turned[...], dqkv[:, :width])
    dout_b_ref[...] = jnp.sum(dqkv[:, :width].astype(F32), axis=0, keepdims=True)

    for r in range(0, padded, BLOCK):
        kt[:, r : r + BLOCK] = qkv_ref[r : r + BLOCK, width : 2 * width].T
    dkeys[...] = jnp.zeros_like(dkeys)
    dvals[...] = jnp.zeros_like(dvals)
    first_half = iota((BLOCK, 128), 1) < HDIM

    def split(pair_rows):
        zero = jnp.zeros_like(pair_rows)
        return jnp.concatenate(
            [jnp.where(first_half, pair_rows, zero), jnp.where(first_half, zero, pair_rows)],
            axis=0,
        )

    def attend(i, carry):
        q_rows = pl.ds(pl.multiple_of(i * BLOCK + WINDOW, 64), BLOCK)
        k_rows = pl.ds(pl.multiple_of(i * BLOCK, BLOCK), SPAN)
        o_rows = pl.ds(pl.multiple_of(i * BLOCK, BLOCK), BLOCK)
        key_segment = segments(bounds, i * BLOCK - WINDOW + iota((SPAN, BLOCK), 0))
        query_segment = segments(bounds, i * BLOCK + iota((1, BLOCK), 1))
        allowed = key_segment == query_segment
        allowed = jnp.concatenate([allowed, allowed], axis=1)
        for pair in range(HEADS // 2):
            lanes = slice(pair * 128, (pair + 1) * 128)
            q = split(qkv_ref[q_rows, lanes])
            out_grad = split(gatt[o_rows, lanes])
            k = qkv_ref[k_rows, width + pair * 128 : width + (pair + 1) * 128]
            v = qkv_ref[k_rows, 2 * width + pair * 128 : 2 * width + (pair + 1) * 128]
            log_total = jnp.concatenate(
                [lse_ref[2 * pair : 2 * pair + 1, o_rows], lse_ref[2 * pair + 1 : 2 * pair + 2, o_rows]],
                axis=1,
            )
            probs = jnp.exp(jnp.where(allowed, dot_t(k, q) * scale, MASK_FILL) - log_total)
            grad_probs = dot_t(v, out_grad)
            inner = jnp.sum(probs * grad_probs, axis=0, keepdims=True)
            grad_scores = (probs * (grad_probs - inner)).astype(BF16)
            dvals[k_rows, lanes] += dot(probs.astype(BF16), out_grad)
            dkeys[k_rows, lanes] += dot(grad_scores, q) * scale
            turned_query = dot(kt[lanes, k_rows], grad_scores) * scale
            turned_query = jnp.concatenate(
                [turned_query[:HDIM, :BLOCK], turned_query[HDIM:, BLOCK:]], axis=0
            )
            dqkv[o_rows, lanes] = turned_query.T.astype(BF16)
        return carry

    lax.fori_loop(0, slots // BLOCK, attend, 0)

    def finish(i, carry):
        r = pl.ds(pl.multiple_of(i * TILE, TILE), TILE)
        from_rows = pl.ds(pl.multiple_of(i * TILE + WINDOW, 64), TILE)
        dqkv[r, width : 2 * width] = dkeys[from_rows, :].astype(BF16)
        dqkv[r, 2 * width :] = dvals[from_rows, :].astype(BF16)
        member = member_block(bounds, i * TILE, TILE)
        turned_member = member_rows(bounds, i * TILE, TILE)
        gmix = dot_t(dqkv[r, :], qkv_w_ref[...])
        normed, row_scale = norm_rows(tokens_ref[r, :].astype(F32))
        gain = 1.0 + part(member, 1)
        turned[:, r] = (normed * gain + part(member, 0)).astype(BF16).T
        collect(turned_member, 0, gmix)
        collect(turned_member, 1, gmix * normed)
        dtok_ref[r, :] = ghid[r, :] + norm_back(gmix * gain, normed, row_scale)
        return carry

    lax.fori_loop(0, blocks, finish, 0)
    dqkv_w_ref[...] = dot(turned[...], dqkv[...])

    def result(i, carry):
        r = pl.ds(pl.multiple_of(i * TILE, TILE), TILE)
        member = member_block(bounds, i * TILE, TILE)
        branch = dot(hot[r, :], res_ref[...]) + shared_ref[r, :]
        layer = hidden_ref[r, :] + part(member, 5) * branch
        layer_ref[r, :] = layer.astype(BF16)
        valid = (i * TILE + iota((TILE, width), 0)) < total
        collect(member_rows(bounds, i * TILE, TILE), 5, cot_ref[r, :].astype(F32) * branch)
        one = jnp.sum(jnp.where(valid, layer * layer, 0.0), axis=0, keepdims=True)
        two = jnp.sum(jnp.where(valid, branch * branch, 0.0), axis=0, keepdims=True)
        return (carry[0] + one, carry[1] + two)

    zero = jnp.zeros((1, width), F32)
    one, two = lax.fori_loop(0, blocks, result, (zero, zero))
    count = jnp.full((1, 1), total * width, jnp.int32).astype(F32)
    one = jnp.sqrt(jnp.sum(one, axis=1, keepdims=True) / count)
    two = jnp.sqrt(jnp.sum(two, axis=1, keepdims=True) / count)
    rms_ref[...] = jnp.where(iota((1, 128), 1) == 0, one, two)

    grad_mod = sums[0:8, :]
    high, low = high_low(grad_mod)
    grad_act = dot_t(high, ada_ref[...]) + dot_t(low, ada_ref[...])
    condition = cond_ref[...]
    sigmoid = 1.0 / (1.0 + jnp.exp(-condition))
    grad_cond = grad_act * (sigmoid * (1.0 + condition * (1.0 - sigmoid)))
    row = iota((8, 128), 0)
    lane = iota((8, 128), 1)
    label = jnp.zeros((8, 128), jnp.int32)
    for image in range(len(bounds)):
        label = jnp.where(row == image, labels_ref[0, image], label)
    time = jnp.full((8, 128), time_ref[0], jnp.int32)
    pieces = [label // 32, label % 32, time // 32, time % 32]
    marks = jnp.zeros((8, 128), jnp.int32)
    for index, piece in enumerate(pieces):
        marks = jnp.where(lane == index, piece, marks)
    real = row < len(bounds)
    marks = jnp.where(real, marks, jnp.where(lane < 4, 255, 0)).astype(F32)
    keep = (iota((8, width), 0) < len(bounds)).astype(F32)
    note = jnp.concatenate(
        [grad_mod, grad_cond * keep, act_ref[...].astype(F32) * keep, marks], axis=1
    )
    note_ref[...] = jnp.concatenate([note, jnp.zeros_like(note)], axis=0).astype(BF16)


def backward(owners, *args):
    tokens, mod, qkv_pad, gates = args[3], args[5], args[8], args[13]
    slots, width = tokens.shape
    padded = qkv_pad.shape[0]
    experts = gates.shape[0]
    return pl.pallas_call(
        functools.partial(backward_kernel, owners, experts // owners),
        in_specs=[in_smem()] * 3 + [in_vmem()] * (len(args) - 3),
        out_specs=[in_vmem()] * 8,
        out_shape=[
            like((slots, width), BF16),
            like((slots, width), F32),
            like((1, 128), F32),
            like((width, 3 * width), F32),
            like((width, width), F32),
            like((1, width), F32),
            like((experts, width), F32),
            like((16, 8 * width + 128), BF16),
        ],
        scratch_shapes=[
            pltpu.VMEM((128, 6 * width), BF16),
            pltpu.VMEM((slots, experts * CAP), BF16),
            pltpu.VMEM((experts * CAP, width + 128), BF16),
            pltpu.VMEM((128, slots), F32),
            pltpu.VMEM((slots, width), F32),
            pltpu.VMEM((slots, width), BF16),
            pltpu.VMEM((width, padded), BF16),
            pltpu.VMEM((padded, width), F32),
            pltpu.VMEM((padded, width), F32),
            pltpu.VMEM((slots, 3 * width), BF16),
            pltpu.VMEM((width, slots), BF16),
            pltpu.VMEM((128, slots), BF16),
            pltpu.VMEM((16, 6 * width), F32),
            pltpu.VMEM((128, 256), F32),
            pltpu.VMEM((256, 128), F32),
            pltpu.VMEM((128, width), BF16),
        ],
        compiler_params=pltpu.CompilerParams(vmem_limit_bytes=VMEM_BYTES),
        name="backward",
    )(*args)


def exchange(blocks, axes):
    return lax.all_to_all(blocks, axes, split_axis=0, concat_axis=0, tiled=True)


def spread(block, axes):
    count = lax.axis_size(axes)
    return exchange(jnp.broadcast_to(block[None], (count,) + block.shape), axes)


def sum_blocks(blocks):
    return jnp.sum(blocks.astype(F32), axis=0)


def sum_everywhere(payload):
    rows, width = payload.shape
    near = ("p2", "expert")
    far = ("p0", "p1")
    near_count = lax.axis_size(near)
    far_count = lax.axis_size(far)
    piece = rows // near_count
    part = exchange(payload.astype(BF16).reshape(near_count, piece, width), near)
    part = sum_blocks(part).astype(BF16)
    part = part.reshape(piece, far_count, width // far_count).transpose(1, 0, 2)
    part = sum_blocks(exchange(part, far)).astype(BF16)
    part = spread(part, far).transpose(1, 0, 2).reshape(piece, width)
    return spread(part, near).reshape(rows, width)


def body(
    tokens,
    cotangent,
    patch_counts,
    time_buckets,
    image_labels,
    expert_routes,
    time_table,
    label_table,
    ada_weight,
    ada_bias,
    qkv_weight,
    out_weight,
    out_bias,
    router_weight,
    expert_up,
    expert_up_bias,
    expert_down,
    expert_down_bias,
    shared_up,
    shared_up_bias,
    shared_down,
    shared_down_bias,
):
    slot_count, width = tokens.shape
    expert_count = router_weight.shape[1]
    local_count, _, hidden = expert_up.shape
    owners = lax.axis_size("expert")
    dp_count = lax.axis_size(("p0", "p1", "p2"))
    outer = lax.axis_size("p0")
    routes = expert_routes[0].T
    router_turned = router_weight.T
    modulation, condition, cond_act, place, targets, grad_branch, branch_rows = front(
        owners,
        patch_counts,
        image_labels,
        time_buckets,
        routes,
        time_table,
        label_table,
        ada_weight,
        ada_bias,
        cotangent,
        expert_count,
    )
    owner_branch = exchange(branch_rows, GROUP)
    qkv_pad, attended_flat, log_totals, hidden_one, moe_in, gates_t, send_rows = attention(
        owners,
        patch_counts,
        tokens,
        modulation,
        qkv_weight,
        out_weight,
        out_bias,
        router_turned,
        routes,
        place,
    )
    (
        shared_total,
        grad_moe_in,
        grad_sup,
        grad_sup_bias,
        grad_sdown,
        grad_sdown_bias,
        owner_rows,
    ) = shared_nets(
        owners,
        moe_in,
        grad_branch,
        shared_up,
        shared_up_bias,
        shared_down,
        shared_down_bias,
        send_rows,
    )
    shared_payload = jnp.concatenate(
        [grad_sup.reshape(-1, hidden), grad_sdown.reshape(-1, hidden)], axis=0
    )
    shared_sums = sum_everywhere(shared_payload).astype(F32)
    owner_res, grad_eup, grad_eup_bias, grad_edown, grad_edown_bias, returned_grads = routed_net(
        owners,
        owner_rows,
        owner_branch,
        expert_up,
        expert_up_bias,
        expert_down,
        expert_down_bias,
    )
    returned = exchange(owner_res, GROUP).reshape(expert_count * CAP, width)

    up_blocks = exchange(grad_eup.reshape(outer, width // outer, hidden), "p0")
    up_part = sum_blocks(up_blocks).astype(BF16).reshape(-1, width // dp_count, hidden)
    sum_eup = exchange(up_part, ("p1", "p2")).astype(F32)
    side = jnp.concatenate(
        [grad_eup_bias.reshape(dp_count, -1), grad_edown_bias.reshape(dp_count, -1)], axis=1
    )
    side_width = side.shape[1]
    side = jnp.pad(side.astype(BF16)[:, None, :], ((0, 0), (0, PAD - 1), (0, width - side_width)))
    down_payload = jnp.concatenate(
        [grad_edown.reshape(dp_count, hidden // dp_count, width), side], axis=1
    )
    down_rows = down_payload.shape[1]
    down_blocks = exchange(down_payload.reshape(outer, -1, down_rows, width), "p0")
    down_part = exchange(sum_blocks(down_blocks).astype(BF16), ("p1", "p2")).astype(F32)
    sum_edown = down_part[:, : hidden // dp_count]
    side_sums = down_part[:, hidden // dp_count]
    sum_eup_bias = side_sums[:, : hidden // dp_count]
    sum_edown_bias = side_sums[:, hidden // dp_count : side_width]

    (
        layer_out,
        grad_tokens,
        rms_row,
        grad_qkv_weight,
        grad_out_weight,
        grad_out_bias,
        grad_router,
        note,
    ) = backward(
        owners,
        patch_counts,
        image_labels,
        time_buckets,
        tokens,
        cotangent,
        modulation,
        condition,
        cond_act,
        qkv_pad,
        attended_flat,
        log_totals,
        hidden_one,
        moe_in,
        gates_t,
        targets,
        shared_total,
        grad_moe_in,
        returned_grads,
        returned,
        qkv_weight,
        out_weight,
        out_bias[None],
        router_turned,
        ada_weight,
    )

    all_rows = spread(note[:8], ALL).reshape(-1, note.shape[1])
    all_modulation = all_rows[:, : 6 * width]
    all_condition = all_rows[:, 6 * width : 7 * width]
    all_cond_act = all_rows[:, 7 * width : 8 * width]
    marks = all_rows[:, 8 * width : 8 * width + 4].astype(jnp.int32)
    sum_ada = lax.dot_general(all_cond_act, all_modulation, ROWS_FIRST, preferred_element_type=F32)
    sum_ada_bias = jnp.sum(all_modulation.astype(F32), axis=0)
    label_ids = jnp.arange(label_table.shape[0], dtype=jnp.int32)
    label_hot = ((marks[:, 0:1] * 32 + marks[:, 1:2]) == label_ids).astype(BF16)
    sum_label = lax.dot_general(label_hot, all_condition, ROWS_FIRST, preferred_element_type=F32)
    time_ids = jnp.arange(time_table.shape[0], dtype=jnp.int32)
    time_hot = ((marks[:, 2:3] * 32 + marks[:, 3:4]) == time_ids).astype(BF16)
    sum_time = lax.dot_general(time_hot, all_condition, ROWS_FIRST, preferred_element_type=F32)

    tail = jnp.concatenate(
        [
            jnp.concatenate([grad_qkv_weight, grad_out_weight], axis=1),
            grad_router.reshape(-1, hidden),
            grad_sup_bias.reshape(-1, hidden),
            jnp.pad(
                jnp.concatenate([grad_out_bias, grad_sdown_bias], axis=1),
                ((0, 0), (0, hidden - 2 * width)),
            ),
        ],
        axis=0,
    )
    used = tail.shape[0]
    near_count = lax.axis_size(("p2", "expert"))
    tail = jnp.pad(tail, ((0, -used % (16 * near_count)), (0, 0)))
    tail = sum_everywhere(tail).astype(F32)
    router_rows = width * expert_count // hidden
    shared_count = shared_up.shape[0]
    sum_qkv = tail[:width, : 3 * width]
    sum_out_weight = tail[:width, 3 * width :]
    place = width + router_rows
    sum_router = tail[width:place].reshape(expert_count, width).T
    sum_sup_bias = tail[place : place + shared_count]
    sum_out_bias = tail[place + shared_count, :width]
    sum_sdown_bias = jnp.broadcast_to(
        tail[place + shared_count, width : 2 * width][None], (shared_count, width)
    )
    half = grad_sup.size // hidden
    sum_sup = shared_sums[:half].reshape(grad_sup.shape)
    sum_sdown = shared_sums[half:].reshape(grad_sdown.shape)
    return (
        layer_out,
        grad_tokens,
        rms_row[:, :2],
        sum_time,
        sum_label,
        sum_ada,
        sum_ada_bias,
        sum_qkv,
        sum_out_weight,
        sum_out_bias,
        sum_router,
        sum_eup,
        sum_eup_bias,
        sum_edown,
        sum_edown_bias,
        sum_sup,
        sum_sup_bias,
        sum_sdown,
        sum_sdown_bias,
    )


def solution(mesh):
    dp_count = mesh.shape["dp"]
    owners = mesh.shape["expert"]
    split = Mesh(mesh.devices.reshape(dp_count // 4, 2, 2, owners), ALL)
    dp = ("p0", "p1", "p2")
    in_specs = (
        P(ALL, None),
        P(ALL, None),
        P(ALL, None),
        P(ALL),
        P(ALL, None),
        P(ALL, None, None),
        P(),
        P(),
        P(),
        P(),
        P(),
        P(),
        P(),
        P(),
        P("expert", None, None),
        P("expert", None),
        P("expert", None, None),
        P("expert", None),
        P(),
        P(),
        P(),
        P(),
    )
    out_specs = (
        P(ALL, None),
        P(ALL, None),
        P(ALL, None),
        P(),
        P(),
        P(),
        P(),
        P(),
        P(),
        P(),
        P(),
        P("expert", dp, None),
        P("expert", dp),
        P("expert", dp, None),
        P("expert", dp),
        P(),
        P(),
        P(),
        P(),
    )
    return jax.shard_map(body, mesh=split, in_specs=in_specs, out_specs=out_specs, check_vma=False)
```

time: 709 us -> 564 us (0.80)
  Pallas kernels: 63.3 us -> 190 us
  matrix products: 120 us -> 5.84 us
  other arithmetic: 85.8 us -> 23 us
  blocking collectives: 68.2 us -> 19.4 us
  local copies, waits for them, and re-layouts: 87.8 us -> 39.6 us
  waiting for transfers between devices: 196 us -> 216 us
  starting transfers between devices: 70.8 us -> 59.1 us
    pallas_call x2 -> x5, Pallas kernels: 63.3 us -> 190 us  [the longest x1 80 us: routed_net(): pl.pallas_call(functools.partial(routed_kernel, owners), in_specs=[in_vme...]
    dot_general x32 -> x0, matrix products: 114 us -> none  [the longest x2 15.4 us: attend_backward(): jnp.einsum('qhd,khd->hqk', grad_rows_here, value_rows, preferred_element_...]
    all_to_all x2 -> x1, blocking collectives: 68.2 us -> 19.4 us  [exchange(): return lax.all_to_all(blocks, axes, split_axis=0, concat_axis=0, tiled=True)]
    convert_element_type x9 -> x1, other arithmetic: 20.8 us -> 0.02 us  [body(): marks = all_rows[:, 8 * width:8 * width + 4].astype(jnp.int32)]
    all_to_all x16 -> x14, waiting for transfers between devices: 196 us -> 216 us  [exchange(): return lax.all_to_all(blocks, axes, split_axis=0, concat_axis=0, tiled=True)]
    slice x16 -> x2, local copies, waits for them, and re-layouts: 15.2 us -> 0.01 us  [the longest x1 0.01 us: body(): all_rows = spread(note[:8], ALL).reshape(-1, note.shape[1])]
    reduce_sum x12 -> x0, other arithmetic: 13.1 us -> none  [the longest x2 5.84 us: attend_forward(): row_total = jnp.sum(expo_scores, axis=-1, keepdims=True)]
    unnamed x236 -> x28, local copies, waits for them, and re-layouts: 12.7 us -> 0.07 us
  transfers between devices with their start and end apart: 16 -> 14, of which waited for: 12 -> 11; matrix products, arithmetic and copies ran while one was open for 30% -> 10% of each run, Pallas kernels for 9% -> 33%
where the time goes in v2:
time: 564 us; the launch traced here: 555 us
  waiting for transfers between devices  216 us (38%)
  Pallas kernels  190 us (34%)
  starting transfers between devices  59.1 us (10%)
  local copies, waits for them, and re-layouts  39.6 us (7%)
  other arithmetic  23 us (4%)
  blocking collectives  19.4 us (3%)
  matrix products  5.84 us (1%)
    all_to_all x14, waiting for transfers between devices, exchange(): return lax.all_to_all(blocks, axes, split_axis=0, concat_axis=0, tiled=True)  216 us
    pallas_call x1, Pallas kernels, routed_net(): pl.pallas_call(functools.partial(routed_kernel, owners), in_specs=[in_vme...  80 us
    all_to_all x14, starting transfers between devices, exchange(): return lax.all_to_all(blocks, axes, split_axis=0, concat_axis=0, tiled=True)  59.1 us
    pallas_call x1, Pallas kernels, backward(): pl.pallas_call(functools.partial(backward_kernel, owners, experts // owne...  40.5 us
    pallas_call x1, Pallas kernels, shared_nets(): pl.pallas_call(functools.partial(shared_kernel, owners), grid=(nets, hidd...  36.6 us
    pallas_call x1, Pallas kernels, attention(): pl.pallas_call(functools.partial(attention_kernel, owners, experts // own...  24.5 us
    all_to_all x1, blocking collectives, exchange(): return lax.all_to_all(blocks, axes, split_axis=0, concat_axis=0, tiled=True)  19.4 us
  transfers between devices with their start and end apart: 14, of which 11 were waited for; matrix products, arithmetic and copies ran while one was open for 10% of the time, Pallas kernels for 33%

profile of v2, /device:TPU:0, one launch (start us, length us, event | category | flops | bytes accessed | tf_op | source)
XLA Modules:
  0.0 554.8 jit_solution(2269496971924239534)
XLA Ops:
  1.3 1.3 broadcast_in_dim.30.ada_bias_ref
  2.6 8.2 %front.1 = (f32[8,2304]{1,0:T(8,128)}, f32[8,384]{1,0:T(8,128)}, bf16[8,384]{1,0:T(8,128)(2,1)}, f32[16,1024]{1,0:T(8,128)}, f32[1024,128]{1,0:T(8,128)}, /*inde...) custom-call(s32[1,5]{1,0:T(1,128)} %counts_ref.5, s32[1,5]{1,0:T(1,128)} %labels_ref.3, s32[1]{0:T(128)S(6)} %copy.69.time_ref, ...), custom_call_target="tpu_custom_call" | custom-call | tf_op jit(solution)/shard_map/front/pallas_call | solution.py:200
  10.8 6.5 %all-to-all-start = ((bf16[16,160,384]{2,1,0:T(8,128)(2,1)}), bf16[16,160,384]{2,1,0:T(8,128)(2,1)}, u32[]{:S(2)}, u32[]{:S(2)}) async-start(bf16[16,160,384]{2,1,0:T(8,128)(2,1)} %get-tuple-element.70), calls=%async_computation | async-start | bytes 3932160 | tf_op jit(solution)/shard_map/all_to_all | solution.py:971
  19.1 24.5 %attention.1 = (bf16[1408,1152]{1,0:T(8,128)(2,1)}, bf16[1024,384]{1,0:T(8,128)(2,1)}, f32[8,1024]{1,0:T(8,128)}, f32[1024,384]{1,0:T(8,128)}, bf16[1024,384]{1,...) custom-call(s32[1,5]{1,0:T(1,128)} %counts_ref.5, bf16[1024,384]{1,0:T(8,128)(2,1)} %tokens_ref.3, ...), custom_call_target="tpu_custom_call" | custom-call | tf_op jit(solution)/shard_map/attention/pallas_call | solution.py:356
  43.6 36.6 %shared_nets.1 = (f32[1024,384]{1,0:T(8,128)}, f32[1024,384]{1,0:T(8,128)}, bf16[2,384,1536]{2,1,0:T(8,128)(2,1)}, f32[2,1,1536]{2,1,0:T(1,128)}, bf16[2,1536,38...) custom-call(bf16[1024,384]{1,0:T(8,128)(2,1)} %get-tuple-element.62.x_ref.moe_ref, ...), custom_call_target="tpu_custom_call" | custom-call | tf_op jit(solution)/shard_map/shared_nets/pallas_call | solution.py:496
  80.2 3.9 reshape.149
  84.1 4.2 pad_maximum_fusion
  88.2 5.1 all-to-all-start.11
  94.6 80.0 %routed_net.1 = (bf16[16,160,384]{2,1,0:T(8,128)(2,1)}, bf16[384,1536]{1,0:T(8,128)(2,1)}, f32[1,1536]{1,0:T(1,128)}, bf16[1536,384]{1,0:T(8,128)(2,1)}, f32[1,3...) custom-call(bf16[16,176,384]{2,1,0:T(8,128)(2,1)} %get-tuple-element.69.x_ref, bf16[16,160,384]{2,1,0:T(8,128)(2,1)} %all-to-all-done.g_ref, ...), custom_call_target="tpu_custom_call" | custom-call | tf_op jit(solution)/shard_map/routed_net/pallas_call | solution.py:648
  174.7 4.1 all-to-all-start.7
  179.1 1.2 pad_maximum_fusion.1
  180.3 28.1 %all-to-all-done.7 = bf16[2,192,1536]{2,1,0:T(8,128)(2,1)S(1)} async-done(((bf16[2,192,1536]{2,1,0:T(8,128)(2,1)}), bf16[2,192,1536]{2,1,0:T(8,128)(2,1)S(1)}, u32[]{:S(2)}, u32[]{:S(2)}) %all-to-all-start.7) | async-done | bytes 1179680 | tf_op jit(solution)/shard_map/all_to_all | solution.py:971
  208.4 3.6 all-to-all-start.9
  212.0 3.3 reduce_sum.86
  215.3 0.9 reshape.151
  216.3 1.1 copy.57
  217.4 23.3 %all-to-all-done.9 = bf16[2,4,208,384]{3,2,1,0:T(8,128)(2,1)S(1)} async-done(((bf16[2,4,208,384]{3,2,1,0:T(8,128)(2,1)}), bf16[2,4,208,384]{3,2,1,0:T(8,128)(2,1)S(1)}, u32[]{:S(2)}, u32[]{:S(2)}) %all-to-all-start.9) | async-done | bytes 1277984 | tf_op jit(solution)/shard_map/all_to_all | solution.py:971
  240.7 19.4 %all_to_all.75 = bf16[4,192,384]{2,1,0:T(8,128)(2,1)} all-to-all(bf16[4,192,384]{2,1,0:T(8,128)(2,1)S(1)} %copy.57), channel_id=1, replica_groups=mesh['p0'=2,'p1'=2,'p2'=2,'expert'=4] {'p0','p1'}, dimensions={0} | all-to-all | bytes 1179648 | tf_op jit(solution)/shard_map/all_to_all | solution.py:971
  260.2 3.9 all-to-all-start.1
  264.1 2.4 reduce_sum.84
  266.6 25.1 %all-to-all-done.1 = bf16[16,160,384]{2,1,0:T(8,128)(2,1)S(1)} async-done(((bf16[16,160,384]{2,1,0:T(8,128)(2,1)}), bf16[16,160,384]{2,1,0:T(8,128)(2,1)S(1)}, u32[]{:S(2)}, u32[]{:S(2)}) %all-to-all-start.1) | async-done | bytes 1966112 | tf_op jit(solution)/shard_map/all_to_all | solution.py:971
  291.6 4.1 all-to-all-start.8
  295.8 40.5 %backward.1 = (bf16[1024,384]{1,0:T(8,128)(2,1)}, f32[1024,384]{1,0:T(8,128)}, f32[1,128]{1,0:T(1,128)}, f32[384,1152]{1,0:T(8,128)}, f32[384,384]{1,0:T(8,128)}...) custom-call(s32[1,5]{1,0:T(1,128)} %counts_ref.5, s32[1,5]{1,0:T(1,128)} %labels_ref.3, ...), custom_call_target="tpu_custom_call" | custom-call | tf_op jit(solution)/shard_map/backward/pallas_call | solution.py:933
  336.3 0.7 convert.45
  337.0 0.7 convert.43
  337.7 1.1 convert.42
  338.9 1.6 convert.41
  340.4 1.3 fusion.8
  341.7 3.9 all-to-all-start.3
  345.6 1.2 reduce_sum.87
  346.8 19.9 %all-to-all-done.3 = bf16[8,64,1536]{2,1,0:T(8,128)(2,1)S(1)} async-done(((bf16[8,64,1536]{2,1,0:T(8,128)(2,1)}), bf16[8,64,1536]{2,1,0:T(8,128)(2,1)S(1)}, u32[]{:S(2)}, u32[]{:S(2)}) %all-to-all-start.3) | async-done | bytes 1572896 | tf_op jit(solution)/shard_map/all_to_all | solution.py:971
  366.7 0.9 broadcast_in_dim.71
  367.5 4.1 all-to-all-start.13
  372.0 0.7 copy.54
  372.7 12.5 %all-to-all-done.13 = bf16[4,192,384]{2,1,0:T(8,128)(2,1)} async-done(((bf16[4,192,384]{2,1,0:T(8,128)(2,1)}), bf16[4,192,384]{2,1,0:T(8,128)(2,1)}, u32[]{:S(2)}, u32[]{:S(2)}) %all-to-all-start.13) | async-done | bytes 589856 | tf_op jit(solution)/shard_map/all_to_all | solution.py:971
  385.1 3.4 all-to-all-start.4
  388.5 1.2 reduce_sum.85
  389.7 5.0 all-to-all-done.4
  394.7 3.5 all-to-all-start.10
  398.3 7.2 %all-to-all-done.10 = bf16[4,208,384]{2,1,0:T(8,128)(2,1)S(1)} async-done(((bf16[4,208,384]{2,1,0:T(8,128)(2,1)}), bf16[4,208,384]{2,1,0:T(8,128)(2,1)S(1)}, u32[]{:S(2)}, u32[]{:S(2)}) %all-to-all-start.10) | async-done | bytes 639008 | tf_op jit(solution)/shard_map/all_to_all | solution.py:971
  405.5 0.7 broadcast_in_dim.68
  406.2 3.4 all-to-all-start.5
  409.6 1.1 copy.62
  410.7 5.1 all-to-all-done.5
  415.8 2.6 broadcast_in_dim.73
  418.4 6.8 %all-to-all-start.14 = ((bf16[8,192,1536]{2,1,0:T(8,128)(2,1)}), bf16[8,192,1536]{2,1,0:T(8,128)(2,1)}, u32[]{:S(2)}, u32[]{:S(2)}) async-start(bf16[8,192,1536]{2,1,0:T(8,128)(2,1)} %broadcast_in_dim.73), calls=%async_computation.14 | async-start | bytes 9437184 | tf_op jit(solution)/shard_map/all_to_all | solution.py:971
  425.2 54.8 %all-to-all-done.14 = bf16[8,192,1536]{2,1,0:T(8,128)(2,1)} async-done(((bf16[8,192,1536]{2,1,0:T(8,128)(2,1)}), bf16[8,192,1536]{2,1,0:T(8,128)(2,1)}, u32[]{:S(2)}, u32[]{:S(2)}) %all-to-all-start.14) | async-done | bytes 4718624 | tf_op jit(solution)/shard_map/all_to_all | solution.py:971
  480.0 1.3 broadcast_in_dim.67
  481.3 2.9 all-to-all-start.2
  484.2 2.2 convert_element_type.55
  486.5 0.7 slice.105
  487.7 1.1 slice.104
  488.8 7.4 %fusion.22 = (f32[4,192,1536]{2,1,0:T(8,128)}, f32[4,192,1536]{2,1,0:T(8,128)}) fusion(bf16[8,192,1536]{2,1,0:T(8,128)(2,1)} %all-to-all-done.14), kind=kLoop, calls=%fused_computation.43 | loop fusion | bytes 18874368 | tf_op jit(solution)/shard_map/slice | solution.py:1188
  496.3 6.1 %reshape.153 = f32[2,1536,384]{2,1,0:T(8,128)} reshape(f32[4,192,1536]{2,1,0:T(8,128)} %get-tuple-element.150) | data formatting | bytes 9437184 | tf_op jit(solution)/shard_map/reshape | solution.py:1188
  502.4 21.1 %all-to-all-done.2 = bf16[32,8,3200]{2,1,0:T(8,128)(2,1)S(1)} async-done(((bf16[32,8,3200]{2,1,0:T(8,128)(2,1)}), bf16[32,8,3200]{2,1,0:T(8,128)(2,1)S(1)}, u32[]{:S(2)}, u32[]{:S(2)}) %all-to-all-start.2) | async-done | bytes 1638432 | tf_op jit(solution)/shard_map/all_to_all | solution.py:971
  523.4 1.3 broadcast_in_dim.70
  524.7 3.6 all-to-all-start.6
  528.6 0.8 convert_reduce_fusion
  529.4 1.7 fusion.9
  531.1 1.7 fusion.10
  532.8 2.5 fusion.11
  535.2 14.0 %all-to-all-done.6 = bf16[8,64,1536]{2,1,0:T(8,128)(2,1)S(1)} async-done(((bf16[8,64,1536]{2,1,0:T(8,128)(2,1)}), bf16[8,64,1536]{2,1,0:T(8,128)(2,1)S(1)}, u32[]{:S(2)}, u32[]{:S(2)}) %all-to-all-start.6) | async-done | bytes 1572896 | tf_op jit(solution)/shard_map/all_to_all | solution.py:971
  551.0 0.9 slice.99
  551.8 1.3 slice.98
  (61 shorter events, 7.6 us)
Async XLA Ops:
  10.8 6.5 %copy-start.10 = (f32[384]{0:T(512)S(1)}, f32[384]{0:T(512)}, u32[]{:S(2)}) copy-start(f32[384]{0:T(512)} %param.34) | copy-start | bytes 4612
  10.8 7.1 %copy-start.9 = (f32[2,384]{1,0:T(2,128)S(1)}, f32[2,384]{1,0:T(2,128)}, u32[]{:S(2)}) copy-start(f32[2,384]{1,0:T(2,128)} %param.43) | copy-start | bytes 9220
  10.8 7.7 %copy-start.5 = (f32[2,1536]{1,0:T(2,128)S(1)}, f32[2,1536]{1,0:T(2,128)}, u32[]{:S(2)}) copy-start(f32[2,1536]{1,0:T(2,128)} %param.41) | copy-start | bytes 36868
  10.8 77.4 %all-to-all-start = ((bf16[16,160,384]{2,1,0:T(8,128)(2,1)}), bf16[16,160,384]{2,1,0:T(8,128)(2,1)}, u32[]{:S(2)}, u32[]{:S(2)}) async-start(bf16[16,160,384]{2,1,0:T(8,128)(2,1)} %get-tuple-element.70), calls=%async_computation | async-start | bytes 3932160 | tf_op jit(solution)/shard_map/all_to_all | solution.py:971
  88.2 5.2 copy-start.7
  88.2 5.8 %copy-start.4 = (f32[4,1536]{1,0:T(4,128)S(1)}, f32[4,1536]{1,0:T(4,128)}, u32[]{:S(2)}) copy-start(f32[4,1536]{1,0:T(4,128)} %param.37) | copy-start | bytes 73732
  88.2 86.4 %all-to-all-start.11 = ((bf16[8,192,1536]{2,1,0:T(8,128)(2,1)}), bf16[8,192,1536]{2,1,0:T(8,128)(2,1)}, u32[]{:S(2)}, u32[]{:S(2)}) async-start(bf16[8,192,1536]{2,1,0:T(8,128)(2,1)} %bitcast.33), calls=%async_computation.11 | async-start | bytes 9437184 | tf_op jit(solution)/shard_map/all_to_all | solution.py:971
  174.6 4.2 copy-start.12
  174.6 4.3 copy-start.8
  174.6 4.5 copy-start.2
  174.7 33.7 %all-to-all-start.7 = ((bf16[2,192,1536]{2,1,0:T(8,128)(2,1)}), bf16[2,192,1536]{2,1,0:T(8,128)(2,1)S(1)}, u32[]{:S(2)}, u32[]{:S(2)}) async-start(bf16[2,192,1536]{2,1,0:T(8,128)(2,1)} %bitcast.46), calls=%async_computation.7 | async-start | bytes 2359296 | tf_op jit(solution)/shard_map/all_to_all | solution.py:971
  208.4 51.7 %copy-start.1 = (bf16[2,192,1536]{2,1,0:T(8,128)(2,1)}, bf16[2,192,1536]{2,1,0:T(8,128)(2,1)S(1)}, u32[]{:S(2)}) copy-start(bf16[2,192,1536]{2,1,0:T(8,128)(2,1)S(1)} %all-to-all-done.7) | copy-start | bytes 3538948
  208.4 32.3 %all-to-all-start.9 = ((bf16[2,4,208,384]{3,2,1,0:T(8,128)(2,1)}), bf16[2,4,208,384]{3,2,1,0:T(8,128)(2,1)S(1)}, u32[]{:S(2)}, u32[]{:S(2)}) async-start(bf16[2,4,208,384]{3,2,1,0:T(8,128)(2,1)} %pad_maximum_fusion.1), calls=%async_computation.9 | async-start | bytes 2555904 | tf_op jit(solution)/shard_map/all_to_all | solution.py:971
  260.2 31.5 %all-to-all-start.1 = ((bf16[16,160,384]{2,1,0:T(8,128)(2,1)}), bf16[16,160,384]{2,1,0:T(8,128)(2,1)S(1)}, u32[]{:S(2)}, u32[]{:S(2)}) async-start(bf16[16,160,384]{2,1,0:T(8,128)(2,1)} %get-tuple-element.72), calls=%async_computation.1 | async-start | bytes 3932160 | tf_op jit(solution)/shard_map/all_to_all | solution.py:971
  264.1 31.7 %copy-start.11 = (f32[1,384]{1,0:T(1,128)S(1)}, f32[1,384]{1,0:T(1,128)}, u32[]{:S(2)}) copy-start(f32[1,384]{1,0:T(1,128)} %get-tuple-element.82) | copy-start | bytes 4612
  264.1 31.7 %copy-start.6 = (f32[2,1,1536]{2,1,0:T(1,128)S(1)}, f32[2,1,1536]{2,1,0:T(1,128)}, u32[]{:S(2)}) copy-start(f32[2,1,1536]{2,1,0:T(1,128)} %get-tuple-element.80) | copy-start | bytes 36868
  291.6 4.2 copy-start
  291.6 50.1 %all-to-all-start.8 = ((bf16[4,48,1536]{2,1,0:T(8,128)(2,1)}), bf16[4,48,1536]{2,1,0:T(8,128)(2,1)}, u32[]{:S(2)}, u32[]{:S(2)}) async-start(bf16[4,48,1536]{2,1,0:T(8,128)(2,1)} %bitcast.42), calls=%async_computation.8 | async-start | bytes 1179648 | tf_op jit(solution)/shard_map/all_to_all | solution.py:971
  341.7 24.9 %all-to-all-start.3 = ((bf16[8,64,1536]{2,1,0:T(8,128)(2,1)}), bf16[8,64,1536]{2,1,0:T(8,128)(2,1)S(1)}, u32[]{:S(2)}, u32[]{:S(2)}) async-start(bf16[8,64,1536]{2,1,0:T(8,128)(2,1)} %bitcast.7), calls=%async_computation.3 | async-start | bytes 3145728 | tf_op jit(solution)/shard_map/all_to_all | solution.py:971
  367.5 17.6 %all-to-all-start.13 = ((bf16[4,192,384]{2,1,0:T(8,128)(2,1)}), bf16[4,192,384]{2,1,0:T(8,128)(2,1)}, u32[]{:S(2)}, u32[]{:S(2)}) async-start(bf16[4,192,384]{2,1,0:T(8,128)(2,1)} %broadcast_in_dim.71), calls=%async_computation.13 | async-start | bytes 1179648 | tf_op jit(solution)/shard_map/all_to_all | solution.py:971
  385.1 9.6 %all-to-all-start.4 = ((bf16[4,64,384]{2,1,0:T(8,128)(2,1)}), bf16[4,64,384]{2,1,0:T(8,128)(2,1)S(1)}, u32[]{:S(2)}, u32[]{:S(2)}) async-start(bf16[4,64,384]{2,1,0:T(8,128)(2,1)} %copy.54), calls=%async_computation.4 | async-start | bytes 393216 | tf_op jit(solution)/shard_map/all_to_all | solution.py:971
  394.7 10.8 %all-to-all-start.10 = ((bf16[4,208,384]{2,1,0:T(8,128)(2,1)}), bf16[4,208,384]{2,1,0:T(8,128)(2,1)S(1)}, u32[]{:S(2)}, u32[]{:S(2)}) async-start(bf16[4,208,384]{2,1,0:T(8,128)(2,1)} %reduce_sum.85), calls=%async_computation.10 | async-start | bytes 1277952 | tf_op jit(solution)/shard_map/all_to_all | solution.py:971
  406.2 9.6 %all-to-all-start.5 = ((bf16[4,64,384]{2,1,0:T(8,128)(2,1)}), bf16[4,64,384]{2,1,0:T(8,128)(2,1)S(1)}, u32[]{:S(2)}, u32[]{:S(2)}) async-start(bf16[4,64,384]{2,1,0:T(8,128)(2,1)} %broadcast_in_dim.68), calls=%async_computation.5 | async-start | bytes 393216 | tf_op jit(solution)/shard_map/all_to_all | solution.py:971
  418.4 6.8 %copy-start.3 = (bf16[16,3200]{1,0:T(8,128)(2,1)S(1)}, bf16[16,3200]{1,0:T(8,128)(2,1)}, u32[]{:S(2)}) copy-start(bf16[16,3200]{1,0:T(8,128)(2,1)} %get-tuple-element.76) | copy-start | bytes 307204
  418.4 61.6 %all-to-all-start.14 = ((bf16[8,192,1536]{2,1,0:T(8,128)(2,1)}), bf16[8,192,1536]{2,1,0:T(8,128)(2,1)}, u32[]{:S(2)}, u32[]{:S(2)}) async-start(bf16[8,192,1536]{2,1,0:T(8,128)(2,1)} %broadcast_in_dim.73), calls=%async_computation.14 | async-start | bytes 9437184 | tf_op jit(solution)/shard_map/all_to_all | solution.py:971
  481.3 42.1 %all-to-all-start.2 = ((bf16[32,8,3200]{2,1,0:T(8,128)(2,1)}), bf16[32,8,3200]{2,1,0:T(8,128)(2,1)S(1)}, u32[]{:S(2)}, u32[]{:S(2)}) async-start(bf16[32,8,3200]{2,1,0:T(8,128)(2,1)} %broadcast_in_dim.67), calls=%async_computation.2 | async-start | bytes 3276800 | tf_op jit(solution)/shard_map/all_to_all | solution.py:971
  524.7 24.5 %all-to-all-start.6 = ((bf16[8,64,1536]{2,1,0:T(8,128)(2,1)}), bf16[8,64,1536]{2,1,0:T(8,128)(2,1)S(1)}, u32[]{:S(2)}, u32[]{:S(2)}) async-start(bf16[8,64,1536]{2,1,0:T(8,128)(2,1)} %broadcast_in_dim.70), calls=%async_computation.6 | async-start | bytes 3145728 | tf_op jit(solution)/shard_map/all_to_all | solution.py:971

commit v3 on v2

--- a/solution.py
+++ b/solution.py
@@ -378,16 +378,61 @@
     )(counts, tokens, mod, qkv_weight, out_weight, out_bias[None], router, routes, pos)
 
 
+def axes_here():
+    return [lax.axis_index(name) for name in ALL]
+
+
 def group_partner(owners, a, b, c):
-    first = lax.rem(lax.axis_index("p1") + a, 2)
-    second = lax.rem(lax.axis_index("p2") + b, 2)
-    third = lax.rem(lax.axis_index("expert") + c, owners)
-    device = (lax.axis_index("p0"), first, second, third)
-    return device, (first * 2 + second) * owners + third
+    zero, one, two, three = axes_here()
+    first = lax.rem(one + a, 2)
+    second = lax.rem(two + b, 2)
+    third = lax.rem(three + c, owners)
+    return (zero, first, second, third), (first * 2 + second) * owners + third
 
 
 def group_offsets(owners):
-    return [(a, b, c) for a in range(2) for b in range(2) for c in range(owners)]
+    offsets = [(a, b, c) for a in range(2) for b in range(2) for c in range(owners)]
+    return sorted(offsets, key=lambda o: -(o[0] + o[1] + (2 * o[2] >= owners)))
+
+
+def sibling():
+    zero, one, two, three = axes_here()
+    odd = lax.rem(three, 2)
+    return (zero, one, two, three + 1 - 2 * odd)
+
+
+def plane_partner(b, h):
+    zero, one, two, three = axes_here()
+    odd = lax.rem(three, 2)
+    second = lax.rem(two + b, 2)
+    half = lax.rem(three // 2 + h, 2)
+    return (zero, one, second, half * 2 + odd), second, half
+
+
+def line_partner(a, b):
+    zero, one, two, three = axes_here()
+    first = lax.rem(zero + a, 2)
+    second = lax.rem(one + b, 2)
+    return (first, second, two, three), first * 2 + second
+
+
+def owner_partner(a, b):
+    zero, one, two, three = axes_here()
+    first = lax.rem(one + a, 2)
+    second = lax.rem(two + b, 2)
+    return (zero, first, second, three), first * 2 + second
+
+
+def column_partner(a, b, c):
+    zero, one, two, three = axes_here()
+    first = lax.rem(zero + a, 2)
+    second = lax.rem(one + b, 2)
+    third = lax.rem(two + c, 2)
+    return (first, second, third, three), (first * 2 + second) * 2 + third
+
+
+OTHERS = [(1, 1), (0, 1), (1, 0)]
+COLUMN = [(1, 1, 1), (1, 1, 0), (1, 0, 1), (1, 0, 0), (0, 1, 1), (0, 1, 0), (0, 0, 1)]
 
 
 def greet(devices):
@@ -395,6 +440,24 @@
     for device in devices:
         pl.semaphore_signal(barrier, inc=1, device_id=device, device_id_type=MESH)
     pl.semaphore_wait(barrier, len(devices))
+
+
+def push(source, target, send_sem, recv_sem, device):
+    copy = pltpu.make_async_remote_copy(
+        src_ref=source,
+        dst_ref=target,
+        send_sem=send_sem,
+        recv_sem=recv_sem,
+        device_id=device,
+        device_id_type=MESH,
+    )
+    copy.start()
+    return copy
+
+
+def finish_all(copies):
+    for copy in copies:
+        copy.wait()
 
 
 def group_copy(owners, index, offsets, source, target, send_sems, recv_sems):
@@ -429,9 +492,8 @@
     rows_ref,
     y_ref,
     dx_ref,
-    dup_ref,
+    wire_ref,
     dbu_ref,
-    ddn_ref,
     dbd_ref,
     owner_ref,
     xt,
@@ -447,14 +509,14 @@
     copies = [
         group_copy(owners, index, offset, rows_ref, owner_ref, send_sems, recv_sems)
         for index, offset in enumerate(offsets)
-        if index
+        if any(offset)
     ]
     _, me = group_partner(owners, 0, 0, 0)
     own = pltpu.make_async_copy(rows_ref.at[me], owner_ref.at[me], own_sem)
 
     @pl.when((net == 0) & (chunk == 0))
     def _():
-        greet([group_partner(owners, *offset)[0] for offset in offsets[1:]])
+        greet([group_partner(owners, *offset)[0] for offset in offsets if any(offset)])
         own.start()
         for copy in copies:
             copy.start()
@@ -473,9 +535,9 @@
     y_ref[...] += dot(act, dn)
     dx_ref[...] += dot_t(dpre, up)
     dup = dot(xt[...], dpre)
-    dup_ref[0] = dup[:width].astype(BF16)
+    wire_ref[0, 0] = dup[:width].astype(BF16)
     dbu_ref[0] = dup[width : width + 1]
-    ddn_ref[0] = dot(gt[...], act).T.astype(BF16)
+    wire_ref[1, 0] = dot(gt[...], act).astype(BF16)
 
     @pl.when((net == pl.num_programs(0) - 1) & (chunk == pl.num_programs(1) - 1))
     def _():
@@ -508,18 +570,16 @@
         out_specs=[
             whole((rows, width)),
             whole((rows, width)),
-            pl.BlockSpec((1, width, chunk), lambda n, h: (n, 0, h)),
+            pl.BlockSpec((2, 1, width, chunk), lambda n, h: (0, n, 0, h)),
             pl.BlockSpec((1, 1, chunk), lambda n, h: (n, 0, h)),
-            pl.BlockSpec((1, chunk, width), lambda n, h: (n, h, 0)),
             whole((1, width)),
             anywhere(),
         ],
         out_shape=[
             like((rows, width), F32),
             like((rows, width), F32),
-            like((nets, width, hidden), BF16),
+            like((2, nets, width, hidden), BF16),
             like((nets, 1, hidden), F32),
-            like((nets, hidden, width), BF16),
             like((1, width), F32),
             like(rows_out.shape, BF16),
         ],
@@ -539,18 +599,21 @@
 
 def routed_kernel(
     owners,
+    reduce,
     x_ref,
     g_ref,
     up_any,
     bu_ref,
     dn_any,
     bd_ref,
+    wire_any,
     y_ref,
     dup_ref,
-    dbu_ref,
     ddn_ref,
-    dbd_ref,
+    side_ref,
     back_ref,
+    part_ref,
+    rest_ref,
     up,
     dn,
     xt,
@@ -564,6 +627,12 @@
     send_sems,
     recv_sems,
     own_sem,
+    keep,
+    got,
+    pieces,
+    keep_sem,
+    sum_sends,
+    sum_recvs,
 ):
     width, hidden = up.shape
     chunk = 768
@@ -576,13 +645,19 @@
         load.start()
     offsets = group_offsets(owners)
     places = [group_partner(owners, *offset)[1] for offset in offsets]
-    greet([group_partner(owners, *offset)[0] for offset in offsets[1:]])
+    greet([group_partner(owners, *offset)[0] for offset in offsets if any(offset)])
     copies = [
         group_copy(owners, index, offset, outgoing, back_ref, send_sems, recv_sems)
-        if index
-        else pltpu.make_async_copy(outgoing.at[places[0]], back_ref.at[places[0]], own_sem)
+        if any(offset)
+        else pltpu.make_async_copy(outgoing.at[places[index]], back_ref.at[places[index]], own_sem)
         for index, offset in enumerate(offsets)
     ]
+    sums = []
+    if reduce:
+        odd = lax.rem(lax.axis_index("expert"), 2)
+        mine = pltpu.make_async_copy(wire_any.at[odd], keep, keep_sem)
+        mine.start()
+        swap = push(wire_any.at[1 - odd], got, sum_sends.at[3], sum_recvs.at[3], sibling())
 
     lines[...] = jnp.zeros_like(lines)
     for index, place in enumerate(places):
@@ -631,31 +706,59 @@
         for k in members:
             outgoing[places[k], CAP:, :] = tail_rows(lines[k - first : k - first + 1, :], width)
             copies[k].start()
-    dbd_ref[...] = dbd
+        if reduce and first == 0:
+            mine.wait()
+            swap.wait()
+            for net in range(keep.shape[0]):
+                for r in range(0, width, 64):
+                    rows = slice(r, r + 64)
+                    total = keep[net, rows].astype(F32) + got[net, rows].astype(F32)
+                    keep[net, rows] = total.astype(BF16)
+            for index, (b, h) in enumerate(OTHERS):
+                device, net, half = plane_partner(b, h)
+                source = keep.at[net, pl.ds(half * (width // 2), width // 2), pl.ds(0, hidden // 2)]
+                sums.append(
+                    push(source, pieces.at[index], sum_sends.at[index], sum_recvs.at[index], device)
+                )
+    side_ref[...] = jnp.zeros_like(side_ref)
+    side_ref[1:2, :width] = dbd
     for h in range(0, hidden, 512):
         dup = dot(xt[...], dpres[:, h : h + 512])
         dup_ref[:, h : h + 512] = dup[:width].astype(BF16)
-        dbu_ref[:, h : h + 512] = dup[width : width + 1]
+        side_ref[0:1, h : h + 512] = dup[width : width + 1]
         ddn_ref[h : h + 512, :] = dot(gt[...], acts[:, h : h + 512]).T.astype(BF16)
-    for copy in copies:
-        copy.wait()
-
-
-def routed_net(owners, x, g, up, bias_up, down, bias_down):
+    if reduce:
+        finish_all(sums)
+        _, net, half = plane_partner(0, 0)
+        own = pl.ds(pl.multiple_of(half * (width // 2), 64), width // 2)
+        total = keep[net, own, : hidden // 2].astype(F32)
+        for index in range(len(OTHERS)):
+            total = total + pieces[index].astype(F32)
+        part_ref[...] = total.astype(BF16)
+        rest_ref[...] = keep[:, :, hidden // 2 :]
+    finish_all(copies)
+
+
+def routed_net(owners, reduce, x, g, up, bias_up, down, bias_down, wire):
     count = x.shape[0]
     rows = count * CAP
     width, hidden = up.shape[1:]
+    nets = wire.shape[1]
+    half = (nets, width, hidden) if reduce else (1, 16, 128)
+    piece = (width // 2, hidden // 2) if reduce else (16, 128)
+    later = (nets, width, hidden // 2) if reduce else (1, 16, 128)
     return pl.pallas_call(
-        functools.partial(routed_kernel, owners),
-        in_specs=[in_vmem(), in_vmem(), anywhere(), in_vmem(), anywhere(), in_vmem()],
-        out_specs=[in_vmem()] * 5 + [anywhere()],
+        functools.partial(routed_kernel, owners, reduce),
+        in_specs=[in_vmem(), in_vmem(), anywhere(), in_vmem(), anywhere(), in_vmem(), anywhere()],
+        out_specs=[in_vmem()] * 4 + [anywhere(), in_vmem(), in_vmem()],
         out_shape=[
             like((count, CAP, width), BF16),
             like((width, hidden), BF16),
-            like((1, hidden), F32),
             like((hidden, width), BF16),
-            like((1, width), F32),
+            like((8, hidden), F32),
             like((count, CAP + PAD, width), BF16),
+            like(piece, BF16),
+            like(later, BF16),
         ],
         scratch_shapes=[
             pltpu.VMEM((width, hidden), BF16),
@@ -671,12 +774,18 @@
             pltpu.SemaphoreType.DMA((count,)),
             pltpu.SemaphoreType.DMA((count,)),
             pltpu.SemaphoreType.DMA,
+            pltpu.VMEM(half, BF16),
+            pltpu.VMEM(half, BF16),
+            pltpu.VMEM((3,) + piece, BF16),
+            pltpu.SemaphoreType.DMA,
+            pltpu.SemaphoreType.DMA((4,)),
+            pltpu.SemaphoreType.DMA((4,)),
         ],
         compiler_params=pltpu.CompilerParams(
             vmem_limit_bytes=VMEM_BYTES, collective_id=2, has_side_effects=True
         ),
         name="routed_net",
-    )(x, g, up, bias_up[:, None, :], down, bias_down[:, None, :])
+    )(x, g, up, bias_up[:, None, :], down, bias_down[:, None, :], wire)
 
 
 def member_rows(bounds, first, rows):
@@ -693,6 +802,7 @@
 def backward_kernel(
     owners,
     local_count,
+    reduce,
     counts_ref,
     labels_ref,
     time_ref,
@@ -700,7 +810,6 @@
     cot_ref,
     mod_ref,
     cond_ref,
-    act_ref,
     qkv_ref,
     att_ref,
     lse_ref,
@@ -717,6 +826,9 @@
     out_b_ref,
     router_ref,
     ada_ref,
+    part_ref,
+    later_ref,
+    eup_any,
     layer_ref,
     dtok_ref,
     rms_ref,
@@ -725,6 +837,9 @@
     dout_b_ref,
     drouter_ref,
     note_ref,
+    quarter_ref,
+    next_ref,
+    eup_ref,
     stack,
     hot,
     rows_ext,
@@ -741,11 +856,64 @@
     lines,
     columns,
     router,
+    res,
+    send_sems,
+    recv_sems,
+    own_sem,
+    zgot,
+    zsum,
+    pieces,
+    zsends,
+    zrecvs,
 ):
     slots, width = tokens_ref.shape
     experts = owners * local_count
     padded = qkv_ref.shape[0]
     blocks = slots // TILE
+    offsets = group_offsets(owners)
+    near = [group_partner(owners, *offset)[0] for offset in offsets if any(offset)]
+    if reduce:
+        near = near + [line_partner(1, 1)[0], line_partner(1, 0)[0]]
+    greet(near)
+    line_rows = zsum.shape[0]
+    line_sums = []
+    later = []
+    if reduce:
+        zero = lax.axis_index("p0")
+        for index, offset in enumerate(OTHERS):
+            device, place = line_partner(*offset)
+            source = part_ref.at[pl.ds(place * line_rows, line_rows)]
+            line_sums.append(
+                push(source, zgot.at[index], zsends.at[index], zrecvs.at[index], device)
+            )
+    _, me = group_partner(owners, 0, 0, 0)
+    own = pltpu.make_async_copy(res_ref.at[me], res.at[me], own_sem)
+    own.start()
+    copies = [
+        group_copy(owners, index, offset, res_ref, res, send_sems, recv_sems)
+        for index, offset in enumerate(offsets)
+        if any(offset)
+    ]
+    for copy in copies:
+        copy.start()
+    if reduce:
+        eup_rows = eup_ref.shape[0]
+        later.append(
+            push(
+                eup_any.at[pl.ds((1 - zero) * eup_rows, eup_rows)],
+                eup_ref,
+                zsends.at[6],
+                zrecvs.at[6],
+                line_partner(1, 0)[0],
+            )
+        )
+        half_rows = next_ref.shape[0]
+        for index, offset in enumerate(OTHERS):
+            device, net, half = plane_partner(*offset)
+            source = later_ref.at[net, pl.ds(half * half_rows, half_rows)]
+            later.append(
+                push(source, pieces.at[index], zsends.at[7 + index], zrecvs.at[7 + index], device)
+            )
     bounds = image_bounds(counts_ref)
     total = bounds[-1][1]
     scale = HDIM ** (-0.5)
@@ -812,6 +980,22 @@
         return carry
 
     lax.fori_loop(0, blocks, routing, 0)
+    line_all = []
+    if reduce:
+        finish_all(line_sums)
+        _, place = line_partner(0, 0)
+        here = pl.ds(pl.multiple_of(place * line_rows, 16), line_rows)
+        summed = part_ref[here].astype(F32)
+        for index in range(len(OTHERS)):
+            summed = summed + zgot[index].astype(F32)
+        zsum[...] = summed.astype(BF16)
+        quarter_ref[here] = zsum[...]
+        target = quarter_ref.at[pl.ds(place * line_rows, line_rows)]
+        for index, offset in enumerate(OTHERS):
+            device, _ = line_partner(*offset)
+            line_all.append(
+                push(zsum, target, zsends.at[3 + index], zrecvs.at[3 + index], device)
+            )
     drouter_ref[...] = dot(dlog[...], moe_ref[...])[:experts]
     dout_w_ref[...] = dot(turned[...], dqkv[:, :width])
     dout_b_ref[...] = jnp.sum(dqkv[:, :width].astype(F32), axis=0, keepdims=True)
@@ -881,10 +1065,15 @@
     lax.fori_loop(0, blocks, finish, 0)
     dqkv_w_ref[...] = dot(turned[...], dqkv[...])
 
+    own.wait()
+    finish_all(copies)
+    for j in range(experts):
+        rows_ext[j * CAP : (j + 1) * CAP, :width] = res[j]
+
     def result(i, carry):
         r = pl.ds(pl.multiple_of(i * TILE, TILE), TILE)
         member = member_block(bounds, i * TILE, TILE)
-        branch = dot(hot[r, :], res_ref[...]) + shared_ref[r, :]
+        branch = dot(hot[r, :], rows_ext[:, :width]) + shared_ref[r, :]
         layer = hidden_ref[r, :] + part(member, 5) * branch
         layer_ref[r, :] = layer.astype(BF16)
         valid = (i * TILE + iota((TILE, width), 0)) < total
@@ -912,28 +1101,42 @@
     for image in range(len(bounds)):
         label = jnp.where(row == image, labels_ref[0, image], label)
     time = jnp.full((8, 128), time_ref[0], jnp.int32)
-    pieces = [label // 32, label % 32, time // 32, time % 32]
+    digits = [label // 32, label % 32, time // 32, time % 32]
     marks = jnp.zeros((8, 128), jnp.int32)
-    for index, piece in enumerate(pieces):
+    for index, piece in enumerate(digits):
         marks = jnp.where(lane == index, piece, marks)
     real = row < len(bounds)
     marks = jnp.where(real, marks, jnp.where(lane < 4, 255, 0)).astype(F32)
     keep = (iota((8, width), 0) < len(bounds)).astype(F32)
-    note = jnp.concatenate(
-        [grad_mod, grad_cond * keep, act_ref[...].astype(F32) * keep, marks], axis=1
-    )
-    note_ref[...] = jnp.concatenate([note, jnp.zeros_like(note)], axis=0).astype(BF16)
-
-
-def backward(owners, *args):
-    tokens, mod, qkv_pad, gates = args[3], args[5], args[8], args[13]
+    note = jnp.concatenate([grad_mod, grad_cond * keep, marks], axis=1)
+    middle = note.shape[1] // 2
+    note_ref[...] = jnp.concatenate([note[:, :middle], note[:, middle:]], axis=0).astype(BF16)
+    finish_all(line_all)
+    finish_all(later)
+    if reduce:
+        _, net, half = plane_partner(0, 0)
+        own_rows = pl.ds(pl.multiple_of(half * half_rows, 64), half_rows)
+        summed = later_ref[net, own_rows].astype(F32)
+        for index in range(len(OTHERS)):
+            summed = summed + pieces[index].astype(F32)
+        next_ref[...] = summed.astype(BF16)
+
+
+def backward(owners, reduce, *args):
+    tokens, mod, qkv_pad, gates, res, part = (args[k] for k in (3, 5, 7, 12, 17, 23))
     slots, width = tokens.shape
     padded = qkv_pad.shape[0]
     experts = gates.shape[0]
+    quarter = part.shape
+    sub = (quarter[0] // 4, quarter[1]) if reduce else (16, 128)
+    in_specs = [in_smem()] * 3 + [in_vmem()] * (len(args) - 3)
+    in_specs[17] = anywhere()
+    in_specs[25] = anywhere()
+    eup = (args[25].shape[0] // 2, args[25].shape[1]) if reduce else (16, 128)
     return pl.pallas_call(
-        functools.partial(backward_kernel, owners, experts // owners),
-        in_specs=[in_smem()] * 3 + [in_vmem()] * (len(args) - 3),
-        out_specs=[in_vmem()] * 8,
+        functools.partial(backward_kernel, owners, experts // owners, reduce),
+        in_specs=in_specs,
+        out_specs=[in_vmem()] * 11,
         out_shape=[
             like((slots, width), BF16),
             like((slots, width), F32),
@@ -942,7 +1145,10 @@
             like((width, width), F32),
             like((1, width), F32),
             like((experts, width), F32),
-            like((16, 8 * width + 128), BF16),
+            like((16, (7 * width + 128) // 2), BF16),
+            like(quarter, BF16),
+            like(quarter, BF16),
+            like(eup, BF16),
         ],
         scratch_shapes=[
             pltpu.VMEM((128, 6 * width), BF16),
@@ -961,10 +1167,449 @@
             pltpu.VMEM((128, 256), F32),
             pltpu.VMEM((256, 128), F32),
             pltpu.VMEM((128, width), BF16),
+            pltpu.VMEM((experts, CAP, width), BF16),
+            pltpu.SemaphoreType.DMA((experts,)),
+            pltpu.SemaphoreType.DMA((experts,)),
+            pltpu.SemaphoreType.DMA,
+            pltpu.VMEM((3,) + sub, BF16),
+            pltpu.VMEM(sub, BF16),
+            pltpu.VMEM((3,) + quarter, BF16),
+            pltpu.SemaphoreType.DMA((10,)),
+            pltpu.SemaphoreType.DMA((10,)),
         ],
-        compiler_params=pltpu.CompilerParams(vmem_limit_bytes=VMEM_BYTES),
+        compiler_params=pltpu.CompilerParams(
+            vmem_limit_bytes=VMEM_BYTES, collective_id=3, has_side_effects=True
+        ),
         name="backward",
     )(*args)
+
+
+def tail_kernel(
+    dqkv_w_ref,
+    dout_w_ref,
+    drouter_ref,
+    dout_b_ref,
+    sup_b_ref,
+    sdn_b_ref,
+    quarter_ref,
+    part_ref,
+    note_ref,
+    side_ref,
+    eup_got_ref,
+    eup_any,
+    edn_any,
+    full_a,
+    full_b,
+    done,
+    notes,
+    up_got,
+    dn_got,
+    sides,
+    load,
+    keep,
+    got,
+    pieces,
+    zslots,
+    zgot,
+    zsum,
+    quarter_b,
+    up_sum,
+    up_mine,
+    dn_sum,
+    dn_mine,
+    side,
+    sends,
+    recvs,
+    locals_,
+):
+    zero, one, two, three = axes_here()
+    odd = lax.rem(three, 2)
+    width = dout_w_ref.shape[0]
+    rows, hidden = load.shape[1], 2 * load.shape[2]
+    lanes = hidden // 2
+    quarter_rows = rows // 2
+    quarter_lanes = lanes // 2
+    _, _, half_here = plane_partner(0, 0)
+    _, line_here = line_partner(0, 0)
+    _, owner_here = owner_partner(0, 0)
+    _, column_here = column_partner(0, 0, 0)
+    counter = iter(range(sends.shape[0]))
+
+    def give(source, target, device):
+        index = next(counter)
+        return push(source, target, sends.at[index], recvs.at[index], device)
+
+    up_rows = up_sum.shape[0]
+    dn_rows = dn_sum.shape[0]
+    half_rows = quarter_ref.shape[0]
+    shared_rows = pl.ds(half_here * half_rows, half_rows)
+    loads = [
+        pltpu.make_async_copy(eup_any.at[pl.ds(zero * up_rows, up_rows)], up_mine, locals_.at[0]),
+        pltpu.make_async_copy(edn_any.at[pl.ds(zero * dn_rows, dn_rows)], dn_mine, locals_.at[1]),
+        pltpu.make_async_copy(quarter_ref, full_a.at[odd, two, shared_rows], locals_.at[2]),
+    ]
+    for copy in loads:
+        copy.start()
+
+    top = jnp.concatenate([dqkv_w_ref[...], dout_w_ref[...]], axis=1).astype(BF16)
+    router = drouter_ref[...]
+    router = jnp.concatenate(
+        [router, jnp.zeros((router.shape[0], hidden - width), F32)], axis=1
+    )
+    vectors = jnp.concatenate(
+        [dout_b_ref[...], sdn_b_ref[...], jnp.zeros((1, hidden - 2 * width), F32)], axis=1
+    )
+    nets = sup_b_ref.shape[0]
+    filler = jnp.zeros((rows - width - router.shape[0] - nets - 1, hidden), F32)
+    bottom = jnp.concatenate(
+        [router] + [sup_b_ref[n] for n in range(nets)] + [vectors, filler], axis=0
+    ).astype(BF16)
+    for part in range(2):
+        load[part, :width] = top[:, part * lanes : (part + 1) * lanes]
+        load[part, width:] = bottom[:, part * lanes : (part + 1) * lanes]
+    side[...] = jnp.concatenate([side_ref[...], jnp.zeros_like(side_ref)], axis=0).astype(BF16)
+
+    greet(
+        [column_partner(*offset)[0] for offset in COLUMN]
+        + [sibling(), plane_partner(0, 1)[0], plane_partner(1, 1)[0]]
+    )
+    swap = give(load.at[1 - odd], got, sibling())
+    note_line = [
+        give(note_ref, notes.at[odd, two, half_here, line_here], line_partner(*o)[0]) for o in OTHERS
+    ]
+    notes[odd, two, half_here, line_here] = note_ref[...]
+    line_rows = zsum.shape[0]
+    shared_line = []
+    for index, offset in enumerate(OTHERS):
+        device, place = line_partner(*offset)
+        source = part_ref.at[pl.ds(place * line_rows, line_rows)]
+        shared_line.append(give(source, zgot.at[index], device))
+
+    swap.wait()
+    keep[...] = (load[odd].astype(F32) + got[...].astype(F32)).astype(BF16)
+    plane_sums = []
+    for index, offset in enumerate(OTHERS):
+        device, second, half = plane_partner(*offset)
+        source = keep.at[
+            pl.ds(second * quarter_rows, quarter_rows),
+            pl.ds(pl.multiple_of(half * quarter_lanes, 128), quarter_lanes),
+        ]
+        plane_sums.append(give(source, pieces.at[index], device))
+
+    finish_all(shared_line)
+    here = pl.ds(pl.multiple_of(line_here * line_rows, 16), line_rows)
+    total = part_ref[here].astype(F32)
+    for index in range(len(OTHERS)):
+        total = total + zgot[index].astype(F32)
+    zsum[...] = total.astype(BF16)
+    quarter_b[here] = zsum[...]
+    shared_all = [
+        give(zsum, quarter_b.at[pl.ds(line_here * line_rows, line_rows)], line_partner(*o)[0])
+        for o in OTHERS
+    ]
+    finish_all(note_line)
+    note_plane = [
+        give(
+            notes.at[odd, two, half_here],
+            notes.at[odd, two, half_here],
+            plane_partner(*o)[0],
+        )
+        for o in OTHERS
+    ]
+
+    down_swap = give(
+        edn_any.at[pl.ds((1 - zero) * dn_rows, dn_rows)], dn_sum, line_partner(1, 0)[0]
+    )
+    side_all = [give(side, sides.at[column_here], column_partner(*o)[0]) for o in COLUMN]
+    sides[column_here] = side[...]
+    loads[0].wait()
+    step = 64
+    for r in range(0, up_rows, step):
+        s = slice(r, r + step)
+        up_sum[s] = (up_mine[s].astype(F32) + eup_got_ref[s].astype(F32)).astype(BF16)
+    up_part = up_rows // 4
+    dn_part = dn_rows // 4
+    spread_rows = []
+    for offset in OTHERS:
+        device, place = owner_partner(*offset)
+        spread_rows.append(
+            give(up_sum.at[pl.ds(place * up_part, up_part)], up_got.at[owner_here], device)
+        )
+    up_got[owner_here] = up_sum[pl.ds(pl.multiple_of(owner_here * up_part, 16), up_part)]
+
+    finish_all(plane_sums)
+    shared_a = full_a.at[odd, two, shared_rows]
+    plane_a = [give(quarter_ref, shared_a, plane_partner(*o)[0]) for o in OTHERS]
+    here_rows = pl.ds(pl.multiple_of(two * quarter_rows, 16), quarter_rows)
+    here_lanes = pl.ds(pl.multiple_of(half_here * quarter_lanes, 128), quarter_lanes)
+    total = keep[here_rows, here_lanes].astype(F32)
+    for index in range(len(OTHERS)):
+        total = total + pieces[index].astype(F32)
+    zslots[line_here] = total.astype(BF16)
+    line_sums = [
+        give(zslots.at[line_here], zslots.at[line_here], line_partner(*o)[0]) for o in OTHERS
+    ]
+    finish_all(note_plane)
+    note_swap = give(notes.at[odd], notes.at[odd], sibling())
+
+    finish_all(shared_all)
+    shared_b = full_b.at[odd, two, shared_rows]
+    own_b = pltpu.make_async_copy(quarter_b, shared_b, locals_.at[3])
+    own_b.start()
+
+    finish_all(line_sums)
+    total = zslots[0].astype(F32)
+    for index in range(1, 4):
+        total = total + zslots[index].astype(F32)
+    done[odd, here_rows, here_lanes] = total.astype(BF16)
+    place = done.at[
+        odd,
+        pl.ds(two * quarter_rows, quarter_rows),
+        pl.ds(pl.multiple_of(half_here * quarter_lanes, 128), quarter_lanes),
+    ]
+    plane_all = [give(place, place, plane_partner(*o)[0]) for o in OTHERS]
+    plane_b = [give(quarter_b, shared_b, plane_partner(*o)[0]) for o in OTHERS]
+
+    down_swap.wait()
+    loads[1].wait()
+    for r in range(0, dn_rows, step):
+        s = slice(r, r + step)
+        dn_sum[s] = (dn_mine[s].astype(F32) + dn_sum[s].astype(F32)).astype(BF16)
+    for offset in OTHERS:
+        device, place = owner_partner(*offset)
+        spread_rows.append(
+            give(dn_sum.at[pl.ds(place * dn_part, dn_part)], dn_got.at[owner_here], device)
+        )
+    dn_got[owner_here] = dn_sum[pl.ds(pl.multiple_of(owner_here * dn_part, 16), dn_part)]
+
+    loads[2].wait()
+    finish_all(plane_a)
+    last = [give(full_a.at[odd], full_a.at[odd], sibling())]
+    finish_all(plane_all)
+    last.append(give(done.at[odd], done.at[odd], sibling()))
+    own_b.wait()
+    finish_all(plane_b)
+    last.append(give(full_b.at[odd], full_b.at[odd], sibling()))
+    note_swap.wait()
+    finish_all(side_all)
+    finish_all(spread_rows)
+    finish_all(last)
+
+
+def tail(*args):
+    dqkv_w, quarter, note, edown = args[0], args[6], args[8], args[12]
+    width = dqkv_w.shape[0]
+    hidden = edown.shape[0]
+    nets = args[4].shape[0]
+    rows = width + 32
+    lanes = hidden // 2
+    half_rows = quarter.shape[0]
+    full = like((2, nets, 2 * half_rows, lanes), BF16)
+    return pl.pallas_call(
+        tail_kernel,
+        in_specs=[in_vmem()] * 11 + [anywhere()] * 2,
+        out_specs=[anywhere()] * 2 + [in_vmem()] * 5,
+        out_shape=[
+            full,
+            full,
+            like((2, rows, lanes), BF16),
+            like((2, 2, 2, 4) + note.shape, BF16),
+            like((4, width // 8, hidden), BF16),
+            like((4, hidden // 8, width), BF16),
+            like((8, 16, hidden), BF16),
+        ],
+        scratch_shapes=[
+            pltpu.VMEM((2, rows, lanes), BF16),
+            pltpu.VMEM((rows, lanes), BF16),
+            pltpu.VMEM((rows, lanes), BF16),
+            pltpu.VMEM((3, rows // 2, lanes // 2), BF16),
+            pltpu.VMEM((4, rows // 2, lanes // 2), BF16),
+            pltpu.VMEM((3, half_rows // 4, lanes), BF16),
+            pltpu.VMEM((half_rows // 4, lanes), BF16),
+            pltpu.VMEM((half_rows, lanes), BF16),
+            pltpu.VMEM((width // 2, hidden), BF16),
+            pltpu.VMEM((width // 2, hidden), BF16),
+            pltpu.VMEM((hidden // 2, width), BF16),
+            pltpu.VMEM((hidden // 2, width), BF16),
+            pltpu.VMEM((16, hidden), BF16),
+            pltpu.SemaphoreType.DMA((48,)),
+            pltpu.SemaphoreType.DMA((48,)),
+            pltpu.SemaphoreType.DMA((4,)),
+        ],
+        compiler_params=pltpu.CompilerParams(
+            vmem_limit_bytes=VMEM_BYTES, collective_id=4, has_side_effects=True
+        ),
+        name="tail",
+    )(*args)
+
+
+def finish_kernel(
+    nets,
+    dp_count,
+    full_a_any,
+    full_b_any,
+    done_ref,
+    notes_ref,
+    up_ref,
+    dn_ref,
+    sides_ref,
+    time_table_ref,
+    label_table_ref,
+    time_any,
+    label_any,
+    ada_any,
+    ada_b_ref,
+    qkv_any,
+    out_any,
+    out_b_ref,
+    router_ref,
+    eup_any,
+    eup_b_ref,
+    edn_any,
+    edn_b_ref,
+    sup_any,
+    sup_b_ref,
+    sdn_any,
+    sdn_b_ref,
+    full_a,
+    full_b,
+    time_out,
+    label_out,
+    ada_out,
+    qkv_out,
+    weight_out,
+    eup_out,
+    edn_out,
+    sup_out,
+    sdn_out,
+    in_sems,
+    out_sems,
+):
+    width = out_any.shape[0]
+    lanes = done_ref.shape[2]
+    experts = router_ref.shape[1]
+    ins = [
+        pltpu.make_async_copy(full_a_any, full_a, in_sems.at[0]),
+        pltpu.make_async_copy(full_b_any, full_b, in_sems.at[1]),
+    ]
+    for copy in ins:
+        copy.start()
+    outs = []
+
+    def write(source, target):
+        copy = pltpu.make_async_copy(source, target, out_sems.at[len(outs)])
+        copy.start()
+        outs.append(copy)
+
+    eup_out[...] = up_ref[...].astype(F32)
+    write(eup_out, eup_any)
+    edn_out[...] = dn_ref[...].astype(F32)
+    write(edn_out, edn_any)
+    rest = qkv_any.shape[1] - lanes
+    qkv_out[:, :lanes] = done_ref[0, :width].astype(F32)
+    qkv_out[:, lanes:] = done_ref[1, :width, :rest].astype(F32)
+    write(qkv_out, qkv_any)
+    weight_out[...] = done_ref[1, :width, rest:].astype(F32)
+    write(weight_out, out_any)
+
+    for index, half in enumerate((full_a, full_b)):
+        ins[index].wait()
+        for net in range(nets):
+            first = index * lanes
+            sup_out[net, :, first : first + lanes] = half[0, net].astype(F32)
+            sdn_out[net, first : first + lanes, :] = half[1, net].astype(F32).T
+            write(
+                sdn_out.at[net, pl.ds(first, lanes)], sdn_any.at[net, pl.ds(first, lanes)]
+            )
+    write(sup_out, sup_any)
+
+    notes = notes_ref[...].reshape(-1, notes_ref.shape[4], notes_ref.shape[5])
+    high = notes[:, 0:8, :].reshape(-1, notes.shape[2])
+    low = notes[:, 8:16, :].reshape(-1, notes.shape[2])
+    rows = jnp.concatenate([high, low], axis=1)
+    count = rows.shape[0]
+    grad_mod = rows[:, : 6 * width]
+    grad_cond = rows[:, 6 * width : 7 * width]
+    marks = rows[:, 7 * width :].astype(F32)
+    label = marks[:, 0:1] * 32.0 + marks[:, 1:2]
+    time = marks[:, 2:3] * 32.0 + marks[:, 3:4]
+
+    def table(marked, out_ref):
+        line = jnp.broadcast_to(marked, (count, 128)).T[0:1, :]
+        tall = (iota((out_ref.shape[0], count), 0).astype(F32) == line).astype(F32).astype(BF16)
+        out_ref[...] = dot(tall, grad_cond)
+
+    table(label, label_out)
+    write(label_out, label_any)
+    table(time, time_out)
+    write(time_out, time_any)
+    label_hot = (iota((count, label_table_ref.shape[0]), 1).astype(F32) == label).astype(F32)
+    time_hot = (iota((count, time_table_ref.shape[0]), 1).astype(F32) == time).astype(F32)
+    condition = dot(label_hot.astype(BF16), label_table_ref[...])
+    condition = condition + dot(time_hot.astype(BF16), time_table_ref[...])
+    act = condition / (1.0 + jnp.exp(-condition))
+    ada_out[...] = dot(act.T.astype(BF16), grad_mod)
+    write(ada_out, ada_any)
+    ada_b_ref[...] = jnp.sum(grad_mod.astype(F32), axis=0, keepdims=True)
+
+    rest_a = done_ref[0, width:].astype(F32)
+    rest_b = done_ref[1, width:].astype(F32)
+    router = jnp.concatenate(
+        [rest_a[:experts, :width], jnp.zeros((128 - experts, width), F32)], axis=0
+    )
+    router_ref[...] = router.T[:, :experts]
+    sup_b_ref[:, :lanes] = rest_a[experts : experts + nets]
+    sup_b_ref[:, lanes:] = rest_b[experts : experts + nets]
+    last = rest_a[experts + nets : experts + nets + 1]
+    out_b_ref[...] = last[:, :width]
+    sdn_b_ref[...] = jnp.broadcast_to(last[:, width:], sdn_b_ref.shape)
+    place = lax.axis_index(("p0", "p1", "p2"))
+    for index in range(4):
+        total = sides_ref[index, 0:8].astype(F32) + sides_ref[4 + index, 0:8].astype(F32)
+        size = total.shape[1]
+        up_rows = eup_b_ref.shape[1]
+        dn_rows = edn_b_ref.shape[1]
+        turned = pltpu.roll(total, size - place * up_rows, 1)
+        eup_b_ref[index : index + 1, :] = turned[0:1, :up_rows]
+        turned = pltpu.roll(total, size - place * dn_rows, 1)
+        edn_b_ref[index : index + 1, :] = turned[1:2, :dn_rows]
+    finish_all(outs)
+
+
+def finish(gathered, time_table, label_table, experts, width, hidden, nets, dp_count):
+    time_shape = time_table.shape
+    label_shape = label_table.shape
+    shapes = [
+        time_shape,
+        label_shape,
+        (width, 6 * width),
+        (1, 6 * width),
+        (width, 3 * width),
+        (width, width),
+        (1, width),
+        (width, experts),
+        (4, width // 8, hidden),
+        (4, hidden // dp_count),
+        (4, hidden // 8, width),
+        (4, width // dp_count),
+        (nets, width, hidden),
+        (nets, hidden),
+        (nets, hidden, width),
+        (nets, width),
+    ]
+    large = (0, 1, 2, 4, 5, 8, 10, 12, 14)
+    specs = [anywhere() if index in large else in_vmem() for index in range(len(shapes))]
+    return pl.pallas_call(
+        functools.partial(finish_kernel, nets, dp_count),
+        in_specs=[anywhere()] * 2 + [in_vmem()] * 7,
+        out_specs=specs,
+        out_shape=[like(shape, F32) for shape in shapes],
+        scratch_shapes=[pltpu.VMEM(gathered[0].shape, BF16), pltpu.VMEM(gathered[1].shape, BF16)]
+        + [pltpu.VMEM(shapes[index], F32) for index in large]
+        + [pltpu.SemaphoreType.DMA((2,)), pltpu.SemaphoreType.DMA((16,))],
+        compiler_params=pltpu.CompilerParams(vmem_limit_bytes=VMEM_BYTES),
+        name="finish",
+    )(*gathered, time_table, label_table)
 
 
 def exchange(blocks, axes):
@@ -1022,9 +1667,13 @@
     slot_count, width = tokens.shape
     expert_count = router_weight.shape[1]
     local_count, _, hidden = expert_up.shape
+    nets = shared_up.shape[0]
     owners = lax.axis_size("expert")
+    outer = lax.axis_size("p0")
     dp_count = lax.axis_size(("p0", "p1", "p2"))
-    outer = lax.axis_size("p0")
+    dp_here = lax.axis_index(("p0", "p1", "p2"))
+    small = outer == 2 and owners == 4
+
     routes = expert_routes[0].T
     router_turned = router_weight.T
     modulation, condition, cond_act, place, targets, grad_branch, branch_rows = front(
@@ -1041,7 +1690,7 @@
         expert_count,
     )
     owner_branch = exchange(branch_rows, GROUP)
-    qkv_pad, attended_flat, log_totals, hidden_one, moe_in, gates_t, send_rows = attention(
+    qkv_pad, attended, log_totals, hidden_one, moe_in, gates, send_rows = attention(
         owners,
         patch_counts,
         tokens,
@@ -1053,15 +1702,7 @@
         routes,
         place,
     )
-    (
-        shared_total,
-        grad_moe_in,
-        grad_sup,
-        grad_sup_bias,
-        grad_sdown,
-        grad_sdown_bias,
-        owner_rows,
-    ) = shared_nets(
+    shared_total, grad_moe_in, wire, grad_sup_bias, grad_sdown_bias, owner_rows = shared_nets(
         owners,
         moe_in,
         grad_branch,
@@ -1071,40 +1712,17 @@
         shared_down_bias,
         send_rows,
     )
-    shared_payload = jnp.concatenate(
-        [grad_sup.reshape(-1, hidden), grad_sdown.reshape(-1, hidden)], axis=0
-    )
-    shared_sums = sum_everywhere(shared_payload).astype(F32)
-    owner_res, grad_eup, grad_eup_bias, grad_edown, grad_edown_bias, returned_grads = routed_net(
+    owner_res, grad_eup, grad_edown, side, returned_grads, part, later = routed_net(
         owners,
+        small,
         owner_rows,
         owner_branch,
         expert_up,
         expert_up_bias,
         expert_down,
         expert_down_bias,
+        wire,
     )
-    returned = exchange(owner_res, GROUP).reshape(expert_count * CAP, width)
-
-    up_blocks = exchange(grad_eup.reshape(outer, width // outer, hidden), "p0")
-    up_part = sum_blocks(up_blocks).astype(BF16).reshape(-1, width // dp_count, hidden)
-    sum_eup = exchange(up_part, ("p1", "p2")).astype(F32)
-    side = jnp.concatenate(
-        [grad_eup_bias.reshape(dp_count, -1), grad_edown_bias.reshape(dp_count, -1)], axis=1
-    )
-    side_width = side.shape[1]
-    side = jnp.pad(side.astype(BF16)[:, None, :], ((0, 0), (0, PAD - 1), (0, width - side_width)))
-    down_payload = jnp.concatenate(
-        [grad_edown.reshape(dp_count, hidden // dp_count, width), side], axis=1
-    )
-    down_rows = down_payload.shape[1]
-    down_blocks = exchange(down_payload.reshape(outer, -1, down_rows, width), "p0")
-    down_part = exchange(sum_blocks(down_blocks).astype(BF16), ("p1", "p2")).astype(F32)
-    sum_edown = down_part[:, : hidden // dp_count]
-    side_sums = down_part[:, hidden // dp_count]
-    sum_eup_bias = side_sums[:, : hidden // dp_count]
-    sum_edown_bias = side_sums[:, hidden // dp_count : side_width]
-
     (
         layer_out,
         grad_tokens,
@@ -1114,8 +1732,12 @@
         grad_out_bias,
         grad_router,
         note,
+        quarter,
+        part_next,
+        eup_got,
     ) = backward(
         owners,
+        small,
         patch_counts,
         image_labels,
         time_buckets,
@@ -1123,69 +1745,130 @@
         cotangent,
         modulation,
         condition,
-        cond_act,
         qkv_pad,
-        attended_flat,
+        attended,
         log_totals,
         hidden_one,
         moe_in,
-        gates_t,
+        gates,
         targets,
         shared_total,
         grad_moe_in,
         returned_grads,
-        returned,
+        owner_res,
         qkv_weight,
         out_weight,
         out_bias[None],
         router_turned,
         ada_weight,
+        part,
+        later,
+        grad_eup,
     )
-
-    all_rows = spread(note[:8], ALL).reshape(-1, note.shape[1])
-    all_modulation = all_rows[:, : 6 * width]
-    all_condition = all_rows[:, 6 * width : 7 * width]
-    all_cond_act = all_rows[:, 7 * width : 8 * width]
-    marks = all_rows[:, 8 * width : 8 * width + 4].astype(jnp.int32)
-    sum_ada = lax.dot_general(all_cond_act, all_modulation, ROWS_FIRST, preferred_element_type=F32)
-    sum_ada_bias = jnp.sum(all_modulation.astype(F32), axis=0)
-    label_ids = jnp.arange(label_table.shape[0], dtype=jnp.int32)
-    label_hot = ((marks[:, 0:1] * 32 + marks[:, 1:2]) == label_ids).astype(BF16)
-    sum_label = lax.dot_general(label_hot, all_condition, ROWS_FIRST, preferred_element_type=F32)
-    time_ids = jnp.arange(time_table.shape[0], dtype=jnp.int32)
-    time_hot = ((marks[:, 2:3] * 32 + marks[:, 3:4]) == time_ids).astype(BF16)
-    sum_time = lax.dot_general(time_hot, all_condition, ROWS_FIRST, preferred_element_type=F32)
-
-    tail = jnp.concatenate(
-        [
-            jnp.concatenate([grad_qkv_weight, grad_out_weight], axis=1),
-            grad_router.reshape(-1, hidden),
-            grad_sup_bias.reshape(-1, hidden),
-            jnp.pad(
-                jnp.concatenate([grad_out_bias, grad_sdown_bias], axis=1),
-                ((0, 0), (0, hidden - 2 * width)),
-            ),
-        ],
-        axis=0,
-    )
-    used = tail.shape[0]
-    near_count = lax.axis_size(("p2", "expert"))
-    tail = jnp.pad(tail, ((0, -used % (16 * near_count)), (0, 0)))
-    tail = sum_everywhere(tail).astype(F32)
-    router_rows = width * expert_count // hidden
-    shared_count = shared_up.shape[0]
-    sum_qkv = tail[:width, : 3 * width]
-    sum_out_weight = tail[:width, 3 * width :]
-    place = width + router_rows
-    sum_router = tail[width:place].reshape(expert_count, width).T
-    sum_sup_bias = tail[place : place + shared_count]
-    sum_out_bias = tail[place + shared_count, :width]
-    sum_sdown_bias = jnp.broadcast_to(
-        tail[place + shared_count, width : 2 * width][None], (shared_count, width)
-    )
-    half = grad_sup.size // hidden
-    sum_sup = shared_sums[:half].reshape(grad_sup.shape)
-    sum_sdown = shared_sums[half:].reshape(grad_sdown.shape)
+    if small:
+        gathered = tail(
+            grad_qkv_weight,
+            grad_out_weight,
+            grad_router,
+            grad_out_bias,
+            grad_sup_bias,
+            grad_sdown_bias,
+            quarter,
+            part_next,
+            note,
+            side,
+            eup_got,
+            grad_eup,
+            grad_edown,
+        )
+        (
+            sum_time,
+            sum_label,
+            sum_ada,
+            sum_ada_bias,
+            sum_qkv,
+            sum_out_weight,
+            sum_out_bias,
+            sum_router,
+            sum_eup,
+            sum_eup_bias,
+            sum_edown,
+            sum_edown_bias,
+            sum_sup,
+            sum_sup_bias,
+            sum_sdown,
+            sum_sdown_bias,
+        ) = finish(
+            gathered, time_table, label_table, expert_count, width, hidden, nets, dp_count
+        )
+        sum_ada_bias = sum_ada_bias[0]
+        sum_out_bias = sum_out_bias[0]
+    else:
+        up_blocks = exchange(grad_eup.reshape(outer, width // outer, hidden), "p0")
+        up_part = sum_blocks(up_blocks).astype(BF16).reshape(-1, width // dp_count, hidden)
+        sum_eup = exchange(up_part, ("p1", "p2")).astype(F32)
+        down_blocks = exchange(grad_edown.reshape(outer, hidden // outer, width), "p0")
+        down_part = sum_blocks(down_blocks).astype(BF16).reshape(-1, hidden // dp_count, width)
+        sum_edown = exchange(down_part, ("p1", "p2")).astype(F32)
+        sides = lax.psum(side, "p0")
+        sides = spread(sides, ("p1", "p2"))
+        side_up = sides[:, 0]
+        side_down = sides[:, 1, :width]
+
+        shared_sums = sum_everywhere(wire.reshape(-1, hidden)).astype(F32).reshape(wire.shape)
+        sum_sup = shared_sums[0]
+        sum_sdown = shared_sums[1].transpose(0, 2, 1)
+
+        all_rows = spread(jnp.concatenate([note[:8], note[8:]], axis=1), ALL)
+        all_rows = all_rows.reshape(-1, 2 * note.shape[1])
+        all_modulation = all_rows[:, : 6 * width]
+        all_condition = all_rows[:, 6 * width : 7 * width]
+        marks = all_rows[:, 7 * width : 7 * width + 4].astype(jnp.int32)
+        label_ids = jnp.arange(label_table.shape[0], dtype=jnp.int32)
+        label_hot = ((marks[:, 0:1] * 32 + marks[:, 1:2]) == label_ids).astype(BF16)
+        time_ids = jnp.arange(time_table.shape[0], dtype=jnp.int32)
+        time_hot = ((marks[:, 2:3] * 32 + marks[:, 3:4]) == time_ids).astype(BF16)
+        all_act = jax.nn.silu(
+            jnp.dot(label_hot, label_table, preferred_element_type=F32)
+            + jnp.dot(time_hot, time_table, preferred_element_type=F32)
+        ).astype(BF16)
+        sum_ada = lax.dot_general(all_act, all_modulation, ROWS_FIRST, preferred_element_type=F32)
+        sum_ada_bias = jnp.sum(all_modulation.astype(F32), axis=0)
+        sum_label = lax.dot_general(
+            label_hot, all_condition, ROWS_FIRST, preferred_element_type=F32
+        )
+        sum_time = lax.dot_general(time_hot, all_condition, ROWS_FIRST, preferred_element_type=F32)
+
+        last = jnp.concatenate(
+            [
+                jnp.concatenate([grad_qkv_weight, grad_out_weight], axis=1),
+                jnp.pad(grad_router, ((0, 0), (0, hidden - width))),
+                grad_sup_bias.reshape(nets, hidden),
+                jnp.pad(
+                    jnp.concatenate([grad_out_bias, grad_sdown_bias], axis=1),
+                    ((0, 0), (0, hidden - 2 * width)),
+                ),
+            ],
+            axis=0,
+        )
+        near_count = lax.axis_size(("p2", "expert"))
+        last = jnp.pad(last, ((0, -last.shape[0] % (16 * near_count)), (0, 0)))
+        last = sum_everywhere(last).astype(F32)
+        sum_qkv = last[:width, : 3 * width]
+        sum_out_weight = last[:width, 3 * width :]
+        rest = last[width:]
+        sum_eup_bias = lax.dynamic_slice_in_dim(
+            side_up, dp_here * (hidden // dp_count), hidden // dp_count, 1
+        )
+        sum_edown_bias = lax.dynamic_slice_in_dim(
+            side_down, dp_here * (width // dp_count), width // dp_count, 1
+        )
+        sum_router = rest[:expert_count, :width].T
+        sum_sup_bias = rest[expert_count : expert_count + nets]
+        sum_out_bias = rest[expert_count + nets, :width]
+        sum_sdown_bias = jnp.broadcast_to(
+            rest[expert_count + nets, width : 2 * width][None], (nets, width)
+        )
     return (
         layer_out,
         grad_tokens,

time: 564 us -> 333 us (0.59); the launches traced: 555 us -> 331 us
  waiting for transfers between devices: 216 us -> 0.01 us
  Pallas kernels: 190 us -> 311 us
  starting transfers between devices: 59.1 us -> 6.43 us
  local copies, waits for them, and re-layouts: 39.6 us -> 9.77 us
  other arithmetic: 23 us -> 2.72 us
  blocking collectives: 19.4 us -> 0 us
  matrix products: 5.84 us -> 0 us
    all_to_all x14 -> x1, waiting for transfers between devices: 216 us -> 0.01 us  [exchange(): return lax.all_to_all(blocks, axes, split_axis=0, concat_axis=0, tiled=True)]
    pallas_call x1 -> x3, Pallas kernels: 80 us -> 172 us  [the longest x1 102 us: tail(): pl.pallas_call(tail_kernel, in_specs=[in_vmem()] * 11 + [anywhere()] * 2,...]
    all_to_all x14 -> x1, starting transfers between devices: 59.1 us -> 6.43 us  [exchange(): return lax.all_to_all(blocks, axes, split_axis=0, concat_axis=0, tiled=True)]
    all_to_all x1 -> x0, blocking collectives: 19.4 us -> none  [exchange(): return lax.all_to_all(blocks, axes, split_axis=0, concat_axis=0, tiled=True)]
    pallas_call x1, Pallas kernels: 40.5 us -> 59 us  [backward(): pl.pallas_call(functools.partial(backward_kernel, owners, experts // owne...]
    slice x11 -> x0, local copies, waits for them, and re-layouts: 13.2 us -> none  [the longest x1 7.44 us: body(): sum_sdown = shared_sums[half:].reshape(grad_sdown.shape)]
    reshape x6 -> x0, local copies, waits for them, and re-layouts: 11.6 us -> none  [the longest x1 6.09 us: body(): sum_sdown = shared_sums[half:].reshape(grad_sdown.shape)]
    pallas_call x1, Pallas kernels: 36.6 us -> 47.4 us  [shared_nets(): pl.pallas_call(functools.partial(shared_kernel, owners), grid=(nets, hidd...]
  transfers between devices with their start and end apart: 14 -> 1, of which waited for: 11 -> 0; matrix products, arithmetic and copies ran while one was open for 10% -> 1% of each run, Pallas kernels for 33% -> 22%
where the time goes in v3:
time: 333 us; the launch traced here: 331 us
  Pallas kernels  311 us (93%)
  local copies, waits for them, and re-layouts  9.77 us (3%)
  starting transfers between devices  6.43 us (2%)
    pallas_call x1, Pallas kernels, tail(): pl.pallas_call(tail_kernel, in_specs=[in_vmem()] * 11 + [anywhere()] * 2,...  102 us
    pallas_call x1, Pallas kernels, backward(): pl.pallas_call(functools.partial(backward_kernel, owners, experts // owne...  59 us
    pallas_call x1, Pallas kernels, routed_net(): pl.pallas_call(functools.partial(routed_kernel, owners, reduce), in_specs...  55.7 us
    pallas_call x1, Pallas kernels, shared_nets(): pl.pallas_call(functools.partial(shared_kernel, owners), grid=(nets, hidd...  47.4 us
    pallas_call x1, Pallas kernels, attention(): pl.pallas_call(functools.partial(attention_kernel, owners, experts // own...  24.5 us
    pallas_call x1, Pallas kernels, finish(): pl.pallas_call(functools.partial(finish_kernel, nets, dp_count), in_specs...  14.6 us
    pallas_call x1, Pallas kernels, front(): pl.pallas_call(functools.partial(front_kernel, owners, experts // owners)...  8.17 us
  transfers between devices with their start and end apart: 1, of which 0 were waited for; matrix products, arithmetic and copies ran while one was open for 1% of the time, Pallas kernels for 22%

profile of v3, /device:TPU:0, one launch (start us, length us, event | category | flops | bytes accessed | tf_op | source)
XLA Modules:
  0.0 331.4 jit_solution(4252478958285201549)
XLA Ops:
  1.3 1.3 broadcast_in_dim.19.ada_bias_ref
  2.6 8.2 %front.1 = (f32[8,2304]{1,0:T(8,128)}, f32[8,384]{1,0:T(8,128)}, bf16[8,384]{1,0:T(8,128)(2,1)}, f32[16,1024]{1,0:T(8,128)}, f32[1024,128]{1,0:T(8,128)}, /*inde...) custom-call(s32[1,5]{1,0:T(1,128)} %counts_ref.5, s32[1,5]{1,0:T(1,128)} %labels_ref.3, s32[1]{0:T(128)S(6)} %copy.45.time_ref, ...), custom_call_target="tpu_custom_call" | custom-call | tf_op jit(solution)/shard_map/front/pallas_call | solution.py:200
  10.8 0.0 copy-start.7
  10.8 0.0 copy-start.6
  10.8 0.0 copy-start.5
  10.8 0.0 copy-start.4
  10.8 0.0 copy-start.3
  10.8 6.4 %all-to-all-start = ((bf16[16,160,384]{2,1,0:T(8,128)(2,1)}), bf16[16,160,384]{2,1,0:T(8,128)(2,1)S(1)}, u32[]{:S(2)}, u32[]{:S(2)}) async-start(bf16[16,160,384]{2,1,0:T(8,128)(2,1)} %get-tuple-element.94), calls=%async_computation | async-start | bytes 3932160 | tf_op jit(solution)/shard_map/all_to_all | solution.py:1616
  17.3 0.0 copy-done.7
  17.3 0.6 broadcast_in_dim.20.out_b_ref
  17.8 0.0 copy-done.6
  17.8 0.6 broadcast_in_dim.22.bd_ref
  18.4 0.0 copy-done.5
  18.4 0.6 broadcast_in_dim.24.bd_ref
  19.0 0.0 copy-done.4
  19.0 0.6 broadcast_in_dim.21.bu_ref
  19.6 0.0 copy-done.3
  19.6 0.6 broadcast_in_dim.23.bu_ref
  20.3 24.5 %attention.1 = (bf16[1408,1152]{1,0:T(8,128)(2,1)}, bf16[1024,384]{1,0:T(8,128)(2,1)}, f32[8,1024]{1,0:T(8,128)}, f32[1024,384]{1,0:T(8,128)}, bf16[1024,384]{1,...) custom-call(s32[1,5]{1,0:T(1,128)} %counts_ref.5, bf16[1024,384]{1,0:T(8,128)(2,1)} %tokens_ref.3, ...), custom_call_target="tpu_custom_call" | custom-call | tf_op jit(solution)/shard_map/attention/pallas_call | solution.py:356
  44.7 47.4 %shared_nets.1 = (f32[1024,384]{1,0:T(8,128)}, f32[1024,384]{1,0:T(8,128)}, bf16[2,2,384,1536]{3,2,1,0:T(8,128)(2,1)}, f32[2,1,1536]{2,1,0:T(1,128)}, f32[1,384]{1,0:T(1,128)}, /*index=5*/bf16[16,176,384]{2,1,0:T(8,128)(2,1)}) custom-call(bf16[1024,384]{1,0:T(8,128)(2,1)} %get-tuple-element.86.x_ref.moe_ref, bf16[1024,384]{1,0:T(8,128)(2,1)} %get-tuple-element.89.g_ref, ...), custom_call_target="tpu_custom_call" | custom-call | tf_op jit(solution)/shard_map/shared_nets/pallas_call | solution.py:558
  92.1 0.0 all-to-all-done.g_ref
  92.1 0.0 copy-start
  92.1 1.3 copy-done
  93.4 55.7 %routed_net.1 = (bf16[16,160,384]{2,1,0:T(8,128)(2,1)}, bf16[384,1536]{1,0:T(8,128)(2,1)}, bf16[1536,384]{1,0:T(8,128)(2,1)}, f32[8,1536]{1,0:T(8,128)}, bf16[16...) custom-call(bf16[16,176,384]{2,1,0:T(8,128)(2,1)} %get-tuple-element.93.x_ref, ...), custom_call_target="tpu_custom_call" | custom-call | tf_op jit(solution)/shard_map/routed_net/pallas_call | solution.py:750
  149.1 59.0 %backward.1 = (bf16[1024,384]{1,0:T(8,128)(2,1)}, f32[1024,384]{1,0:T(8,128)}, f32[1,128]{1,0:T(1,128)}, f32[384,1152]{1,0:T(8,128)}, f32[384,384]{1,0:T(8,128)}...) custom-call(s32[1,5]{1,0:T(1,128)} %counts_ref.5, ...), custom_call_target="tpu_custom_call" | custom-call | tf_op jit(solution)/shard_map/backward/pallas_call | solution.py:1136
  208.1 101.6 %tail.1 = (bf16[2,2,384,768]{3,2,1,0:T(8,128)(2,1)}, bf16[2,2,384,768]{3,2,1,0:T(8,128)(2,1)}, bf16[2,416,768]{2,1,0:T(8,128)(2,1)}, bf16[2,2,2,4,16,1408]{5,4,3...) custom-call(f32[384,1152]{1,0:T(8,128)} %get-tuple-element.104.dqkv_w, ...), custom_call_target="tpu_custom_call" | custom-call | tf_op jit(solution)/shard_map/tail/pallas_call | solution.py:1408
  309.7 0.0 copy-start.2
  309.7 14.6 %finish.1 = (f32[1000,384]{1,0:T(8,128)}, f32[1001,384]{1,0:T(8,128)}, f32[384,2304]{1,0:T(8,128)}, f32[1,2304]{1,0:T(1,128)}, f32[384,1152]{1,0:T(8,128)}, /*in...) custom-call(bf16[2,2,384,768]{3,2,1,0:T(8,128)(2,1)} %get-tuple-elem, ...), custom_call_target="tpu_custom_call" | custom-call | tf_op jit(solution)/shard_map/finish/pallas_call | solution.py:1602
  324.3 0.0 copy-start.1
  324.3 1.4 reduce.1
  325.7 1.3 reduce
  327.0 1.6 copy.41
  328.7 0.0 copy-done.2
  328.7 0.9 copy.46
  329.5 0.0 copy-done.1
  329.5 0.0 copy-start.8
  329.5 1.1 copy.47
  330.7 0.0 copy-done.8
  330.7 0.5 copy.48
Async XLA Ops:
  10.8 6.5 %copy-start.7 = (f32[384]{0:T(512)S(1)}, f32[384]{0:T(512)}, u32[]{:S(2)}) copy-start(f32[384]{0:T(512)} %param.34) | copy-start | bytes 4612
  10.8 7.1 %copy-start.6 = (f32[2,384]{1,0:T(2,128)S(1)}, f32[2,384]{1,0:T(2,128)}, u32[]{:S(2)}) copy-start(f32[2,384]{1,0:T(2,128)} %param.43) | copy-start | bytes 9220
  10.8 7.6 %copy-start.5 = (f32[4,384]{1,0:T(4,128)S(1)}, f32[4,384]{1,0:T(4,128)}, u32[]{:S(2)}) copy-start(f32[4,384]{1,0:T(4,128)} %param.39) | copy-start | bytes 18436
  10.8 8.2 %copy-start.4 = (f32[2,1536]{1,0:T(2,128)S(1)}, f32[2,1536]{1,0:T(2,128)}, u32[]{:S(2)}) copy-start(f32[2,1536]{1,0:T(2,128)} %param.41) | copy-start | bytes 36868
  10.8 8.8 %copy-start.3 = (f32[4,1536]{1,0:T(4,128)S(1)}, f32[4,1536]{1,0:T(4,128)}, u32[]{:S(2)}) copy-start(f32[4,1536]{1,0:T(4,128)} %param.37) | copy-start | bytes 73732
  10.8 81.3 %all-to-all-start = ((bf16[16,160,384]{2,1,0:T(8,128)(2,1)}), bf16[16,160,384]{2,1,0:T(8,128)(2,1)S(1)}, u32[]{:S(2)}, u32[]{:S(2)}) async-start(bf16[16,160,384]{2,1,0:T(8,128)(2,1)} %get-tuple-element.94), calls=%async_computation | async-start | bytes 3932160 | tf_op jit(solution)/shard_map/all_to_all | solution.py:1616
  92.1 1.3 copy-start
  309.7 19.0 %copy-start.2 = (bf16[1024,384]{1,0:T(8,128)(2,1)S(1)}, bf16[1024,384]{1,0:T(8,128)(2,1)}, u32[]{:S(2)}) copy-start(bf16[1024,384]{1,0:T(8,128)(2,1)} %get-tuple-element.177) | copy-start | bytes 2359300
  324.3 5.3 %copy-start.1 = (f32[1024,384]{1,0:T(8,128)S(1)}, f32[1024,384]{1,0:T(8,128)}, u32[]{:S(2)}) copy-start(f32[1024,384]{1,0:T(8,128)} %get-tuple-element.178) | copy-start | bytes 4718596
  329.5 1.1 copy-start.8
